TPU v7x, 32 devices: a whole 2x2x4 slice. The times are simulated.
32 devices in a mesh: row: 4 (over y, x), col: 8 (over z, core).
Axes of the slice: x: 2, y: 2, z: 4, core: 2. Of those that a mesh axis runs over, the one named last changes fastest.
Arguments:
- gradient: bfloat16 [3072, 8192], P('row', 'col'), may hold values from -6 to 6
- left_basis: bfloat16 [3072, 3072], P('row'), may hold values from -0.109375 to 0.109375
- right_basis: bfloat16 [8192, 8192], P('col'), may hold values from -0.0625 to 0.0625
- first_moment: float32 [3072, 8192], P('row', 'col'), may hold values from -6 to 6
- second_moment: float32 [3072, 8192], P('row', 'col'), may hold values from 0.1 to 4
Outputs:
- new_first: float32 [3072, 8192], P('row', 'col')
- new_second: float32 [3072, 8192], P('row', 'col')
- update: float32 [3072, 8192], P('row', 'col')
All inputs are finite; a program needn't handle non-finite values.
Results may differ from a plain program's by a relative error of at most 0.0095.
Values may be sent and summed in bfloat16 or wider, within the bound.
No kernel may reach another device: no remote copies, remote signals or barrier semaphores. Data moves between devices by JAX's collectives and lax.ppermute only.
A program may use at most 128 MiB of HBM per device.

v0:
```python
import jax
import jax.numpy as jnp
from jax import lax
from jax.sharding import PartitionSpec as P


def body(gradient, left_basis, right_basis, first_moment, second_moment):
    panel = right_basis
    summed = lax.psum_scatter(
        lax.dot_general(
            panel, gradient, (((0,), (1,)), ((), ())), preferred_element_type=jnp.float32
        ).astype(jnp.bfloat16),
        "col",
        scatter_dimension=0,
        tiled=True,
    )
    right_rotated = summed.T
    panel = left_basis
    rotated = lax.psum_scatter(
        lax.dot_general(
            panel, right_rotated, (((0,), (0,)), ((), ())), preferred_element_type=jnp.float32
        ).astype(jnp.bfloat16),
        "row",
        scatter_dimension=0,
        tiled=True,
    ).astype(jnp.float32)
    new_first = 0.9 * first_moment + 0.1 * rotated
    new_second = 0.95 * second_moment + 0.05 * rotated * rotated
    first_fix = 1.0 - 0.9**20
    second_fix = 1.0 - 0.95**20
    step_rotated = (new_first / first_fix / (jnp.sqrt(new_second / second_fix) + 1e-08)).astype(
        jnp.bfloat16
    )
    panel = left_basis
    back_left = jnp.dot(
        panel,
        lax.all_gather(step_rotated, "row", axis=0, tiled=True),
        preferred_element_type=jnp.float32,
    ).astype(jnp.bfloat16)
    panel = right_basis
    update = lax.dot_general(
        lax.all_gather(back_left, "col", axis=1, tiled=True),
        panel,
        (((1,), (1,)), ((), ())),
        preferred_element_type=jnp.float32,
    )
    return (new_first, new_second, update)


def solution(mesh):
    return jax.shard_map(
        body,
        mesh=mesh,
        in_specs=(
            P("row", "col"),
            P("row", None),
            P("col", None),
            P("row", "col"),
            P("row", "col"),
        ),
        out_specs=(P("row", "col"), P("row", "col"), P("row", "col")),
        check_vma=False,
    )
```

profile of v0, /device:TPU:0, one launch (start us, length us, event | category | flops | bytes accessed | tf_op | source)
XLA Modules:
  0.0 472.3 jit_solution(5028666509595222156)
XLA Ops:
  7.2 0.0 copy-start
  7.2 0.0 reduce-scatter.3.cloned.1.call-start
  7.2 1.4 copy-done
  8.6 22.3 %convolution_convert_fusion = bf16[8192,768]{1,0:T(8,128)(2,1)} fusion(bf16[1024,8192]{1,0:T(8,128)(2,1)} %param.7, bf16[768,1024]{1,0:T(8,128)(2,1)S(1)} %copy-done), kind=kOutput, calls=%fused_computation | convolution fusion | flops 12891193344 | bytes 30932992 | tf_op jit(solution)/shard_map/dot_general | solution.py:10
  30.9 0.0 reduce-scatter.3.cloned.1.call-update
  30.9 0.0 reduce-scatter.5.cloned.1.call-start
  31.0 132.0 %reduce-scatter.3.cloned.1.call-done = bf16[1024,768]{1,0:T(8,128)(2,1)} async-done(((bf16[8192,768]{1,0:T(8,128)(2,1)}), bf16[1024,768]{1,0:T(8,128)(2,1)}) %reduce-scatter.3.cloned.1.call-update) | async-done | bytes 1572880 | tf_op jit(solution)/shard_map/reduce_scatter | solution.py:9
  163.0 9.1 %convert_bitcast_fusion = bf16[3072,1024]{0,1:T(8,128)(2,1)} fusion(bf16[1024,768]{1,0:T(8,128)(2,1)} %reduce-scatter.3.cloned.1.call-done, bf16[768,3072]{1,0:T(8,128)(2,1)} %param.6), kind=kOutput, calls=%fused_computation.1 | convolution fusion | flops 4834983936 | bytes 12582912 | tf_op jit(solution)/shard_map/dot_general | solution.py:20
  172.1 0.0 copy-start.2
  172.1 0.0 reduce-scatter.5.cloned.1.call-update
  172.2 0.0 all-gather.3.cloned.1.call-start
  172.2 1.8 copy-done.2
  174.0 2.4 copy.8
  176.4 4.4 copy.9
  180.8 60.1 %reduce-scatter.5.cloned.1.call-done = bf16[768,1024]{0,1:T(8,128)(2,1)} async-done(((bf16[3072,1024]{0,1:T(8,128)(2,1)}), bf16[768,1024]{0,1:T(8,128)(2,1)}) %reduce-scatter.5.cloned.1.call-update) | async-done | bytes 1572880 | tf_op jit(solution)/shard_map/reduce_scatter | solution.py:19
  240.9 7.7 %divide_convert_fusion = (bf16[768,1024]{0,1:T(8,128)(2,1)}, f32[768,1024]{0,1:T(8,128)}, f32[768,1024]{0,1:T(8,128)S(1)}) fusion(bf16[768,1024]{0,1:T(8,128)(2,1)} %reduce-scatter.5.cloned.1.call-done, f32[768,1024]{0,1:T(8,128)} %copy.9, f32[768,1024]{0,1:T(8,128)} %copy.8), kind=kLoop, calls=%fused_computation.6 | loop fusion | flops 10223616 | bytes 15728640 | tf_op jit(solution)/shard_map/convert_element_type | solution.py:31
  248.6 0.0 all-gather.3.cloned.1.call-update
  248.6 0.2 all-gather.5.cloned.1.call-start
  248.9 70.1 %all-gather.3.cloned.1.call-done = bf16[3072,1024]{0,1:T(8,128)(2,1)} async-done(((bf16[768,1024]{0,1:T(8,128)(2,1)}), bf16[3072,1024]{0,1:T(8,128)(2,1)}) %all-gather.3.cloned.1.call-update) | async-done | bytes 6291472 | tf_op jit(solution)/shard_map/all_gather | solution.py:37
  319.0 9.5 %fusion.2 = bf16[768,1024]{0,1:T(8,128)(2,1)} fusion(bf16[3072,1024]{0,1:T(8,128)(2,1)} %all-gather.3.cloned.1.call-done, bf16[768,3072]{1,0:T(8,128)(2,1)} %param.6), kind=kOutput, calls=%fused_computation.8 | convolution fusion | flops 4832624640 | bytes 12582912 | tf_op jit(solution)/shard_map/dot_general | solution.py:35
  328.4 0.0 all-gather.5.cloned.1.call-update
  328.5 3.5 copy.11
  332.0 2.4 copy.10
  334.4 111.0 %all-gather.5.cloned.1.call-done = bf16[768,8192]{0,1:T(8,128)(2,1)} async-done(((bf16[768,1024]{0,1:T(8,128)(2,1)}), bf16[768,8192]{0,1:T(8,128)(2,1)}) %all-gather.5.cloned.1.call-update) | async-done | bytes 12582928 | tf_op jit(solution)/shard_map/all_gather | solution.py:42
  445.4 0.0 copy-start.1
  445.4 20.4 %fusion.5 = f32[768,1024]{1,0:T(8,128)} fusion(bf16[768,8192]{0,1:T(8,128)(2,1)} %all-gather.5.cloned.1.call-done, bf16[1024,8192]{1,0:T(8,128)(2,1)} %param.7), kind=kOutput, calls=%fused_computation.9 | convolution fusion | flops 12884901888 | bytes 32505856 | tf_op jit(solution)/shard_map/dot_general | solution.py:41
  465.7 0.0 copy-done.1
Async XLA Ops:
  7.2 1.4 copy-start
  7.2 155.8 %reduce-scatter.3.cloned.1.call-start = ((), (), s32[]{:S(2)}) async-start(), calls=%async_computation.2 | async-start | bytes 14155776 | tf_op jit(solution)/shard_map/reduce_scatter | solution.py:9
  30.9 210.0 %reduce-scatter.5.cloned.1.call-start = ((), (), s32[]{:S(2)}) async-start(), calls=%async_computation.3 | async-start | bytes 7864320 | tf_op jit(solution)/shard_map/reduce_scatter | solution.py:19
  172.1 1.9 copy-start.2
  172.2 146.8 %all-gather.3.cloned.1.call-start = ((), (), s32[]{:S(2)}) async-start(), calls=%async_computation.4 | async-start | bytes 7864320 | tf_op jit(solution)/shard_map/all_gather | solution.py:37
  248.6 196.7 %all-gather.5.cloned.1.call-start = ((), (), s32[]{:S(2)}) async-start(), calls=%async_computation.5 | async-start | bytes 14155776 | tf_op jit(solution)/shard_map/all_gather | solution.py:42
  445.4 20.4 %copy-start.1 = (bf16[768,1024]{1,0:T(8,128)(2,1)S(1)}, bf16[768,1024]{1,0:T(8,128)(2,1)}, u32[]{:S(2)}) copy-start(bf16[768,1024]{1,0:T(8,128)(2,1)} %param.5) | copy-start | bytes 4718596
Sparse Core Ops, SparseCore 0:
  31.1 131.9 reduce-scatter.2
  172.3 68.5 reduce-scatter.4
  248.8 70.1 all-gather.2
  328.6 116.7 all-gather.4
where the time goes:
time: 473 us; the launch traced here: 472 us
  waiting for transfers between devices  373 us (79%)
  matrix products  61.3 us (13%)
  local copies, waits for them, and re-layouts  15.9 us (3%)
  between operations  13.8 us (3%)
  other arithmetic  7.7 us (2%)
    reduce_scatter x1, waiting for transfers between devices, body(): lax.psum_scatter(lax.dot_general(panel, gradient, (((0,), (1,)), ((), ())...  132 us
    all_gather x1, waiting for transfers between devices, body(): lax.all_gather(back_left, 'col', axis=1, tiled=True)  111 us
    all_gather x1, waiting for transfers between devices, body(): lax.all_gather(step_rotated, 'row', axis=0, tiled=True)  70.1 us
    reduce_scatter x1, waiting for transfers between devices, body(): lax.psum_scatter(lax.dot_general(panel, right_rotated, (((0,), (0,)), (()...  60.1 us
    dot_general x1, matrix products, body(): lax.dot_general(panel, gradient, (((0,), (1,)), ((), ())), preferred_elem...  22.3 us
    dot_general x1, matrix products, body(): lax.dot_general(lax.all_gather(back_left, 'col', axis=1, tiled=True), pan...  20.4 us
    unnamed x10, local copies, waits for them, and re-layouts  15.9 us
    dot_general x1, matrix products, body(): jnp.dot(panel, lax.all_gather(step_rotated, 'row', axis=0, tiled=True), p...  9.49 us
  transfers between devices with their start and end apart: 4, of which 4 were waited for; matrix products, arithmetic and copies ran while one was open for 3% of the time, Pallas kernels for 0%

commit v1 on v0

v1 whole, which is shorter than its diff:
```python
import functools

import jax
import jax.numpy as jnp
import numpy as np
from jax import lax
from jax.experimental import pallas as pl
from jax.experimental.pallas import tpu as pltpu
from jax.sharding import PartitionSpec as P

F32, BF16 = jnp.float32, jnp.bfloat16
VMEM_BYTES = 40 * 2**20
ANY = pl.BlockSpec(memory_space=pl.ANY)


def like(shape, dtype):
    return jax.ShapeDtypeStruct(tuple(shape), dtype)


class Order:
    def __init__(self):
        self.last = None

    def call(self, kernel, place, inputs, in_specs, outs, out_specs, grid, aliases=None):
        n_in = len(inputs)
        extra = [] if self.last is None else [self.last]

        def wrapped(place_ref, *refs):
            kernel(place_ref, refs[:n_in], refs[n_in + len(extra) :])

        got = pl.pallas_call(
            wrapped,
            out_shape=outs,
            grid_spec=pltpu.PrefetchScalarGridSpec(
                num_scalar_prefetch=1,
                grid=grid,
                in_specs=list(in_specs) + [ANY] * len(extra),
                out_specs=out_specs,
            ),
            input_output_aliases={k + 1: v for k, v in (aliases or {}).items()},
            compiler_params=pltpu.CompilerParams(vmem_limit_bytes=VMEM_BYTES),
            cost_estimate=pl.CostEstimate(flops=10**12, bytes_accessed=1, transcendentals=0),
        )(place, *inputs, *extra)
        self.last = got[0]
        return got


def streams(spots, gather):
    out = []
    for t in range(spots - 1):
        for parity in range(2):
            edges = range(parity, spots - 1, 2)
            if gather:
                pairs = [(e, e + 1) for e in edges if e >= t]
                pairs += [(e + 1, e) for e in edges if e + 1 <= spots - 1 - t]
            else:
                pairs = [(e, e + 1) for e in edges if e <= t]
                pairs += [(e + 1, e) for e in edges if e >= spots - 2 - t]
            if pairs:
                out.append((t, parity, pairs))
    return out


def slots_of(spots, gather):
    groups, users, slot, table = [], [], {}, []
    for t, parity, pairs in streams(spots, gather):
        who = {}
        for a, b in pairs:
            if gather:
                who[b] = b - (t + 1) if a < b else b + (t + 1)
            else:
                who[a] = a + (spots - 1 - t) if a < b else a - (spots - 1 - t)
        for k in range(len(groups) + 1):
            if k == len(groups):
                groups.append([])
                users.append({})
            if not set(users[k]) & set(who):
                break
        groups[k].append((t, parity))
        users[k].update(who)
        slot[t, parity] = k
    table = [[users[k].get(z, 0) for k in range(len(groups))] for z in range(spots)]
    return groups, slot, np.array(table, np.int32)


STEPS = {
    "pack": -30.0,
    "right": -10.0,
    "sum 1 1": 20.0,
    "sum 2 1": 37.0,
    "sum 2 0": 41.0,
    "left": 62.0,
    "fold": 87.0,
    "moments": 100.0,
    "unfold": 116.0,
    "back": 138.0,
    "pass 1 0": 163.1,
    "pass 1 1": 163.0,
    "pass 2 0": 184.0,
    "away": 205.0,
    "near": 226.0,
}
APART = 45.0


def nominal(step, index):
    if step == "end":
        return 1e6
    if step in STEPS:
        return STEPS[step] + APART * index
    kind, t, _ = step.split()
    return STEPS["left" if kind == "sum" else "pass 2 0"] - 1.0 / (1 + int(t)) + APART * index


def run(tasks):
    waiting = {k: next(task) for k, task in enumerate(tasks)}
    while waiting:
        k = min(waiting, key=lambda k: (nominal(waiting[k], k), k))
        try:
            waiting[k] = next(tasks[k])
        except StopIteration:
            del waiting[k]


def body(row_size, col_size, widths, gradient, left_basis, right_basis, first_moment, second_moment):
    height, columns = first_moment.shape
    spots = col_size // 2
    col, row = lax.axis_index("col"), lax.axis_index("row")
    at, core = col // 2, col % 2
    direct, square = row_size in (2, 4), row_size == 4
    slots = np.arange(row_size, dtype=np.int32)

    _, sum_slot, sum_table = slots_of(spots, False)
    groups, gather_slot, gather_table = slots_of(spots, True)
    n_sum, n_gather = sum_table.shape[1] + 1, gather_table.shape[1] + 1
    own = np.arange(spots, dtype=np.int32)[:, None]
    sum_table = np.concatenate([sum_table, own], 1)
    gather_table = np.concatenate([own, gather_table], 1)
    same = np.array(
        [[list(sum_table[z]).index(d) for d in gather_table[z]] for z in range(spots)], np.int32
    )
    table = np.concatenate([sum_table, gather_table, same], 1)
    place = jnp.concatenate(
        [
            core.astype(jnp.int32).reshape(1),
            (slots ^ row.astype(jnp.int32)) if direct else jnp.asarray(slots),
            jnp.asarray(table)[at],
        ]
    )
    at_row, at_sum = 1, 1 + row_size
    at_gather, at_same = at_sum + n_sum, at_sum + n_sum + n_gather

    order = Order()

    def swap(x):
        return lax.ppermute(x, "col", [(j, j ^ 1) for j in range(col_size)])

    def along(x, pairs):
        return lax.ppermute(x, "col", [(2 * a + c, 2 * b + c) for a, b in pairs for c in range(2)])

    def to_partner(x, s):
        return lax.ppermute(x, "row", [(i, i ^ s) for i in range(row_size)])

    def across(blocks):
        if not direct:
            return [lax.psum_scatter(jnp.concatenate(blocks), "row", scatter_dimension=0, tiled=True)]
        return [blocks[0]] + [
            to_partner(blocks[s], s) for s in range(1, row_size)
        ]

    def spread(block):
        if not direct:
            whole = lax.all_gather(block, "row", axis=0, tiled=False)
            return [whole[s] for s in range(row_size)]
        return across([block] * row_size)

    other_gradient = swap(gradient)

    def turn():
        def kernel(_, ins, outs):
            outs[0][...] = ins[0][...].T

        return order.call(
            kernel,
            place,
            [left_basis],
            [pl.BlockSpec((height, height), lambda s, p: (0, p[at_row + s]))],
            [like((row_size * height, height), BF16)],
            [pl.BlockSpec((height, height), lambda s, p: (s, 0))],
            (row_size,),
        )[0]

    def pack(first, width):
        stride = columns // width

        def kernel(_, ins, outs):
            outs[0][0] = ins[0][...]

        depth = right_basis.shape[0]
        return order.call(
            kernel,
            place,
            [right_basis],
            [
                pl.BlockSpec(
                    (depth, width),
                    lambda s, p: (0, (2 * p[at_sum + s] + 1 - p[0]) * stride + first // width),
                )
            ],
            [like((n_sum, depth, width), BF16)],
            [pl.BlockSpec((1, depth, width), lambda s, p: (s, 0, 0))],
            (n_sum,),
        )[0]

    def right(packed, first, width):
        stride = columns // width
        depth = right_basis.shape[0]

        def kernel(_, ins, outs):
            mine, theirs, basis, other = ins
            value = jnp.dot(mine[...], basis[...], preferred_element_type=F32)
            value += jnp.dot(theirs[...], other[0], preferred_element_type=F32)
            value = value.astype(BF16)
            for s in range(n_sum):

                @pl.when(pl.program_id(0) == s)
                def _(s=s):
                    outs[s][...] = value

        whole = pl.BlockSpec((height, depth), lambda s, p: (0, 0))
        return order.call(
            kernel,
            place,
            [gradient, other_gradient, right_basis, packed],
            [
                whole,
                whole,
                pl.BlockSpec(
                    (depth, width),
                    lambda s, p: (0, (2 * p[at_sum + s] + p[0]) * stride + first // width),
                ),
                pl.BlockSpec((1, depth, width), lambda s, p: (s, 0, 0)),
            ],
            [like((height, width), BF16)] * n_sum,
            [pl.BlockSpec((height, width), lambda s, p: (0, 0))] * n_sum,
            (n_sum,),
        )

    def add(x, y):
        def kernel(_, ins, outs):
            outs[0][...] = (ins[0][...].astype(F32) + ins[1][...].astype(F32)).astype(BF16)

        spec = pl.BlockSpec(x.shape, lambda s, p: (0, 0))
        return order.call(kernel, place, [x, y], [spec, spec], [like(x.shape, BF16)], [spec], (1,))[0]

    def hand_on(x, also=()):
        def kernel(_, ins, outs):
            pass

        return order.call(
            kernel, place, [x, *also], [ANY] * (1 + len(also)), [like(x.shape, BF16)], [ANY], (1,), {0: 0}
        )[0]

    def left_sums(terms):
        width = terms[0].shape[1]
        n = len(terms)
        half = height // 2

        def kernel(_, ins, outs):
            total = ins[0][...].astype(F32)
            for term in ins[1:n]:
                total += term[...].astype(F32)
            value = jnp.dot(ins[n][...], total.astype(BF16), preferred_element_type=F32).astype(BF16)
            for s in range(row_size):

                @pl.when(pl.program_id(0) == s)
                def _(s=s):
                    if not square:
                        outs[s][...] = value
                        return
                    keep, by_x, by_y, then_y, then_x = outs
                    if s == 0:
                        keep[...] = value
                    if s & 1:
                        by_x[s // 2] = value[:half]
                    if s & 2:
                        by_y[s - 2] = value[half:]
                    if s == 2:
                        then_y[...] = value[:half]
                    if s == 1:
                        then_x[...] = value[half:]

        spec = pl.BlockSpec((height, width), lambda s, p: (0, 0))
        if square:
            shapes = [(height, width), (2, half, width), (2, half, width), (half, width), (half, width)]
        else:
            shapes = [(height, width)] * row_size
        return order.call(
            kernel,
            place,
            [*terms, turned_left[0]],
            [spec] * n + [pl.BlockSpec((height, height), lambda s, p: (s, 0))],
            [like(shape, BF16) for shape in shapes],
            [pl.BlockSpec(shape, lambda s, p, zeros=(0,) * len(shape): zeros) for shape in shapes],
            (row_size,),
        )

    def whole_spec(x):
        return pl.BlockSpec(x.shape, lambda s, p, zeros=(0,) * x.ndim: zeros)

    def fold(then_y, got_x, then_x, got_y):
        def kernel(_, ins, outs):
            for k in range(2):
                outs[k][...] = (ins[2 * k][...].astype(F32) + ins[2 * k + 1][1].astype(F32)).astype(BF16)

        inputs = [then_y, got_x, then_x, got_y]
        outs = [like(then_y.shape, BF16)] * 2
        return order.call(
            kernel, place, inputs, [whole_spec(x) for x in inputs], outs, [whole_spec(x) for x in outs], (1,)
        )

    def unfold(upper, got_upper, lower, got_lower):
        def kernel(_, ins, outs):
            for k in range(2):
                outs[k][0] = ins[2 * k][...]
                outs[k][1] = ins[2 * k + 1][...]

        inputs = [upper, got_upper, lower, got_lower]
        outs = [like((2, *upper.shape), BF16)] * 2
        return order.call(
            kernel, place, inputs, [whole_spec(x) for x in inputs], outs, [whole_spec(x) for x in outs], (1,)
        )

    def left_times(blocks):
        width = blocks[0][0][0].shape[-1]
        tile = height // 3 if height % 48 == 0 else height
        inputs, layout = [], []
        for views in blocks:
            refs = []
            for x, k in views:
                n = next((n for n, y in enumerate(inputs) if x is y), len(inputs))
                if n == len(inputs):
                    inputs.append(x)
                refs.append((n, k))
            layout.append(refs)
        first = len(inputs)

        def kernel(_, ins, outs):
            total = 0.0
            for s, refs in enumerate(layout):
                parts = [ins[n][...] if k is None else ins[n][k] for n, k in refs]
                x = parts[0] if len(parts) == 1 else jnp.concatenate(parts, axis=0)
                total += jnp.dot(ins[first + s][...], x, preferred_element_type=F32)
            outs[0][...] = total.astype(BF16)

        return order.call(
            kernel,
            place,
            [*inputs, *([left_basis] * row_size)],
            [whole_spec(x) for x in inputs]
            + [
                pl.BlockSpec((tile, height), lambda r, p, s=s: (r, p[at_row + s]))
                for s in range(row_size)
            ],
            [like((height, width), BF16)],
            [pl.BlockSpec((tile, width), lambda r, p: (r, 0))],
            (height // tile,),
        )[0]

    kept = []

    def moments(parts, first, width):
        tile = height // 4 if height % 64 == 0 else height // 2
        per_half = height // 2 // tile
        first_fix = 1.0 - 0.9**20
        second_fix = 1.0 - 0.95**20
        inputs, specs, halves = [], [], [[], []]
        for part in parts:
            if not isinstance(part, list):
                for k in range(2):
                    halves[k].append(len(inputs))
                inputs.append(part)
                specs.append(pl.BlockSpec((tile, width), lambda r, p: (r, 0)))
                continue
            for k, (x, at_x) in enumerate(part):
                halves[k].append(len(inputs))
                inputs.append(x)
                low = k * per_half

                def at(r, p, low=low, at_x=at_x):
                    r = jnp.clip(r - low, 0, per_half - 1)
                    return (r, 0) if at_x is None else (at_x, r, 0)

                specs.append(pl.BlockSpec((tile, width) if at_x is None else (None, tile, width), at))
        n = len(inputs)

        def kernel(_, ins, outs):
            for k in range(2):

                @pl.when(pl.program_id(0) // per_half == k)
                def _(k=k):
                    rotated = sum(ins[m][...].astype(F32) for m in halves[k])
                    nf = 0.9 * ins[n][...] + 0.1 * rotated
                    ns = 0.95 * ins[n + 1][...] + 0.05 * rotated * rotated
                    outs[2][...] = nf
                    outs[3][...] = ns
                    outs[k][...] = (nf / first_fix / (jnp.sqrt(ns / second_fix) + 1e-08)).astype(BF16)

        spot = pl.BlockSpec((tile, width), lambda r, p: (r, first // width))
        half_specs = [
            pl.BlockSpec((tile, width), lambda r, p, k=k: (jnp.clip(r - k * per_half, 0, per_half - 1), 0))
            for k in range(2)
        ]
        upper, lower, *kept[:] = order.call(
            kernel,
            place,
            [*inputs, first_moment, second_moment, *kept],
            specs + [spot, spot] + [ANY] * len(kept),
            [like((height // 2, width), BF16)] * 2 + [like((height, columns), F32)] * 2,
            [*half_specs, spot, spot],
            (height // tile,),
            {n + 2: 2, n + 3: 3} if kept else None,
        )
        return upper, lower

    def back(chunks, mine, dtype, ends=(), both=False):
        depth = right_basis.shape[0]
        tile = min(256, depth)
        inputs, specs, layout = [], [], []
        whole = [pl.BlockSpec((height, width), lambda r, p: (0, 0)) for _, width, _, _ in chunks]
        for at_chunk, (first, width, packed, gathered) in enumerate(chunks):
            stride = columns // width
            for flip in range(2 if both else 1):
                for g in range(n_gather):
                    xs = [swap(x) for x in gathered[g]] if flip else gathered[g]
                    inputs += xs
                    specs += [whole[at_chunk]] * len(xs)
                    layout.append(len(xs))
                    if mine:

                        def at(r, p, g=g, flip=flip, stride=stride, first=first, width=width):
                            half = p[0] if flip == 0 else 1 - p[0]
                            return (r, (2 * p[at_gather + g] + half) * stride + first // width)

                        inputs.append(right_basis)
                        specs.append(pl.BlockSpec((tile, width), at))
                    else:
                        inputs.append(packed)
                        specs.append(
                            pl.BlockSpec((1, tile, width), lambda r, p, g=g: (p[at_same + g], r, 0))
                        )
        out_spec = pl.BlockSpec((height, tile), lambda r, p: (0, r))
        n = len(inputs)
        inputs += list(ends)
        specs += [out_spec] * len(ends)

        def kernel(_, ins, outs):
            total = jnp.zeros((height, tile), F32)
            k = 0
            for count in layout:
                x = ins[k][...]
                for more in ins[k + 1 : k + count]:
                    x = x + more[...]
                basis = ins[k + count][...] if mine else ins[k + count][0]
                total += lax.dot_general(x, basis, (((1,), (1,)), ((), ())), preferred_element_type=F32)
                k += count + 1
            for end in ins[n:]:
                total += end[...].astype(F32)
            outs[0][...] = total.astype(dtype)

        return order.call(
            kernel, place, inputs, specs, [like((height, depth), dtype)], [out_spec], (depth // tile,)
        )[0]

    held, totals, turned_left = [], [], []

    def chunk(index, first, width):
        yield "pack"
        packed = swap(pack(first, width))
        yield "right"
        blocks = right(packed, first, width)
        if index == 0:
            turned_left.append(turn())
        got = {}
        for t, parity, pairs in streams(spots, False):
            value = blocks[sum_slot[t, parity]]
            before = got.get((t - 1, 1 - parity))
            if before is not None:
                yield f"sum {t} {parity}"
                value = add(value, before)
            got[t, parity] = along(value, pairs)
        yield "left"
        sums = left_sums([blocks[n_sum - 1]] + [got[k] for k in got if k[0] == spots - 2])
        if square:
            keep, by_x, by_y, then_y, then_x = sums
            got_x, got_y = to_partner(by_x, 1), to_partner(by_y, 2)
            yield "fold"
            then_y, then_x = fold(then_y, got_x, then_x, got_y)
            last_y, last_x = to_partner(then_y, 2), to_partner(then_x, 1)
            parts = [keep, [(got_x, 0), (got_y, 0)], [(last_y, None), (last_x, None)]]
        else:
            parts = across(sums)
        yield "moments"
        upper, lower = moments(parts, first, width)
        if square:
            upper_y, lower_x = to_partner(upper, 2), to_partner(lower, 1)
            yield "unfold"
            uppers, lowers = unfold(upper, upper_y, lower, lower_x)
            by_x, by_y = to_partner(uppers, 1), to_partner(lowers, 2)
            steps = [
                [(upper, None), (lower, None)],
                [(by_x, 0), (lower_x, None)],
                [(upper_y, None), (by_y, 0)],
                [(by_x, 1), (by_y, 1)],
            ]
        else:
            steps = [[(x, None)] for x in spread(jnp.concatenate([upper, lower]))]
        yield "back"
        turned = left_times(steps)
        got = {}
        for t, parity, pairs in streams(spots, True):
            value = turned
            if t:
                before = (t - 1, 1 - parity)
                yield f"pass {t} {parity}"
                value = hand_on(got[before], [got[t - 1, parity]] if t > 1 and (t - 1, parity) in got else [])
                got[before] = value
            got[t, parity] = along(value, pairs)
        held.append((first, width, packed, [[turned]] + [[got[k] for k in group] for group in groups]))
        last = index == len(widths) - 1
        if index < len(widths) - 2:
            return
        if not last:
            yield "away"
            away = swap(back(held[: index + 1], False, BF16))
            yield "near"
            totals.extend([away, back(held[: index + 1], True, F32)])
        else:
            yield "end"
            totals[:] = [back(held[-1:], True, F32, totals, True)]

    run([chunk(k, first, width) for k, (first, width) in enumerate(widths)])
    return (kept[0], kept[1], totals[0])


def solution(mesh):
    row_size, col_size = mesh.shape["row"], mesh.shape["col"]

    def whole(gradient, *rest):
        columns = gradient.shape[1] // col_size
        width = columns // 2
        widths = [(first, width) for first in range(0, columns, width)]
        return jax.shard_map(
            functools.partial(body, row_size, col_size, widths),
            mesh=mesh,
            in_specs=(
                P("row", "col"),
                P("row", None),
                P("col", None),
                P("row", "col"),
                P("row", "col"),
            ),
            out_specs=(P("row", "col"), P("row", "col"), P("row", "col")),
            check_vma=False,
        )(gradient, *rest)

    return whole
```

time: 473 us -> 341 us (0.72)
  waiting for transfers between devices: 373 us -> 125 us
  Pallas kernels: 0 us -> 125 us
  starting transfers between devices: 0.35 us -> 81.2 us
  matrix products: 61.3 us -> 0 us
  between operations: 13.8 us -> 0.99 us
  local copies, waits for them, and re-layouts: 15.9 us -> 7.26 us
  other arithmetic: 7.7 us -> 0.08 us
    reduce_scatter x2 -> x0, waiting for transfers between devices: 192 us -> none  [the longest x1 132 us: body(): lax.psum_scatter(lax.dot_general(panel, gradient, (((0,), (1,)), ((), ())...]
    all_gather x2 -> x0, waiting for transfers between devices: 181 us -> none  [the longest x1 111 us: body(): lax.all_gather(back_left, 'col', axis=1, tiled=True)]
    ppermute x0 -> x46, waiting for transfers between devices: none -> 125 us  [the longest x20 79.1 us: along(): lax.ppermute(x, 'col', [(2 * a + c, 2 * b + c) for a, b in pairs for c in...]
    pallas_call x0 -> x30, Pallas kernels: none -> 125 us  [call(): pl.pallas_call(wrapped, out_shape=outs, grid_spec=pltpu.PrefetchScalarGri...]
    ppermute x0 -> x46, starting transfers between devices: none -> 81.2 us  [the longest x20 62.5 us: along(): lax.ppermute(x, 'col', [(2 * a + c, 2 * b + c) for a, b in pairs for c in...]
    dot_general x4 -> x0, matrix products: 61.3 us -> none  [the longest x1 22.3 us: body(): lax.dot_general(panel, gradient, (((0,), (1,)), ((), ())), preferred_elem...]
    unnamed x10 -> x50, local copies, waits for them, and re-layouts: 15.9 us -> 6.57 us
    convert_element_type x1 -> x0, other arithmetic: 7.7 us -> none  [body(): (new_first / first_fix / (jnp.sqrt(new_second / second_fix) + 1e-08)).ast...]
  transfers between devices with their start and end apart: 4 -> 46, of which waited for: 4 -> 24; matrix products, arithmetic and copies ran while one was open for 3% -> 0% of each run, Pallas kernels for 0% -> 25%
where the time goes in v1:
time: 341 us; the launch traced here: 340 us
  Pallas kernels  125 us (37%)
  waiting for transfers between devices  125 us (37%)
  starting transfers between devices  81.2 us (24%)
  local copies, waits for them, and re-layouts  7.26 us (2%)
    pallas_call x30, Pallas kernels, call(): pl.pallas_call(wrapped, out_shape=outs, grid_spec=pltpu.PrefetchScalarGri...  125 us
    ppermute x20, waiting for transfers between devices, along(): lax.ppermute(x, 'col', [(2 * a + c, 2 * b + c) for a, b in pairs for c in...  79.1 us
    ppermute x20, starting transfers between devices, along(): lax.ppermute(x, 'col', [(2 * a + c, 2 * b + c) for a, b in pairs for c in...  62.5 us
    ppermute x16, waiting for transfers between devices, to_partner(): return lax.ppermute(x, 'row', [(i, i ^ s) for i in range(row_size)])  34.9 us
    ppermute x16, starting transfers between devices, to_partner(): return lax.ppermute(x, 'row', [(i, i ^ s) for i in range(row_size)])  16.8 us
    ppermute x10, waiting for transfers between devices, swap(): return lax.ppermute(x, 'col', [(j, j ^ 1) for j in range(col_size)])  11.2 us
  transfers between devices with their start and end apart: 46, of which 24 were waited for; matrix products, arithmetic and copies ran while one was open for 0% of the time, Pallas kernels for 25%

profile of v1, /device:TPU:0, one launch (start us, length us, event | category | flops | bytes accessed | tf_op | source)
XLA Modules:
  0.0 339.8 jit_solution(1544244251092639610)
XLA Ops:
  1.4 3.6 %shard_map.94.refs_4_ = bf16[4,1024,512]{2,1,0:T(8,128)(2,1)S(1)} custom-call(s32[17]{0:T(128)S(1)} %pad_add_fusion.place_ref, bf16[1024,8192]{1,0:T(8,128)(2,1)} %refs_19_.1), custom_call_target="tpu_custom_call" | custom-call | flops 999999995904 | bytes 1 | tf_op jit(solution)/shard_map/pallas_call | solution.py:31
  5.6 8.9 %collective-permute-done.refs_1_ = bf16[768,1024]{1,0:T(8,128)(2,1)S(1)} collective-permute-done((bf16[768,1024]{1,0:T(8,128)(2,1)S(1)}, bf16[768,1024]{1,0:T(8,128)(2,1)S(1)}, u32[]{:S(2)}, u32[]{:S(2)}) %collective-permute-start) | collective-permute-done | bytes 1572896 | tf_op jit(solution)/shard_map/ppermute | solution.py:156
  14.6 11.3 %shard_map.95 = (bf16[768,512]{1,0:T(8,128)(2,1)}, bf16[768,512]{1,0:T(8,128)(2,1)}, bf16[768,512]{1,0:T(8,128)(2,1)S(1)}, bf16[768,512]{1,0:T(8,128)(2,1)S(1)}) custom-call(s32[17]{0:T(128)S(1)} %pad_add_fusion.place_ref, bf16[768,1024]{1,0:T(8,128)(2,1)S(1)} %copy-done.6, bf16[768,1024]{1,0:T(8,128)(2,1)S(1)} %collective-permute-done.refs_1_, ...), custom_call_target="tpu_custom_call" | custom-call | flops 999999995904 | bytes 1 | tf_op jit(solution)/shard_map/pallas_call | solution.py:31
  27.7 5.8 %collective-permute-start.3 = (bf16[768,512]{1,0:T(8,128)(2,1)}, bf16[768,512]{1,0:T(8,128)(2,1)}, u32[]{:S(2)}, u32[]{:S(2)}) collective-permute-start(bf16[768,512]{1,0:T(8,128)(2,1)} %get-tuple-element.37.refs_1_.refs_0_), channel_id=1, source_target_pairs={{0,2},{1,3},{6,4},{7,5},{8,10},{9,11},{14,12},{15,13},{16,18},{17,... | collective-permute-start | bytes 2359304 | tf_op jit(solution)/shard_map/ppermute | solution.py:159
  35.9 6.1 %shard_map.97.refs_2_ = bf16[4,1024,512]{2,1,0:T(8,128)(2,1)} custom-call(s32[17]{0:T(128)S(1)} %pad_add_fusion.place_ref, bf16[1024,8192]{1,0:T(8,128)(2,1)} %refs_19_.1, bf16[3072,768]{1,0:T(8,128)(2,1)S(1)} %shard_map.96.refs_1_.refs_3_), custom_call_target="tpu_custom_call" | custom-call | flops 999999995904 | bytes 1 | tf_op jit(solution)/shard_map/pallas_call | solution.py:31
  44.2 6.6 %collective-permute-done.3.refs_1_ = bf16[768,512]{1,0:T(8,128)(2,1)} collective-permute-done((bf16[768,512]{1,0:T(8,128)(2,1)}, bf16[768,512]{1,0:T(8,128)(2,1)}, u32[]{:S(2)}, u32[]{:S(2)}) %collective-permute-start.3) | collective-permute-done | bytes 786464 | tf_op jit(solution)/shard_map/ppermute | solution.py:159
  50.8 3.3 shard_map.98.refs_4_
  55.6 10.8 %shard_map.99 = (bf16[768,512]{1,0:T(8,128)(2,1)}, bf16[768,512]{1,0:T(8,128)(2,1)}, bf16[768,512]{1,0:T(8,128)(2,1)S(1)}, bf16[768,512]{1,0:T(8,128)(2,1)S(1)}) custom-call(s32[17]{0:T(128)S(1)} %pad_add_fusion.place_ref, bf16[768,1024]{1,0:T(8,128)(2,1)S(1)} %copy-done.7, bf16[768,1024]{1,0:T(8,128)(2,1)S(1)} %copy-done.9, bf16[1024,8192]{1,0:T(8,128)(2,1)} %refs_19_.1, ...), custom_call_target="tpu_custom_call" | custom-call | flops 999999995904 | bytes 1 | tf_op jit(solution)/shard_map/pallas_call | solution.py:31
  71.2 13.0 %collective-permute-start.6 = (bf16[768,512]{1,0:T(8,128)(2,1)S(1)}, bf16[768,512]{1,0:T(8,128)(2,1)S(1)}, u32[]{:S(2)}, u32[]{:S(2)}) collective-permute-start(bf16[768,512]{1,0:T(8,128)(2,1)S(1)} %shard_map.100.refs_2_), channel_id=1, source_target_pairs={{0,2},{1,3},{4,6},{5,7},{2,0},{3,1},{6,4},{7,5},{8,10},{9,11},{12,... | collective-permute-start | bytes 2359304 | tf_op jit(solution)/shard_map/ppermute | solution.py:159
  87.0 15.2 %collective-permute-done.6.refs_1_ = bf16[768,512]{1,0:T(8,128)(2,1)S(1)} collective-permute-done((bf16[768,512]{1,0:T(8,128)(2,1)S(1)}, bf16[768,512]{1,0:T(8,128)(2,1)S(1)}, u32[]{:S(2)}, u32[]{:S(2)}) %collective-permute-start.6) | collective-permute-done | bytes 786464 | tf_op jit(solution)/shard_map/ppermute | solution.py:159
  104.5 5.4 %shard_map.102 = (bf16[768,512]{1,0:T(8,128)(2,1)S(1)}, bf16[2,384,512]{2,1,0:T(8,128)(2,1)}, bf16[2,384,512]{2,1,0:T(8,128)(2,1)}, bf16[384,512]{1,0:T(8,128)(2,1)S(1)}, bf16[384,512]{1,0:T(8,128)(2,1)S(1)}) custom-call(s32[17]{0:T(128)S(1)} %pad_add_fusion.place_ref, bf16[768,512]{1,0:T(8,128)(2,1)S(1)} %copy-done.18, ...), custom_call_target="tpu_custom_call" | custom-call | flops 999999995904 | bytes 1 | tf_op jit(solution)/shard_map/pallas_call | solution.py:31
  110.0 5.4 %collective-permute-done.4.refs_1_ = bf16[768,512]{1,0:T(8,128)(2,1)} collective-permute-done((bf16[768,512]{1,0:T(8,128)(2,1)}, bf16[768,512]{1,0:T(8,128)(2,1)}, u32[]{:S(2)}, u32[]{:S(2)}) %collective-permute-start.4) | collective-permute-done | bytes 786464 | tf_op jit(solution)/shard_map/ppermute | solution.py:159
  118.2 7.0 %collective-permute-start.11 = (bf16[768,512]{1,0:T(8,128)(2,1)}, bf16[768,512]{1,0:T(8,128)(2,1)}, u32[]{:S(2)}, u32[]{:S(2)}) collective-permute-start(bf16[768,512]{1,0:T(8,128)(2,1)} %get-tuple-element.45.refs_0_), channel_id=1, source_target_pairs={{0,2},{1,3},{6,4},{7,5},{8,10},{9,11},{14,12},{15,13},{16,18},{17,... | collective-permute-start | bytes 2359304 | tf_op jit(solution)/shard_map/ppermute | solution.py:159
  129.8 7.8 %collective-permute-done.11.refs_1_ = bf16[768,512]{1,0:T(8,128)(2,1)} collective-permute-done((bf16[768,512]{1,0:T(8,128)(2,1)}, bf16[768,512]{1,0:T(8,128)(2,1)}, u32[]{:S(2)}, u32[]{:S(2)}) %collective-permute-start.11) | collective-permute-done | bytes 786464 | tf_op jit(solution)/shard_map/ppermute | solution.py:159
  148.0 4.3 %collective-permute-start.10 = (bf16[768,512]{1,0:T(8,128)(2,1)}, bf16[768,512]{1,0:T(8,128)(2,1)}, u32[]{:S(2)}, u32[]{:S(2)}) collective-permute-start(bf16[768,512]{1,0:T(8,128)(2,1)} %shard_map.104.refs_2_), channel_id=1, source_target_pairs={{0,2},{1,3},{4,6},{5,7},{2,0},{3,1},{6,4},{7,5},{8,10},{9,11},{12,... | collective-permute-start | bytes 2359304 | tf_op jit(solution)/shard_map/ppermute | solution.py:159
  153.9 5.3 %shard_map.107 = (bf16[384,512]{1,0:T(8,128)(2,1)}, bf16[384,512]{1,0:T(8,128)(2,1)}, f32[768,1024]{1,0:T(8,128)}, f32[768,1024]{1,0:T(8,128)}) custom-call(s32[17]{0:T(128)S(1)} %pad_add_fusion.place_ref, bf16[768,512]{1,0:T(8,128)(2,1)S(1)} %get-tuple-element.44.refs_2_.refs_0_, bf16[2,384,512]{2,1,0:T(8,128)(2,1)} %collective-permute-done.13.refs_1_, ...), custom_call_target="tpu_custom_call" | custom-call | flops 999999995904 | bytes 1 | tf_op jit(solution)/shard_map/pallas_call | solution.py:31
  160.0 4.6 %collective-permute-done.10.refs_1_ = bf16[768,512]{1,0:T(8,128)(2,1)} collective-permute-done((bf16[768,512]{1,0:T(8,128)(2,1)}, bf16[768,512]{1,0:T(8,128)(2,1)}, u32[]{:S(2)}, u32[]{:S(2)}) %collective-permute-start.10) | collective-permute-done | bytes 786464 | tf_op jit(solution)/shard_map/ppermute | solution.py:159
  167.0 6.9 %shard_map.108 = (bf16[768,512]{1,0:T(8,128)(2,1)S(1)}, bf16[2,384,512]{2,1,0:T(8,128)(2,1)}, bf16[2,384,512]{2,1,0:T(8,128)(2,1)}, bf16[384,512]{1,0:T(8,128)(2,1)S(1)}, bf16[384,512]{1,0:T(8,128)(2,1)S(1)}) custom-call(s32[17]{0:T(128)S(1)} %pad_add_fusion.place_ref, bf16[768,512]{1,0:T(8,128)(2,1)S(1)} %copy-done.22, ...), custom_call_target="tpu_custom_call" | custom-call | flops 999999995904 | bytes 1 | tf_op jit(solution)/shard_map/pallas_call | solution.py:31
  181.0 13.6 %collective-permute-done.17.refs_1_ = bf16[2,384,512]{2,1,0:T(8,128)(2,1)} collective-permute-done((bf16[2,384,512]{2,1,0:T(8,128)(2,1)}, bf16[2,384,512]{2,1,0:T(8,128)(2,1)}, u32[]{:S(2)}, u32[]{:S(2)}) %collective-permute-start.17) | collective-permute-done | bytes 786464 | tf_op jit(solution)/shard_map/ppermute | solution.py:162
  200.1 8.3 %collective-permute-done.23.refs_2_ = bf16[2,384,512]{2,1,0:T(8,128)(2,1)} collective-permute-done((bf16[2,384,512]{2,1,0:T(8,128)(2,1)}, bf16[2,384,512]{2,1,0:T(8,128)(2,1)}, u32[]{:S(2)}, u32[]{:S(2)}) %collective-permute-start.23) | collective-permute-done | bytes 786464 | tf_op jit(solution)/shard_map/ppermute | solution.py:162
  208.6 6.8 %shard_map.111.refs_9_.refs_0_ = bf16[768,512]{1,0:T(8,128)(2,1)} custom-call(s32[17]{0:T(128)S(1)} %pad_add_fusion.place_ref, bf16[384,512]{1,0:T(8,128)(2,1)} %get-tuple-element.52.refs_4_.refs_0_, bf16[384,512]{1,0:T(8,128)(2,1)} %get-tuple-element.58.refs_2_.refs_1_, bf16[2,384,512]{2,1,0:T(8,128)(2,1)} %collective-permute-done.23.refs_2_, ...), custom_call_target="tpu_custom_call" | custom-call | flops 999999995904 | bytes 1 | tf_op jit(solution)/shard_map/pallas_call | solution.py:31
  215.4 5.4 %shard_map.112 = (bf16[384,512]{1,0:T(8,128)(2,1)S(1)}, bf16[384,512]{1,0:T(8,128)(2,1)S(1)}, f32[768,1024]{1,0:T(8,128)}, f32[768,1024]{1,0:T(8,128)}) custom-call(s32[17]{0:T(128)S(1)} %pad_add_fusion.place_ref, bf16[768,512]{1,0:T(8,128)(2,1)S(1)} %copy-done.24, ...), custom_call_target="tpu_custom_call", output_to_operand_aliasing={{2}: (8, {}), {3}: (9, {})} | custom-call | flops 999999995904 | bytes 1 | tf_op jit(solution)/shard_map/pallas_call | solution.py:31
  226.7 6.1 %collective-permute-done.25.refs_1_.refs_4_ = bf16[384,512]{1,0:T(8,128)(2,1)S(1)} collective-permute-done((bf16[384,512]{1,0:T(8,128)(2,1)S(1)}, bf16[384,512]{1,0:T(8,128)(2,1)S(1)}, u32[]{:S(2)}, u32[]{:S(2)}) %collective-permute-start.25) | collective-permute-done | bytes 393248 | tf_op jit(solution)/shard_map/ppermute | solution.py:162
  240.0 4.4 %collective-permute-done.29.refs_0_ = bf16[768,512]{1,0:T(8,128)(2,1)} collective-permute-done((bf16[768,512]{1,0:T(8,128)(2,1)}, bf16[768,512]{1,0:T(8,128)(2,1)}, u32[]{:S(2)}, u32[]{:S(2)}) %collective-permute-start.29) | collective-permute-done | bytes 786464 | tf_op jit(solution)/shard_map/ppermute | solution.py:159
  249.0 5.9 %shard_map.116.refs_2_.refs_0_ = bf16[768,512]{1,0:T(8,128)(2,1)} custom-call(s32[17]{0:T(128)S(1)} %pad_add_fusion.place_ref, bf16[384,512]{1,0:T(8,128)(2,1)S(1)} %get-tuple-element.67.refs_0_.refs_4_, bf16[384,512]{1,0:T(8,128)(2,1)S(1)} %get-tuple-element.68.refs_2_.refs_1_, bf16[2,384,512]{2,1,0:T(8,128)(2,1)} %collective-permute-done.27.refs_2_, ...), custom_call_target="tpu_custom_call" | custom-call | flops 999999995904 | bytes 1 | tf_op jit(solution)/shard_map/pallas_call | solution.py:31
  261.1 9.1 %collective-permute-start.31 = (bf16[768,512]{1,0:T(8,128)(2,1)}, bf16[768,512]{1,0:T(8,128)(2,1)}, u32[]{:S(2)}, u32[]{:S(2)}) collective-permute-start(bf16[768,512]{1,0:T(8,128)(2,1)} %shard_map.116.refs_2_.refs_0_), channel_id=1, source_target_pairs={{0,2},{1,3},{4,6},{5,7},{2,0},{3,1},{6,4},{7,5},{8,10},{9,11},{12,... | collective-permute-start | bytes 2359304 | tf_op jit(solution)/shard_map/ppermute | solution.py:159
  270.2 9.3 %collective-permute-done.35.refs_8_ = bf16[768,512]{1,0:T(8,128)(2,1)S(1)} collective-permute-done((bf16[768,512]{1,0:T(8,128)(2,1)}, bf16[768,512]{1,0:T(8,128)(2,1)S(1)}, u32[]{:S(2)}, u32[]{:S(2)}) %collective-permute-start.35) | collective-permute-done | bytes 786464 | tf_op jit(solution)/shard_map/ppermute | solution.py:159
  279.5 7.6 %shard_map.118.refs_1_ = bf16[768,1024]{1,0:T(8,128)(2,1)} custom-call(s32[17]{0:T(128)S(1)} %pad_add_fusion.place_ref, bf16[768,512]{1,0:T(8,128)(2,1)} %shard_map.111.refs_9_.refs_0_, bf16[4,1024,512]{2,1,0:T(8,128)(2,1)S(1)} %collective-permute-done.1.refs_3_.refs_1_.refs_6_.refs_9_, bf16[768,512]{1,0:T(8,128)(2,1)} %shard_map.115.refs_10_.refs_2_, ...), custom_call_target="tpu_custom_call" | custom-call | flops 999999995904 | bytes 1 | tf_op jit(solution)/shard_map/pallas_call | solution.py:31
  288.9 3.4 %collective-permute-done.31.refs_0_ = bf16[768,512]{1,0:T(8,128)(2,1)} collective-permute-done((bf16[768,512]{1,0:T(8,128)(2,1)}, bf16[768,512]{1,0:T(8,128)(2,1)}, u32[]{:S(2)}, u32[]{:S(2)}) %collective-permute-start.31) | collective-permute-done | bytes 786464 | tf_op jit(solution)/shard_map/ppermute | solution.py:159
  295.0 7.6 %shard_map.121.refs_2_.refs_21_ = f32[768,1024]{1,0:T(8,128)S(1)} custom-call(s32[17]{0:T(128)S(1)} %pad_add_fusion.place_ref, bf16[768,512]{1,0:T(8,128)(2,1)} %shard_map.111.refs_9_.refs_0_, bf16[1024,8192]{1,0:T(8,128)(2,1)} %refs_19_.1, bf16[768,512]{1,0:T(8,128)(2,1)} %shard_map.115.refs_10_.refs_2_, bf16[1024,8192]{1,0:T(8,128)(2,1)} %refs_19_.1, ...), custom_call_target="tpu_custom_call" | custom-call | flops 999999995904 | bytes 1 | tf_op jit(solution)/shard_map/pallas_call | solution.py:31
  307.4 17.3 %collective-permute-done.38.refs_8_ = bf16[768,512]{1,0:T(8,128)(2,1)S(1)} collective-permute-done((bf16[768,512]{1,0:T(8,128)(2,1)}, bf16[768,512]{1,0:T(8,128)(2,1)S(1)}, u32[]{:S(2)}, u32[]{:S(2)}) %collective-permute-start.38) | collective-permute-done | bytes 786464 | tf_op jit(solution)/shard_map/ppermute | solution.py:159
  327.0 12.9 %shard_map.123 = f32[768,1024]{1,0:T(8,128)} custom-call(s32[17]{0:T(128)S(1)} %pad_add_fusion.place_ref, bf16[768,512]{1,0:T(8,128)(2,1)} %shard_map.116.refs_2_.refs_0_, bf16[1024,8192]{1,0:T(8,128)(2,1)} %refs_19_.1, bf16[768,512]{1,0:T(8,128)(2,1)} %shard_map.120.refs_10_.refs_2_, bf16[1024,8192]{1,0:T(8,128)(2,1)} %refs_19_.1, ...), custom_call_target="tpu_custom_call" | custom-call | flops 999999995904 | bytes 1 | tf_op jit(solution)/shard_map/pallas_call | solution.py:31
  (143 shorter events, 89.9 us)
Async XLA Ops:
  27.7 23.1 %collective-permute-start.3 = (bf16[768,512]{1,0:T(8,128)(2,1)}, bf16[768,512]{1,0:T(8,128)(2,1)}, u32[]{:S(2)}, u32[]{:S(2)}) collective-permute-start(bf16[768,512]{1,0:T(8,128)(2,1)} %get-tuple-element.37.refs_1_.refs_0_), channel_id=1, source_target_pairs={{0,2},{1,3},{6,4},{7,5},{8,10},{9,11},{14,12},{15,13},{16,18},{17,... | collective-permute-start | bytes 2359304 | tf_op jit(solution)/shard_map/ppermute | solution.py:159
  42.0 13.6 %collective-permute-start.2 = (bf16[4,1024,512]{2,1,0:T(8,128)(2,1)}, bf16[4,1024,512]{2,1,0:T(8,128)(2,1)}, u32[]{:S(2)}, u32[]{:S(2)}) collective-permute-start(bf16[4,1024,512]{2,1,0:T(8,128)(2,1)} %shard_map.97.refs_2_), channel_id=1, source_target_pairs={{0,1},{1,0},{2,3},{3,2},{4,5},{5,4},{6,7},{7,6},{8,9},{9,8},{10,11... | collective-permute-start | bytes 12582920 | tf_op jit(solution)/shard_map/ppermute | solution.py:156
  42.0 26.3 %collective-permute-start.7 = (bf16[768,512]{1,0:T(8,128)(2,1)}, bf16[768,512]{1,0:T(8,128)(2,1)}, u32[]{:S(2)}, u32[]{:S(2)}) collective-permute-start(bf16[768,512]{1,0:T(8,128)(2,1)} %get-tuple-element.43.refs_0_), channel_id=1, source_target_pairs={{0,2},{1,3},{6,4},{7,5},{8,10},{9,11},{14,12},{15,13},{16,18},{17,... | collective-permute-start | bytes 2359304 | tf_op jit(solution)/shard_map/ppermute | solution.py:159
  70.5 16.6 %collective-permute-start.8 = (bf16[768,512]{1,0:T(8,128)(2,1)S(1)}, bf16[768,512]{1,0:T(8,128)(2,1)S(1)}, u32[]{:S(2)}, u32[]{:S(2)}) collective-permute-start(bf16[768,512]{1,0:T(8,128)(2,1)S(1)} %shard_map.101.refs_4_), channel_id=1, source_target_pairs={{2,4},{3,5},{4,2},{5,3},{10,12},{11,13},{12,10},{13,11},{18,20},{1... | collective-permute-start | bytes 2359304 | tf_op jit(solution)/shard_map/ppermute | solution.py:159
  71.2 31.0 %collective-permute-start.6 = (bf16[768,512]{1,0:T(8,128)(2,1)S(1)}, bf16[768,512]{1,0:T(8,128)(2,1)S(1)}, u32[]{:S(2)}, u32[]{:S(2)}) collective-permute-start(bf16[768,512]{1,0:T(8,128)(2,1)S(1)} %shard_map.100.refs_2_), channel_id=1, source_target_pairs={{0,2},{1,3},{4,6},{5,7},{2,0},{3,1},{6,4},{7,5},{8,10},{9,11},{12,... | collective-permute-start | bytes 2359304 | tf_op jit(solution)/shard_map/ppermute | solution.py:159
  84.2 31.2 %collective-permute-start.4 = (bf16[768,512]{1,0:T(8,128)(2,1)}, bf16[768,512]{1,0:T(8,128)(2,1)}, u32[]{:S(2)}, u32[]{:S(2)}) collective-permute-start(bf16[768,512]{1,0:T(8,128)(2,1)} %get-tuple-element.40.refs_2_.refs_0_), channel_id=1, source_target_pairs={{0,2},{1,3},{6,4},{7,5},{8,10},{9,11},{14,12},{15,13},{16,18},{17,... | collective-permute-start | bytes 2359304 | tf_op jit(solution)/shard_map/ppermute | solution.py:159
  118.2 19.4 %collective-permute-start.11 = (bf16[768,512]{1,0:T(8,128)(2,1)}, bf16[768,512]{1,0:T(8,128)(2,1)}, u32[]{:S(2)}, u32[]{:S(2)}) collective-permute-start(bf16[768,512]{1,0:T(8,128)(2,1)} %get-tuple-element.45.refs_0_), channel_id=1, source_target_pairs={{0,2},{1,3},{6,4},{7,5},{8,10},{9,11},{14,12},{15,13},{16,18},{17,... | collective-permute-start | bytes 2359304 | tf_op jit(solution)/shard_map/ppermute | solution.py:159
  125.2 15.6 %collective-permute-start.13 = (bf16[2,384,512]{2,1,0:T(8,128)(2,1)}, bf16[2,384,512]{2,1,0:T(8,128)(2,1)}, u32[]{:S(2)}, u32[]{:S(2)}) collective-permute-start(bf16[2,384,512]{2,1,0:T(8,128)(2,1)} %get-tuple-element.46), channel_id=1, source_target_pairs={{0,8},{8,0},{16,24},{24,16},{1,9},{9,1},{17,25},{25,17},{2,10},{10... | collective-permute-start | bytes 2359304 | tf_op jit(solution)/shard_map/ppermute | solution.py:162
  126.7 15.5 %collective-permute-start.14 = (bf16[2,384,512]{2,1,0:T(8,128)(2,1)}, bf16[2,384,512]{2,1,0:T(8,128)(2,1)}, u32[]{:S(2)}, u32[]{:S(2)}) collective-permute-start(bf16[2,384,512]{2,1,0:T(8,128)(2,1)} %get-tuple-element.47), channel_id=1, source_target_pairs={{0,16},{8,24},{16,0},{24,8},{1,17},{9,25},{17,1},{25,9},{2,18},{10... | collective-permute-start | bytes 2359304 | tf_op jit(solution)/shard_map/ppermute | solution.py:162
  146.4 13.6 %collective-permute-start.12 = (bf16[768,512]{1,0:T(8,128)(2,1)}, bf16[768,512]{1,0:T(8,128)(2,1)}, u32[]{:S(2)}, u32[]{:S(2)}) collective-permute-start(bf16[768,512]{1,0:T(8,128)(2,1)} %shard_map.105.refs_4_), channel_id=1, source_target_pairs={{2,4},{3,5},{4,2},{5,3},{10,12},{11,13},{12,10},{13,11},{18,20},{1... | collective-permute-start | bytes 2359304 | tf_op jit(solution)/shard_map/ppermute | solution.py:159
  148.0 16.7 %collective-permute-start.10 = (bf16[768,512]{1,0:T(8,128)(2,1)}, bf16[768,512]{1,0:T(8,128)(2,1)}, u32[]{:S(2)}, u32[]{:S(2)}) collective-permute-start(bf16[768,512]{1,0:T(8,128)(2,1)} %shard_map.104.refs_2_), channel_id=1, source_target_pairs={{0,2},{1,3},{4,6},{5,7},{2,0},{3,1},{6,4},{7,5},{8,10},{9,11},{12,... | collective-permute-start | bytes 2359304 | tf_op jit(solution)/shard_map/ppermute | solution.py:159
  159.2 15.7 %collective-permute-start.19 = (bf16[384,512]{1,0:T(8,128)(2,1)}, bf16[384,512]{1,0:T(8,128)(2,1)}, u32[]{:S(2)}, u32[]{:S(2)}) collective-permute-start(bf16[384,512]{1,0:T(8,128)(2,1)} %get-tuple-element.52.refs_4_.refs_0_), channel_id=1, source_target_pairs={{0,16},{8,24},{16,0},{24,8},{1,17},{9,25},{17,1},{25,9},{2,18},{10... | collective-permute-start | bytes 1179656 | tf_op jit(solution)/shard_map/ppermute | solution.py:162
  159.7 15.2 %collective-permute-start.20 = (bf16[384,512]{1,0:T(8,128)(2,1)}, bf16[384,512]{1,0:T(8,128)(2,1)}, u32[]{:S(2)}, u32[]{:S(2)}) collective-permute-start(bf16[384,512]{1,0:T(8,128)(2,1)} %get-tuple-element.58.refs_2_.refs_1_), channel_id=1, source_target_pairs={{0,8},{8,0},{16,24},{24,16},{1,9},{9,1},{17,25},{25,17},{2,10},{10... | collective-permute-start | bytes 1179656 | tf_op jit(solution)/shard_map/ppermute | solution.py:162
  173.9 20.8 %collective-permute-start.17 = (bf16[2,384,512]{2,1,0:T(8,128)(2,1)}, bf16[2,384,512]{2,1,0:T(8,128)(2,1)}, u32[]{:S(2)}, u32[]{:S(2)}) collective-permute-start(bf16[2,384,512]{2,1,0:T(8,128)(2,1)} %get-tuple-element.54), channel_id=1, source_target_pairs={{0,8},{8,0},{16,24},{24,16},{1,9},{9,1},{17,25},{25,17},{2,10},{10... | collective-permute-start | bytes 2359304 | tf_op jit(solution)/shard_map/ppermute | solution.py:162
  174.4 20.8 %collective-permute-start.18 = (bf16[2,384,512]{2,1,0:T(8,128)(2,1)}, bf16[2,384,512]{2,1,0:T(8,128)(2,1)}, u32[]{:S(2)}, u32[]{:S(2)}) collective-permute-start(bf16[2,384,512]{2,1,0:T(8,128)(2,1)} %get-tuple-element.55), channel_id=1, source_target_pairs={{0,16},{8,24},{16,0},{24,8},{1,17},{9,25},{17,1},{25,9},{2,18},{10... | collective-permute-start | bytes 2359304 | tf_op jit(solution)/shard_map/ppermute | solution.py:162
  178.0 30.4 %collective-permute-start.23 = (bf16[2,384,512]{2,1,0:T(8,128)(2,1)}, bf16[2,384,512]{2,1,0:T(8,128)(2,1)}, u32[]{:S(2)}, u32[]{:S(2)}) collective-permute-start(bf16[2,384,512]{2,1,0:T(8,128)(2,1)} %get-tuple-element.59.refs_4_), channel_id=1, source_target_pairs={{0,8},{8,0},{16,24},{24,16},{1,9},{9,1},{17,25},{25,17},{2,10},{10... | collective-permute-start | bytes 2359304 | tf_op jit(solution)/shard_map/ppermute | solution.py:162
  179.5 29.1 %collective-permute-start.24 = (bf16[2,384,512]{2,1,0:T(8,128)(2,1)}, bf16[2,384,512]{2,1,0:T(8,128)(2,1)}, u32[]{:S(2)}, u32[]{:S(2)}) collective-permute-start(bf16[2,384,512]{2,1,0:T(8,128)(2,1)} %get-tuple-element.64), channel_id=1, source_target_pairs={{0,16},{8,24},{16,0},{24,8},{1,17},{9,25},{17,1},{25,9},{2,18},{10... | collective-permute-start | bytes 2359304 | tf_op jit(solution)/shard_map/ppermute | solution.py:162
  198.1 17.3 %collective-permute-start.21 = (bf16[384,512]{1,0:T(8,128)(2,1)}, bf16[384,512]{1,0:T(8,128)(2,1)}, u32[]{:S(2)}, u32[]{:S(2)}) collective-permute-start(bf16[384,512]{1,0:T(8,128)(2,1)} %get-tuple-element.60.refs_10_), channel_id=1, source_target_pairs={{0,16},{8,24},{16,0},{24,8},{1,17},{9,25},{17,1},{25,9},{2,18},{10... | collective-permute-start | bytes 1179656 | tf_op jit(solution)/shard_map/ppermute | solution.py:162
  198.5 16.8 %collective-permute-start.22 = (bf16[384,512]{1,0:T(8,128)(2,1)}, bf16[384,512]{1,0:T(8,128)(2,1)}, u32[]{:S(2)}, u32[]{:S(2)}) collective-permute-start(bf16[384,512]{1,0:T(8,128)(2,1)} %get-tuple-element.61), channel_id=1, source_target_pairs={{0,8},{8,0},{16,24},{24,16},{1,9},{9,1},{17,25},{25,17},{2,10},{10... | collective-permute-start | bytes 1179656 | tf_op jit(solution)/shard_map/ppermute | solution.py:162
  222.8 15.4 %collective-permute-start.30 = (bf16[768,512]{1,0:T(8,128)(2,1)}, bf16[768,512]{1,0:T(8,128)(2,1)}, u32[]{:S(2)}, u32[]{:S(2)}) collective-permute-start(bf16[768,512]{1,0:T(8,128)(2,1)} %shard_map.111.refs_9_.refs_0_), channel_id=1, source_target_pairs={{2,4},{3,5},{4,2},{5,3},{10,12},{11,13},{12,10},{13,11},{18,20},{1... | collective-permute-start | bytes 2359304 | tf_op jit(solution)/shard_map/ppermute | solution.py:159
  224.3 20.0 %collective-permute-start.29 = (bf16[768,512]{1,0:T(8,128)(2,1)}, bf16[768,512]{1,0:T(8,128)(2,1)}, u32[]{:S(2)}, u32[]{:S(2)}) collective-permute-start(bf16[768,512]{1,0:T(8,128)(2,1)} %shard_map.111.refs_9_.refs_0_), channel_id=1, source_target_pairs={{0,2},{1,3},{4,6},{5,7},{2,0},{3,1},{6,4},{7,5},{8,10},{9,11},{12,... | collective-permute-start | bytes 2359304 | tf_op jit(solution)/shard_map/ppermute | solution.py:159
  238.7 18.9 %collective-permute-start.33 = (bf16[768,512]{1,0:T(8,128)(2,1)}, bf16[768,512]{1,0:T(8,128)(2,1)}, u32[]{:S(2)}, u32[]{:S(2)}) collective-permute-start(bf16[768,512]{1,0:T(8,128)(2,1)} %shard_map.114.refs_1_.refs_4_), channel_id=1, source_target_pairs={{4,6},{5,7},{2,0},{3,1},{12,14},{13,15},{10,8},{11,9},{20,22},{21,... | collective-permute-start | bytes 2359304 | tf_op jit(solution)/shard_map/ppermute | solution.py:159
  258.2 21.3 %collective-permute-start.35 = (bf16[768,512]{1,0:T(8,128)(2,1)}, bf16[768,512]{1,0:T(8,128)(2,1)S(1)}, u32[]{:S(2)}, u32[]{:S(2)}) collective-permute-start(bf16[768,512]{1,0:T(8,128)(2,1)} %shard_map.117.refs_7_.refs_10_), channel_id=1, source_target_pairs={{4,6},{5,7},{2,0},{3,1},{12,14},{13,15},{10,8},{11,9},{20,22},{21,... | collective-permute-start | bytes 2359304 | tf_op jit(solution)/shard_map/ppermute | solution.py:159
  259.5 27.5 %collective-permute-start.32 = (bf16[768,512]{1,0:T(8,128)(2,1)}, bf16[768,512]{1,0:T(8,128)(2,1)}, u32[]{:S(2)}, u32[]{:S(2)}) collective-permute-start(bf16[768,512]{1,0:T(8,128)(2,1)} %shard_map.116.refs_2_.refs_0_), channel_id=1, source_target_pairs={{2,4},{3,5},{4,2},{5,3},{10,12},{11,13},{12,10},{13,11},{18,20},{1... | collective-permute-start | bytes 2359304 | tf_op jit(solution)/shard_map/ppermute | solution.py:159
  261.1 31.2 %collective-permute-start.31 = (bf16[768,512]{1,0:T(8,128)(2,1)}, bf16[768,512]{1,0:T(8,128)(2,1)}, u32[]{:S(2)}, u32[]{:S(2)}) collective-permute-start(bf16[768,512]{1,0:T(8,128)(2,1)} %shard_map.116.refs_2_.refs_0_), channel_id=1, source_target_pairs={{0,2},{1,3},{4,6},{5,7},{2,0},{3,1},{6,4},{7,5},{8,10},{9,11},{12,... | collective-permute-start | bytes 2359304 | tf_op jit(solution)/shard_map/ppermute | solution.py:159
  270.2 36.6 %collective-permute-start.39 = (bf16[768,512]{1,0:T(8,128)(2,1)}, bf16[768,512]{1,0:T(8,128)(2,1)}, u32[]{:S(2)}, u32[]{:S(2)}) collective-permute-start(bf16[768,512]{1,0:T(8,128)(2,1)} %shard_map.116.refs_2_.refs_0_), channel_id=1, source_target_pairs={{0,1},{1,0},{2,3},{3,2},{4,5},{5,4},{6,7},{7,6},{8,9},{9,8},{10,11... | collective-permute-start | bytes 2359304 | tf_op jit(solution)/shard_map/ppermute | solution.py:156
  287.6 17.3 %collective-permute-start.36 = (bf16[768,512]{1,0:T(8,128)(2,1)}, bf16[768,512]{1,0:T(8,128)(2,1)}, u32[]{:S(2)}, u32[]{:S(2)}) collective-permute-start(bf16[768,512]{1,0:T(8,128)(2,1)} %shard_map.119.refs_1_.refs_4_), channel_id=1, source_target_pairs={{4,6},{5,7},{2,0},{3,1},{12,14},{13,15},{10,8},{11,9},{20,22},{21,... | collective-permute-start | bytes 2359304 | tf_op jit(solution)/shard_map/ppermute | solution.py:159
  294.5 30.2 %collective-permute-start.45 = (bf16[768,1024]{1,0:T(8,128)(2,1)}, bf16[768,1024]{1,0:T(8,128)(2,1)}, u32[]{:S(2)}, u32[]{:S(2)}) collective-permute-start(bf16[768,1024]{1,0:T(8,128)(2,1)} %shard_map.118.refs_1_), channel_id=1, source_target_pairs={{0,1},{1,0},{2,3},{3,2},{4,5},{5,4},{6,7},{7,6},{8,9},{9,8},{10,11... | collective-permute-start | bytes 4718600 | tf_op jit(solution)/shard_map/ppermute | solution.py:156
  305.4 19.3 %collective-permute-start.38 = (bf16[768,512]{1,0:T(8,128)(2,1)}, bf16[768,512]{1,0:T(8,128)(2,1)S(1)}, u32[]{:S(2)}, u32[]{:S(2)}) collective-permute-start(bf16[768,512]{1,0:T(8,128)(2,1)} %shard_map.122.refs_7_.refs_22_), channel_id=1, source_target_pairs={{4,6},{5,7},{2,0},{3,1},{12,14},{13,15},{10,8},{11,9},{20,22},{21,... | collective-permute-start | bytes 2359304 | tf_op jit(solution)/shard_map/ppermute | solution.py:159
  306.7 18.0 %collective-permute-start.41 = (bf16[768,512]{1,0:T(8,128)(2,1)}, bf16[768,512]{1,0:T(8,128)(2,1)S(1)}, u32[]{:S(2)}, u32[]{:S(2)}) collective-permute-start(bf16[768,512]{1,0:T(8,128)(2,1)} %shard_map.119.refs_1_.refs_4_), channel_id=1, source_target_pairs={{0,1},{1,0},{2,3},{3,2},{4,5},{5,4},{6,7},{7,6},{8,9},{9,8},{10,11... | collective-permute-start | bytes 2359304 | tf_op jit(solution)/shard_map/ppermute | solution.py:156
  306.8 17.9 %collective-permute-start.43 = (bf16[768,512]{1,0:T(8,128)(2,1)}, bf16[768,512]{1,0:T(8,128)(2,1)S(1)}, u32[]{:S(2)}, u32[]{:S(2)}) collective-permute-start(bf16[768,512]{1,0:T(8,128)(2,1)} %shard_map.122.refs_7_.refs_22_), channel_id=1, source_target_pairs={{0,1},{1,0},{2,3},{3,2},{4,5},{5,4},{6,7},{7,6},{8,9},{9,8},{10,11... | collective-permute-start | bytes 2359304 | tf_op jit(solution)/shard_map/ppermute | solution.py:156
  307.3 17.4 %collective-permute-start.42 = (bf16[768,512]{1,0:T(8,128)(2,1)}, bf16[768,512]{1,0:T(8,128)(2,1)S(1)}, u32[]{:S(2)}, u32[]{:S(2)}) collective-permute-start(bf16[768,512]{1,0:T(8,128)(2,1)} %collective-permute-done.36.refs_1_.refs_5_), channel_id=1, source_target_pairs={{0,1},{1,0},{2,3},{3,2},{4,5},{5,4},{6,7},{7,6},{8,9},{9,8},{10,11... | collective-permute-start | bytes 2359304 | tf_op jit(solution)/shard_map/ppermute | solution.py:156
  (39 other events, 325.4 us)

commit v2 on v1

--- a/solution.py
+++ b/solution.py
@@ -10,6 +10,7 @@
 
 F32, BF16 = jnp.float32, jnp.bfloat16
 VMEM_BYTES = 40 * 2**20
+FLOPS_A_US = 10**10
 ANY = pl.BlockSpec(memory_space=pl.ANY)
 
 
@@ -21,7 +22,7 @@
     def __init__(self):
         self.last = None
 
-    def call(self, kernel, place, inputs, in_specs, outs, out_specs, grid, aliases=None):
+    def call(self, us, kernel, place, inputs, in_specs, outs, out_specs, grid, aliases=None):
         n_in = len(inputs)
         extra = [] if self.last is None else [self.last]
 
@@ -39,7 +40,7 @@
             ),
             input_output_aliases={k + 1: v for k, v in (aliases or {}).items()},
             compiler_params=pltpu.CompilerParams(vmem_limit_bytes=VMEM_BYTES),
-            cost_estimate=pl.CostEstimate(flops=10**12, bytes_accessed=1, transcendentals=0),
+            cost_estimate=pl.CostEstimate(flops=int(us * FLOPS_A_US), bytes_accessed=1, transcendentals=0),
         )(place, *inputs, *extra)
         self.last = got[0]
         return got
@@ -84,23 +85,25 @@
 
 
 STEPS = {
-    "pack": -30.0,
-    "right": -10.0,
+    "pack first": -24.0,
+    "pack": -20.0,
+    "right first": -16.0,
+    "right": -4.0,
     "sum 1 1": 20.0,
     "sum 2 1": 37.0,
     "sum 2 0": 41.0,
     "left": 62.0,
-    "fold": 87.0,
-    "moments": 100.0,
-    "unfold": 116.0,
+    "fold": 88.0,
+    "moments": 101.0,
+    "unfold": 117.0,
     "back": 138.0,
     "pass 1 0": 163.1,
     "pass 1 1": 163.0,
     "pass 2 0": 184.0,
     "away": 205.0,
-    "near": 226.0,
+    "near": 186.0,
 }
-APART = 45.0
+APART = 58.0
 
 
 def nominal(step, index):
@@ -112,10 +115,16 @@
     return STEPS["left" if kind == "sum" else "pass 2 0"] - 1.0 / (1 + int(t)) + APART * index
 
 
-def run(tasks):
+TURNS = "000010100110101100101100101011111"
+
+
+def run(short, tasks):
     waiting = {k: next(task) for k, task in enumerate(tasks)}
+    turns = [int(k) for k in TURNS] if short else []
     while waiting:
         k = min(waiting, key=lambda k: (nominal(waiting[k], k), k))
+        if turns:
+            k = turns.pop(0)
         try:
             waiting[k] = next(tasks[k])
         except StopIteration:
@@ -181,6 +190,7 @@
             outs[0][...] = ins[0][...].T
 
         return order.call(
+            4.0,
             kernel,
             place,
             [left_basis],
@@ -190,7 +200,7 @@
             (row_size,),
         )[0]
 
-    def pack(first, width):
+    def pack(first, width, low, high):
         stride = columns // width
 
         def kernel(_, ins, outs):
@@ -198,21 +208,22 @@
 
         depth = right_basis.shape[0]
         return order.call(
+            1.5 * (high - low),
             kernel,
             place,
             [right_basis],
             [
                 pl.BlockSpec(
                     (depth, width),
-                    lambda s, p: (0, (2 * p[at_sum + s] + 1 - p[0]) * stride + first // width),
+                    lambda s, p: (0, (2 * p[at_sum + low + s] + 1 - p[0]) * stride + first // width),
                 )
             ],
-            [like((n_sum, depth, width), BF16)],
+            [like((high - low, depth, width), BF16)],
             [pl.BlockSpec((1, depth, width), lambda s, p: (s, 0, 0))],
-            (n_sum,),
+            (high - low,),
         )[0]
 
-    def right(packed, first, width):
+    def right(packed, first, width, low, high):
         stride = columns // width
         depth = right_basis.shape[0]
 
@@ -221,7 +232,7 @@
             value = jnp.dot(mine[...], basis[...], preferred_element_type=F32)
             value += jnp.dot(theirs[...], other[0], preferred_element_type=F32)
             value = value.astype(BF16)
-            for s in range(n_sum):
+            for s in range(high - low):
 
                 @pl.when(pl.program_id(0) == s)
                 def _(s=s):
@@ -229,6 +240,7 @@
 
         whole = pl.BlockSpec((height, depth), lambda s, p: (0, 0))
         return order.call(
+            2.5 * (high - low),
             kernel,
             place,
             [gradient, other_gradient, right_basis, packed],
@@ -237,13 +249,13 @@
                 whole,
                 pl.BlockSpec(
                     (depth, width),
-                    lambda s, p: (0, (2 * p[at_sum + s] + p[0]) * stride + first // width),
+                    lambda s, p: (0, (2 * p[at_sum + low + s] + p[0]) * stride + first // width),
                 ),
                 pl.BlockSpec((1, depth, width), lambda s, p: (s, 0, 0)),
             ],
-            [like((height, width), BF16)] * n_sum,
-            [pl.BlockSpec((height, width), lambda s, p: (0, 0))] * n_sum,
-            (n_sum,),
+            [like((height, width), BF16)] * (high - low),
+            [pl.BlockSpec((height, width), lambda s, p: (0, 0))] * (high - low),
+            (high - low,),
         )
 
     def add(x, y):
@@ -251,13 +263,14 @@
             outs[0][...] = (ins[0][...].astype(F32) + ins[1][...].astype(F32)).astype(BF16)
 
         spec = pl.BlockSpec(x.shape, lambda s, p: (0, 0))
-        return order.call(kernel, place, [x, y], [spec, spec], [like(x.shape, BF16)], [spec], (1,))[0]
+        return order.call(2.0, kernel, place, [x, y], [spec, spec], [like(x.shape, BF16)], [spec], (1,))[0]
 
     def hand_on(x, also=()):
         def kernel(_, ins, outs):
             pass
 
         return order.call(
+            0.5,
             kernel, place, [x, *also], [ANY] * (1 + len(also)), [like(x.shape, BF16)], [ANY], (1,), {0: 0}
         )[0]
 
@@ -296,6 +309,7 @@
         else:
             shapes = [(height, width)] * row_size
         return order.call(
+            5.0,
             kernel,
             place,
             [*terms, turned_left[0]],
@@ -316,6 +330,7 @@
         inputs = [then_y, got_x, then_x, got_y]
         outs = [like(then_y.shape, BF16)] * 2
         return order.call(
+            1.0,
             kernel, place, inputs, [whole_spec(x) for x in inputs], outs, [whole_spec(x) for x in outs], (1,)
         )
 
@@ -328,6 +343,7 @@
         inputs = [upper, got_upper, lower, got_lower]
         outs = [like((2, *upper.shape), BF16)] * 2
         return order.call(
+            1.5,
             kernel, place, inputs, [whole_spec(x) for x in inputs], outs, [whole_spec(x) for x in outs], (1,)
         )
 
@@ -354,6 +370,7 @@
             outs[0][...] = total.astype(BF16)
 
         return order.call(
+            5.0,
             kernel,
             place,
             [*inputs, *([left_basis] * row_size)],
@@ -412,6 +429,7 @@
             for k in range(2)
         ]
         upper, lower, *kept[:] = order.call(
+            5.0,
             kernel,
             place,
             [*inputs, first_moment, second_moment, *kept],
@@ -423,19 +441,20 @@
         )
         return upper, lower
 
-    def back(chunks, mine, dtype, ends=(), both=False):
+    def back(chunks, mine, dtype, ends=(), both=False, some=None):
         depth = right_basis.shape[0]
         tile = min(256, depth)
-        inputs, specs, layout = [], [], []
+        inputs, specs, layout, at_g = [], [], [], []
         whole = [pl.BlockSpec((height, width), lambda r, p: (0, 0)) for _, width, _, _ in chunks]
         for at_chunk, (first, width, packed, gathered) in enumerate(chunks):
             stride = columns // width
             for flip in range(2 if both else 1):
-                for g in range(n_gather):
+                for g in range(n_gather) if some is None else some:
                     xs = [swap(x) for x in gathered[g]] if flip else gathered[g]
                     inputs += xs
                     specs += [whole[at_chunk]] * len(xs)
                     layout.append(len(xs))
+                    at_g.append(g)
                     if mine:
 
                         def at(r, p, g=g, flip=flip, stride=stride, first=first, width=width):
@@ -445,50 +464,64 @@
                         inputs.append(right_basis)
                         specs.append(pl.BlockSpec((tile, width), at))
                     else:
-                        inputs.append(packed)
-                        specs.append(
-                            pl.BlockSpec((1, tile, width), lambda r, p, g=g: (p[at_same + g], r, 0))
-                        )
+                        for k, x in enumerate(packed):
+                            low, high = (0, 1) if k == 0 else (1, n_sum)
+
+                            def at_packed(r, p, g=g, low=low, high=high):
+                                return (jnp.clip(p[at_same + g] - low, 0, high - low - 1), r, 0)
+
+                            inputs.append(x)
+                            specs.append(pl.BlockSpec((1, tile, width), at_packed))
         out_spec = pl.BlockSpec((height, tile), lambda r, p: (0, r))
         n = len(inputs)
         inputs += list(ends)
         specs += [out_spec] * len(ends)
 
-        def kernel(_, ins, outs):
+        def kernel(p_ref, ins, outs):
             total = jnp.zeros((height, tile), F32)
             k = 0
-            for count in layout:
+            for j, count in enumerate(layout):
                 x = ins[k][...]
                 for more in ins[k + 1 : k + count]:
                     x = x + more[...]
-                basis = ins[k + count][...] if mine else ins[k + count][0]
+                if mine:
+                    basis = ins[k + count][...]
+                else:
+                    basis = jnp.where(p_ref[at_same + at_g[j]] == 0, ins[k + count][0], ins[k + count + 1][0])
                 total += lax.dot_general(x, basis, (((1,), (1,)), ((), ())), preferred_element_type=F32)
-                k += count + 1
+                k += count + (1 if mine else 2)
             for end in ins[n:]:
                 total += end[...].astype(F32)
             outs[0][...] = total.astype(dtype)
 
         return order.call(
+            8.0,
             kernel, place, inputs, specs, [like((height, depth), dtype)], [out_spec], (depth // tile,)
         )[0]
 
     held, totals, turned_left = [], [], []
 
     def chunk(index, first, width):
+        parts = ((0, 1), (1, n_sum))
+        yield "pack first"
+        packed = [swap(pack(first, width, *parts[0]))]
         yield "pack"
-        packed = swap(pack(first, width))
-        yield "right"
-        blocks = right(packed, first, width)
+        packed.append(swap(pack(first, width, *parts[1])))
+        yield "right first"
+        blocks = list(right(packed[0], first, width, *parts[0]))
+        early = along(blocks[0], streams(spots, False)[0][2])
         if index == 0:
             turned_left.append(turn())
+        yield "right"
+        blocks += right(packed[1], first, width, *parts[1])
         got = {}
-        for t, parity, pairs in streams(spots, False):
+        for t, parity, pairs in sorted(streams(spots, False), key=lambda x: x[:2]):
             value = blocks[sum_slot[t, parity]]
             before = got.get((t - 1, 1 - parity))
             if before is not None:
                 yield f"sum {t} {parity}"
                 value = add(value, before)
-            got[t, parity] = along(value, pairs)
+            got[t, parity] = along(value, pairs) if got else early
         yield "left"
         sums = left_sums([blocks[n_sum - 1]] + [got[k] for k in got if k[0] == spots - 2])
         if square:
@@ -533,13 +566,21 @@
         if not last:
             yield "away"
             away = swap(back(held[: index + 1], False, BF16))
+            totals.append(away)
+        else:
             yield "near"
-            totals.extend([away, back(held[: index + 1], True, F32)])
-        else:
+            half = n_gather - 1
+            most = back(held[-1:], True, F32, (), True, range(half))
+            if index:
+                totals.append(back(held[:-1], True, F32, [most]))
+            else:
+                totals.append(most)
             yield "end"
-            totals[:] = [back(held[-1:], True, F32, totals, True)]
-
-    run([chunk(k, first, width) for k, (first, width) in enumerate(widths)])
+            final = held[-1][3][-1]
+            final[:] = [hand_on(x) for x in final]
+            totals[:] = [back(held[-1:], True, F32, totals, True, range(half, n_gather))]
+
+    run(spots == 4, [chunk(k, first, width) for k, (first, width) in enumerate(widths)])
     return (kept[0], kept[1], totals[0])
 
 

time: 341 us -> 289 us (0.85)
  waiting for transfers between devices: 125 us -> 88.8 us
  Pallas kernels: 125 us -> 100 us
  local copies, waits for them, and re-layouts: 7.26 us -> 21.5 us
  starting transfers between devices: 81.2 us -> 76.1 us
    ppermute x20, waiting for transfers between devices: 79.1 us -> 48.5 us  [along(): lax.ppermute(x, 'col', [(2 * a + c, 2 * b + c) for a, b in pairs for c in...]
    pallas_call x30 -> x37, Pallas kernels: 125 us -> 100 us  [call(): pl.pallas_call(wrapped, out_shape=outs, grid_spec=pltpu.PrefetchScalarGri...]
    unnamed x50 -> x86, local copies, waits for them, and re-layouts: 6.57 us -> 20.8 us
    ppermute x20, starting transfers between devices: 62.5 us -> 54.3 us  [along(): lax.ppermute(x, 'col', [(2 * a + c, 2 * b + c) for a, b in pairs for c in...]
    ppermute x10 -> x12, waiting for transfers between devices: 11.2 us -> 4.77 us  [swap(): return lax.ppermute(x, 'col', [(j, j ^ 1) for j in range(col_size)])]
  transfers between devices with their start and end apart: 46 -> 48, of which waited for: 24 -> 25; matrix products, arithmetic and copies ran while one was open for 0% -> 0% of each run, Pallas kernels for 25% -> 30%
where the time goes in v2:
time: 289 us; the launch traced here: 288 us
  Pallas kernels  100 us (35%)
  waiting for transfers between devices  88.8 us (31%)
  starting transfers between devices  76.1 us (26%)
  local copies, waits for them, and re-layouts  21.5 us (7%)
    pallas_call x37, Pallas kernels, call(): pl.pallas_call(wrapped, out_shape=outs, grid_spec=pltpu.PrefetchScalarGri...  100 us
    ppermute x20, starting transfers between devices, along(): lax.ppermute(x, 'col', [(2 * a + c, 2 * b + c) for a, b in pairs for c in...  54.3 us
    ppermute x20, waiting for transfers between devices, along(): lax.ppermute(x, 'col', [(2 * a + c, 2 * b + c) for a, b in pairs for c in...  48.5 us
    ppermute x16, waiting for transfers between devices, to_partner(): return lax.ppermute(x, 'row', [(i, i ^ s) for i in range(row_size)])  35.6 us
    unnamed x86, local copies, waits for them, and re-layouts  20.8 us
    ppermute x16, starting transfers between devices, to_partner(): return lax.ppermute(x, 'row', [(i, i ^ s) for i in range(row_size)])  18.9 us
  transfers between devices with their start and end apart: 48, of which 25 were waited for; matrix products, arithmetic and copies ran while one was open for 0% of the time, Pallas kernels for 30%

profile of v2, /device:TPU:0, one launch (start us, length us, event | category | flops | bytes accessed | tf_op | source)
XLA Modules:
  0.0 288.0 jit_solution(7238200343523465575)
XLA Ops:
  4.2 3.2 %shard_map.95.refs_4_ = bf16[3,1024,512]{2,1,0:T(8,128)(2,1)S(1)} custom-call(s32[17]{0:T(128)S(1)} %pad_add_fusion.place_ref, bf16[1024,8192]{1,0:T(8,128)(2,1)} %refs_5_.5, bf16[1,1024,512]{2,1,0:T(8,128)(2,1)S(1)} %shard_map.94.refs_1_), custom_call_target="tpu_custom_call" | custom-call | flops 44999999488 | bytes 1 | tf_op jit(solution)/shard_map/pallas_call | solution.py:32
  8.6 3.6 %shard_map.96.refs_1_.refs_0_ = bf16[768,512]{1,0:T(8,128)(2,1)S(1)} custom-call(s32[17]{0:T(128)S(1)} %pad_add_fusion.place_ref, bf16[768,1024]{1,0:T(8,128)(2,1)S(1)} %copy-done.4, bf16[768,1024]{1,0:T(8,128)(2,1)S(1)} %collective-permute-done.refs_1_, bf16[1024,8192]{1,0:T(8,128)(2,1)} %refs_5_.5, ...), custom_call_target="tpu_custom_call" | custom-call | flops 24999999488 | bytes 1 | tf_op jit(solution)/shard_map/pallas_call | solution.py:32
  12.2 4.9 %collective-permute-start.2 = (bf16[768,512]{1,0:T(8,128)(2,1)S(1)}, bf16[768,512]{1,0:T(8,128)(2,1)S(1)}, u32[]{:S(2)}, u32[]{:S(2)}) collective-permute-start(bf16[768,512]{1,0:T(8,128)(2,1)S(1)} %shard_map.96.refs_1_.refs_0_), channel_id=1, source_target_pairs={{0,2},{1,3},{6,4},{7,5},{8,10},{9,11},{14,12},{15,13},{16,18},{17,... | collective-permute-start | bytes 2359304 | tf_op jit(solution)/shard_map/ppermute | solution.py:168
  19.6 8.3 %shard_map.98 = (bf16[768,512]{1,0:T(8,128)(2,1)S(1)}, bf16[768,512]{1,0:T(8,128)(2,1)S(1)}, bf16[768,512]{1,0:T(8,128)(2,1)S(1)}) custom-call(s32[17]{0:T(128)S(1)} %pad_add_fusion.place_ref, bf16[768,1024]{1,0:T(8,128)(2,1)S(1)} %copy-done.4, bf16[768,1024]{1,0:T(8,128)(2,1)S(1)} %collective-permute-done.refs_1_, bf16[1024,8192]{1,0:T(8,128)(2,1)} %refs_5_.5, ...), custom_call_target="tpu_custom_call" | custom-call | flops 74999996416 | bytes 1 | tf_op jit(solution)/shard_map/pallas_call | solution.py:32
  38.6 3.2 %shard_map.101.refs_2_ = bf16[3,1024,512]{2,1,0:T(8,128)(2,1)S(1)} custom-call(s32[17]{0:T(128)S(1)} %pad_add_fusion.place_ref, bf16[1024,8192]{1,0:T(8,128)(2,1)} %refs_5_.5, bf16[768,512]{1,0:T(8,128)(2,1)S(1)} %shard_map.100.refs_1_), custom_call_target="tpu_custom_call" | custom-call | flops 44999999488 | bytes 1 | tf_op jit(solution)/shard_map/pallas_call | solution.py:32
  42.7 18.3 %collective-permute-start.9 = (bf16[768,512]{1,0:T(8,128)(2,1)S(1)}, bf16[768,512]{1,0:T(8,128)(2,1)S(1)}, u32[]{:S(2)}, u32[]{:S(2)}) collective-permute-start(bf16[768,512]{1,0:T(8,128)(2,1)S(1)} %shard_map.102.refs_2_), channel_id=1, source_target_pairs={{0,2},{1,3},{4,6},{5,7},{2,0},{3,1},{6,4},{7,5},{8,10},{9,11},{12,... | collective-permute-start | bytes 2359304 | tf_op jit(solution)/shard_map/ppermute | solution.py:168
  62.4 3.6 %shard_map.104.refs_4_.refs_0_ = bf16[768,512]{1,0:T(8,128)(2,1)S(1)} custom-call(s32[17]{0:T(128)S(1)} %pad_add_fusion.place_ref, bf16[768,1024]{1,0:T(8,128)(2,1)S(1)} %copy-done.4, bf16[768,1024]{1,0:T(8,128)(2,1)S(1)} %collective-permute-done.refs_1_, bf16[1024,8192]{1,0:T(8,128)(2,1)} %refs_5_.5, ...), custom_call_target="tpu_custom_call" | custom-call | flops 24999999488 | bytes 1 | tf_op jit(solution)/shard_map/pallas_call | solution.py:32
  66.0 4.8 %collective-permute-start.8 = (bf16[768,512]{1,0:T(8,128)(2,1)S(1)}, bf16[768,512]{1,0:T(8,128)(2,1)S(1)}, u32[]{:S(2)}, u32[]{:S(2)}) collective-permute-start(bf16[768,512]{1,0:T(8,128)(2,1)S(1)} %shard_map.104.refs_4_.refs_0_), channel_id=1, source_target_pairs={{0,2},{1,3},{6,4},{7,5},{8,10},{9,11},{14,12},{15,13},{16,18},{17,... | collective-permute-start | bytes 2359304 | tf_op jit(solution)/shard_map/ppermute | solution.py:168
  70.8 7.5 %shard_map.105 = (bf16[768,512]{1,0:T(8,128)(2,1)S(1)}, bf16[768,512]{1,0:T(8,128)(2,1)S(1)}, bf16[768,512]{1,0:T(8,128)(2,1)S(1)}) custom-call(s32[17]{0:T(128)S(1)} %pad_add_fusion.place_ref, bf16[768,1024]{1,0:T(8,128)(2,1)S(1)} %copy-done.4, bf16[768,1024]{1,0:T(8,128)(2,1)S(1)} %collective-permute-done.refs_1_, bf16[1024,8192]{1,0:T(8,128)(2,1)} %refs_5_.5, ...), custom_call_target="tpu_custom_call" | custom-call | flops 74999996416 | bytes 1 | tf_op jit(solution)/shard_map/pallas_call | solution.py:32
  86.9 4.3 %shard_map.106 = (bf16[768,512]{1,0:T(8,128)(2,1)S(1)}, bf16[2,384,512]{2,1,0:T(8,128)(2,1)S(1)}, bf16[2,384,512]{2,1,0:T(8,128)(2,1)S(1)}, bf16[384,512]{1,0:T(8,128)(2,1)S(1)}, bf16[384,512]{1,0:T(8,128)(2,1)S(1)}) custom-call(s32[17]{0:T(128)S(1)} %pad_add_fusion.place_ref, bf16[768,512]{1,0:T(8,128)(2,1)S(1)} %copy-done.40, ...), custom_call_target="tpu_custom_call" | custom-call | flops 49999998976 | bytes 1 | tf_op jit(solution)/shard_map/pallas_call | solution.py:32
  97.3 10.5 %collective-permute-done.12.refs_1_ = bf16[2,384,512]{2,1,0:T(8,128)(2,1)S(1)} collective-permute-done((bf16[2,384,512]{2,1,0:T(8,128)(2,1)S(1)}, bf16[2,384,512]{2,1,0:T(8,128)(2,1)S(1)}, u32[]{:S(2)}, u32[]{:S(2)}) %collective-permute-start.12) | collective-permute-done | bytes 786464 | tf_op jit(solution)/shard_map/ppermute | solution.py:171
  113.5 4.5 %collective-permute-done.18.refs_4_ = bf16[384,512]{1,0:T(8,128)(2,1)S(1)} collective-permute-done((bf16[384,512]{1,0:T(8,128)(2,1)S(1)}, bf16[384,512]{1,0:T(8,128)(2,1)S(1)}, u32[]{:S(2)}, u32[]{:S(2)}) %collective-permute-start.18) | collective-permute-done | bytes 393248 | tf_op jit(solution)/shard_map/ppermute | solution.py:171
  118.3 3.8 %shard_map.111 = (bf16[384,512]{1,0:T(8,128)(2,1)S(1)}, bf16[384,512]{1,0:T(8,128)(2,1)S(1)}, f32[768,1024]{1,0:T(8,128)}, f32[768,1024]{1,0:T(8,128)}) custom-call(s32[17]{0:T(128)S(1)} %pad_add_fusion.place_ref, bf16[768,512]{1,0:T(8,128)(2,1)S(1)} %get-tuple-element.41.refs_2_.refs_0_, bf16[2,384,512]{2,1,0:T(8,128)(2,1)S(1)} %collective-permute-done.12.refs_1_, ...), custom_call_target="tpu_custom_call" | custom-call | flops 49999998976 | bytes 1 | tf_op jit(solution)/shard_map/pallas_call | solution.py:32
  126.3 4.1 %collective-permute-done.19.refs_1_.refs_4_ = bf16[384,512]{1,0:T(8,128)(2,1)S(1)} collective-permute-done((bf16[384,512]{1,0:T(8,128)(2,1)S(1)}, bf16[384,512]{1,0:T(8,128)(2,1)S(1)}, u32[]{:S(2)}, u32[]{:S(2)}) %collective-permute-start.19) | collective-permute-done | bytes 393248 | tf_op jit(solution)/shard_map/ppermute | solution.py:171
  130.4 2.8 collective-permute-done.20.refs_3_
  144.9 4.3 %shard_map.113 = (bf16[768,512]{1,0:T(8,128)(2,1)S(1)}, bf16[2,384,512]{2,1,0:T(8,128)(2,1)S(1)}, bf16[2,384,512]{2,1,0:T(8,128)(2,1)S(1)}, bf16[384,512]{1,0:T(8,128)(2,1)S(1)}, bf16[384,512]{1,0:T(8,128)(2,1)S(1)}) custom-call(s32[17]{0:T(128)S(1)} %pad_add_fusion.place_ref, bf16[768,512]{1,0:T(8,128)(2,1)S(1)} %copy-done.38, ...), custom_call_target="tpu_custom_call" | custom-call | flops 49999998976 | bytes 1 | tf_op jit(solution)/shard_map/pallas_call | solution.py:32
  154.5 5.0 %shard_map.114.refs_4_.refs_0_ = bf16[768,512]{1,0:T(8,128)(2,1)S(1)} custom-call(s32[17]{0:T(128)S(1)} %pad_add_fusion.place_ref, bf16[384,512]{1,0:T(8,128)(2,1)S(1)} %get-tuple-element.48.refs_0_.refs_4_, bf16[384,512]{1,0:T(8,128)(2,1)S(1)} %copy-done.22, bf16[2,384,512]{2,1,0:T(8,128)(2,1)} %collective-permute-done.23.refs_2_, ...), custom_call_target="tpu_custom_call" | custom-call | flops 49999998976 | bytes 1 | tf_op jit(solution)/shard_map/pallas_call | solution.py:32
  159.5 6.6 %collective-permute-done.21.refs_1_ = bf16[2,384,512]{2,1,0:T(8,128)(2,1)S(1)} collective-permute-done((bf16[2,384,512]{2,1,0:T(8,128)(2,1)S(1)}, bf16[2,384,512]{2,1,0:T(8,128)(2,1)S(1)}, u32[]{:S(2)}, u32[]{:S(2)}) %collective-permute-start.21) | collective-permute-done | bytes 786464 | tf_op jit(solution)/shard_map/ppermute | solution.py:171
  170.4 3.8 %collective-permute-start.29 = (bf16[768,512]{1,0:T(8,128)(2,1)S(1)}, bf16[768,512]{1,0:T(8,128)(2,1)S(1)}, u32[]{:S(2)}, u32[]{:S(2)}) collective-permute-start(bf16[768,512]{1,0:T(8,128)(2,1)S(1)} %shard_map.114.refs_4_.refs_0_), channel_id=1, source_target_pairs={{0,2},{1,3},{4,6},{5,7},{2,0},{3,1},{6,4},{7,5},{8,10},{9,11},{12,... | collective-permute-start | bytes 2359304 | tf_op jit(solution)/shard_map/ppermute | solution.py:168
  176.4 3.8 %shard_map.116 = (bf16[384,512]{1,0:T(8,128)(2,1)S(1)}, bf16[384,512]{1,0:T(8,128)(2,1)S(1)}, f32[768,1024]{1,0:T(8,128)}, f32[768,1024]{1,0:T(8,128)}) custom-call(s32[17]{0:T(128)S(1)} %pad_add_fusion.place_ref, bf16[768,512]{1,0:T(8,128)(2,1)S(1)} %copy-done.36, ...), custom_call_target="tpu_custom_call", output_to_operand_aliasing={{2}: (8, {}), {3}: (9, {})} | custom-call | flops 49999998976 | bytes 1 | tf_op jit(solution)/shard_map/pallas_call | solution.py:32
  183.2 5.5 %collective-permute-done.29.refs_0_ = bf16[768,512]{1,0:T(8,128)(2,1)S(1)} collective-permute-done((bf16[768,512]{1,0:T(8,128)(2,1)S(1)}, bf16[768,512]{1,0:T(8,128)(2,1)S(1)}, u32[]{:S(2)}, u32[]{:S(2)}) %collective-permute-start.29) | collective-permute-done | bytes 786464 | tf_op jit(solution)/shard_map/ppermute | solution.py:168
  195.5 6.5 %collective-permute-done.34.refs_1_.refs_7_.refs_5_ = bf16[768,512]{1,0:T(8,128)(2,1)S(1)} collective-permute-done((bf16[768,512]{1,0:T(8,128)(2,1)S(1)}, bf16[768,512]{1,0:T(8,128)(2,1)S(1)}, u32[]{:S(2)}, u32[]{:S(2)}) %collective-permute-start.34) | collective-permute-done | bytes 786464 | tf_op jit(solution)/shard_map/ppermute | solution.py:168
  205.5 3.9 %shard_map.121.refs_14_.refs_0_ = bf16[768,512]{1,0:T(8,128)(2,1)S(1)} custom-call(s32[17]{0:T(128)S(1)} %pad_add_fusion.place_ref, bf16[384,512]{1,0:T(8,128)(2,1)S(1)} %get-tuple-element.63.refs_1_.refs_0_, bf16[384,512]{1,0:T(8,128)(2,1)S(1)} %get-tuple-element.64.refs_2_.refs_1_, bf16[2,384,512]{2,1,0:T(8,128)(2,1)S(1)} %collective-permute-done.31.refs_2_, ...), custom_call_target="tpu_custom_call" | custom-call | flops 49999998976 | bytes 1 | tf_op jit(solution)/shard_map/pallas_call | solution.py:32
  210.1 7.5 %collective-permute-start.35 = (bf16[768,512]{1,0:T(8,128)(2,1)S(1)}, bf16[768,512]{1,0:T(8,128)(2,1)S(1)}, u32[]{:S(2)}, u32[]{:S(2)}) collective-permute-start(bf16[768,512]{1,0:T(8,128)(2,1)S(1)} %shard_map.121.refs_14_.refs_0_), channel_id=1, source_target_pairs={{0,2},{1,3},{4,6},{5,7},{2,0},{3,1},{6,4},{7,5},{8,10},{9,11},{12,... | collective-permute-start | bytes 2359304 | tf_op jit(solution)/shard_map/ppermute | solution.py:168
  217.6 7.7 %collective-permute-done.37.refs_11_.refs_8_ = bf16[768,512]{1,0:T(8,128)(2,1)S(1)} collective-permute-done((bf16[768,512]{1,0:T(8,128)(2,1)S(1)}, bf16[768,512]{1,0:T(8,128)(2,1)S(1)}, u32[]{:S(2)}, u32[]{:S(2)}) %collective-permute-start.37) | collective-permute-done | bytes 786464 | tf_op jit(solution)/shard_map/ppermute | solution.py:168
  225.3 5.6 %shard_map.122.refs_1_ = bf16[768,1024]{1,0:T(8,128)(2,1)} custom-call(s32[17]{0:T(128)S(1)} %pad_add_fusion.place_ref, bf16[768,512]{1,0:T(8,128)(2,1)S(1)} %shard_map.114.refs_4_.refs_0_, bf16[1,1024,512]{2,1,0:T(8,128)(2,1)S(1)} %copy-done.6, bf16[3,1024,512]{2,1,0:T(8,128)(2,1)S(1)} %copy-done.3, bf16[768,512]{1,0:T(8,128)(2,1)S(1)} %copy-done.8, ...), custom_call_target="tpu_custom_call" | custom-call | flops 80000000000 | bytes 1 | tf_op jit(solution)/shard_map/pallas_call | solution.py:32
  232.8 9.4 %collective-permute-done.35.refs_0_ = bf16[768,512]{1,0:T(8,128)(2,1)S(1)} collective-permute-done((bf16[768,512]{1,0:T(8,128)(2,1)S(1)}, bf16[768,512]{1,0:T(8,128)(2,1)S(1)}, u32[]{:S(2)}, u32[]{:S(2)}) %collective-permute-start.35) | collective-permute-done | bytes 786464 | tf_op jit(solution)/shard_map/ppermute | solution.py:168
  244.7 7.4 %collective-permute-done.39.refs_1_.refs_5_ = bf16[768,512]{1,0:T(8,128)(2,1)S(1)} collective-permute-done((bf16[768,512]{1,0:T(8,128)(2,1)S(1)}, bf16[768,512]{1,0:T(8,128)(2,1)S(1)}, u32[]{:S(2)}, u32[]{:S(2)}) %collective-permute-start.39) | collective-permute-done | bytes 786464 | tf_op jit(solution)/shard_map/ppermute | solution.py:168
  255.5 8.1 %shard_map.126.refs_10_.refs_11_ = f32[768,1024]{1,0:T(8,128)S(1)} custom-call(s32[17]{0:T(128)S(1)} %pad_add_fusion.place_ref, bf16[768,512]{1,0:T(8,128)(2,1)S(1)} %shard_map.121.refs_14_.refs_0_, bf16[1024,8192]{1,0:T(8,128)(2,1)} %refs_5_.5, bf16[768,512]{1,0:T(8,128)(2,1)S(1)} %shard_map.124.refs_2_, bf16[1024,8192]{1,0:T(8,128)(2,1)} %refs_5_.5, ...), custom_call_target="tpu_custom_call" | custom-call | flops 80000000000 | bytes 1 | tf_op jit(solution)/shard_map/pallas_call | solution.py:32
  263.6 6.4 %shard_map.127.refs_1_.refs_7_ = f32[768,1024]{1,0:T(8,128)S(1)} custom-call(s32[17]{0:T(128)S(1)} %pad_add_fusion.place_ref, bf16[768,512]{1,0:T(8,128)(2,1)S(1)} %shard_map.114.refs_4_.refs_0_, bf16[1024,8192]{1,0:T(8,128)(2,1)} %refs_5_.5, bf16[768,512]{1,0:T(8,128)(2,1)S(1)} %copy-done.8, bf16[1024,8192]{1,0:T(8,128)(2,1)} %refs_5_.5, ...), custom_call_target="tpu_custom_call" | custom-call | flops 80000000000 | bytes 1 | tf_op jit(solution)/shard_map/pallas_call | solution.py:32
  270.0 6.5 %collective-permute-done.44.refs_0_ = bf16[768,512]{1,0:T(8,128)(2,1)} collective-permute-done((bf16[768,512]{1,0:T(8,128)(2,1)}, bf16[768,512]{1,0:T(8,128)(2,1)}, u32[]{:S(2)}, u32[]{:S(2)}) %collective-permute-start.44) | collective-permute-done | bytes 786464 | tf_op jit(solution)/shard_map/ppermute | solution.py:168
  281.4 6.6 %shard_map.130 = f32[768,1024]{1,0:T(8,128)} custom-call(s32[17]{0:T(128)S(1)} %pad_add_fusion.place_ref, bf16[768,512]{1,0:T(8,128)(2,1)} %shard_map.128.refs_1_.refs_0_, bf16[768,512]{1,0:T(8,128)(2,1)} %shard_map.129.refs_1_.refs_8_, bf16[1024,8192]{1,0:T(8,128)(2,1)} %refs_5_.5, bf16[768,512]{1,0:T(8,128)(2,1)S(1)} %collective-permute-done.45.refs_3_, ...), custom_call_target="tpu_custom_call" | custom-call | flops 80000000000 | bytes 1 | tf_op jit(solution)/shard_map/pallas_call | solution.py:32
  (191 shorter events, 94.7 us)
Async XLA Ops:
  7.4 12.1 %collective-permute-start.3 = (bf16[3,1024,512]{2,1,0:T(8,128)(2,1)S(1)}, bf16[3,1024,512]{2,1,0:T(8,128)(2,1)S(1)}, u32[]{:S(2)}, u32[]{:S(2)}) collective-permute-start(bf16[3,1024,512]{2,1,0:T(8,128)(2,1)S(1)} %shard_map.95.refs_4_), channel_id=1, source_target_pairs={{0,1},{1,0},{2,3},{3,2},{4,5},{5,4},{6,7},{7,6},{8,9},{9,8},{10,11... | collective-permute-start | bytes 9437192 | tf_op jit(solution)/shard_map/ppermute | solution.py:165
  12.2 22.7 %collective-permute-start.2 = (bf16[768,512]{1,0:T(8,128)(2,1)S(1)}, bf16[768,512]{1,0:T(8,128)(2,1)S(1)}, u32[]{:S(2)}, u32[]{:S(2)}) collective-permute-start(bf16[768,512]{1,0:T(8,128)(2,1)S(1)} %shard_map.96.refs_1_.refs_0_), channel_id=1, source_target_pairs={{0,2},{1,3},{6,4},{7,5},{8,10},{9,11},{14,12},{15,13},{16,18},{17,... | collective-permute-start | bytes 2359304 | tf_op jit(solution)/shard_map/ppermute | solution.py:168
  28.8 32.2 %collective-permute-start.6 = (bf16[768,512]{1,0:T(8,128)(2,1)S(1)}, bf16[768,512]{1,0:T(8,128)(2,1)S(1)}, u32[]{:S(2)}, u32[]{:S(2)}) collective-permute-start(bf16[768,512]{1,0:T(8,128)(2,1)S(1)} %get-tuple-element.35.refs_1_.refs_0_), channel_id=1, source_target_pairs={{0,2},{1,3},{6,4},{7,5},{8,10},{9,11},{14,12},{15,13},{16,18},{17,... | collective-permute-start | bytes 2359304 | tf_op jit(solution)/shard_map/ppermute | solution.py:168
  32.1 30.3 %collective-permute-start.5 = (bf16[1,1024,512]{2,1,0:T(8,128)(2,1)S(1)}, bf16[1,1024,512]{2,1,0:T(8,128)(2,1)S(1)}, u32[]{:S(2)}, u32[]{:S(2)}) collective-permute-start(bf16[1,1024,512]{2,1,0:T(8,128)(2,1)S(1)} %shard_map.99.refs_2_), channel_id=1, source_target_pairs={{0,1},{1,0},{2,3},{3,2},{4,5},{5,4},{6,7},{7,6},{8,9},{9,8},{10,11... | collective-permute-start | bytes 3145736 | tf_op jit(solution)/shard_map/ppermute | solution.py:165
  41.8 28.9 %collective-permute-start.4 = (bf16[3,1024,512]{2,1,0:T(8,128)(2,1)S(1)}, bf16[3,1024,512]{2,1,0:T(8,128)(2,1)S(1)}, u32[]{:S(2)}, u32[]{:S(2)}) collective-permute-start(bf16[3,1024,512]{2,1,0:T(8,128)(2,1)S(1)} %shard_map.101.refs_2_), channel_id=1, source_target_pairs={{0,1},{1,0},{2,3},{3,2},{4,5},{5,4},{6,7},{7,6},{8,9},{9,8},{10,11... | collective-permute-start | bytes 9437192 | tf_op jit(solution)/shard_map/ppermute | solution.py:165
  42.7 39.6 %collective-permute-start.9 = (bf16[768,512]{1,0:T(8,128)(2,1)S(1)}, bf16[768,512]{1,0:T(8,128)(2,1)S(1)}, u32[]{:S(2)}, u32[]{:S(2)}) collective-permute-start(bf16[768,512]{1,0:T(8,128)(2,1)S(1)} %shard_map.102.refs_2_), channel_id=1, source_target_pairs={{0,2},{1,3},{4,6},{5,7},{2,0},{3,1},{6,4},{7,5},{8,10},{9,11},{12,... | collective-permute-start | bytes 2359304 | tf_op jit(solution)/shard_map/ppermute | solution.py:168
  61.7 19.7 %collective-permute-start.10 = (bf16[768,512]{1,0:T(8,128)(2,1)S(1)}, bf16[768,512]{1,0:T(8,128)(2,1)S(1)}, u32[]{:S(2)}, u32[]{:S(2)}) collective-permute-start(bf16[768,512]{1,0:T(8,128)(2,1)S(1)} %shard_map.103.refs_4_), channel_id=1, source_target_pairs={{2,4},{3,5},{4,2},{5,3},{10,12},{11,13},{12,10},{13,11},{18,20},{1... | collective-permute-start | bytes 2359304 | tf_op jit(solution)/shard_map/ppermute | solution.py:168
  66.0 29.8 %collective-permute-start.8 = (bf16[768,512]{1,0:T(8,128)(2,1)S(1)}, bf16[768,512]{1,0:T(8,128)(2,1)S(1)}, u32[]{:S(2)}, u32[]{:S(2)}) collective-permute-start(bf16[768,512]{1,0:T(8,128)(2,1)S(1)} %shard_map.104.refs_4_.refs_0_), channel_id=1, source_target_pairs={{0,2},{1,3},{6,4},{7,5},{8,10},{9,11},{14,12},{15,13},{16,18},{17,... | collective-permute-start | bytes 2359304 | tf_op jit(solution)/shard_map/ppermute | solution.py:168
  80.1 32.7 %collective-permute-start.15 = (bf16[768,512]{1,0:T(8,128)(2,1)S(1)}, bf16[768,512]{1,0:T(8,128)(2,1)S(1)}, u32[]{:S(2)}, u32[]{:S(2)}) collective-permute-start(bf16[768,512]{1,0:T(8,128)(2,1)S(1)} %get-tuple-element.40.refs_4_.refs_0_), channel_id=1, source_target_pairs={{0,2},{1,3},{6,4},{7,5},{8,10},{9,11},{14,12},{15,13},{16,18},{17,... | collective-permute-start | bytes 2359304 | tf_op jit(solution)/shard_map/ppermute | solution.py:168
  91.2 16.5 %collective-permute-start.12 = (bf16[2,384,512]{2,1,0:T(8,128)(2,1)S(1)}, bf16[2,384,512]{2,1,0:T(8,128)(2,1)S(1)}, u32[]{:S(2)}, u32[]{:S(2)}) collective-permute-start(bf16[2,384,512]{2,1,0:T(8,128)(2,1)S(1)} %get-tuple-element.43), channel_id=1, source_target_pairs={{0,8},{8,0},{16,24},{24,16},{1,9},{9,1},{17,25},{25,17},{2,10},{10... | collective-permute-start | bytes 2359304 | tf_op jit(solution)/shard_map/ppermute | solution.py:171
  92.8 16.6 %collective-permute-start.13 = (bf16[2,384,512]{2,1,0:T(8,128)(2,1)S(1)}, bf16[2,384,512]{2,1,0:T(8,128)(2,1)S(1)}, u32[]{:S(2)}, u32[]{:S(2)}) collective-permute-start(bf16[2,384,512]{2,1,0:T(8,128)(2,1)S(1)} %get-tuple-element.45), channel_id=1, source_target_pairs={{0,16},{8,24},{16,0},{24,8},{1,17},{9,25},{17,1},{25,9},{2,18},{10... | collective-permute-start | bytes 2359304 | tf_op jit(solution)/shard_map/ppermute | solution.py:171
  96.6 15.5 %collective-permute-start.11 = (bf16[768,512]{1,0:T(8,128)(2,1)S(1)}, bf16[768,512]{1,0:T(8,128)(2,1)S(1)}, u32[]{:S(2)}, u32[]{:S(2)}) collective-permute-start(bf16[768,512]{1,0:T(8,128)(2,1)S(1)} %shard_map.107.refs_4_), channel_id=1, source_target_pairs={{2,4},{3,5},{4,2},{5,3},{10,12},{11,13},{12,10},{13,11},{18,20},{1... | collective-permute-start | bytes 2359304 | tf_op jit(solution)/shard_map/ppermute | solution.py:168
  125.4 13.1 %collective-permute-start.14 = (bf16[768,512]{1,0:T(8,128)(2,1)S(1)}, bf16[768,512]{1,0:T(8,128)(2,1)S(1)}, u32[]{:S(2)}, u32[]{:S(2)}) collective-permute-start(bf16[768,512]{1,0:T(8,128)(2,1)S(1)} %shard_map.109.refs_2_), channel_id=1, source_target_pairs={{0,2},{1,3},{4,6},{5,7},{2,0},{3,1},{6,4},{7,5},{8,10},{9,11},{12,... | collective-permute-start | bytes 2359304 | tf_op jit(solution)/shard_map/ppermute | solution.py:168
  125.4 14.0 %collective-permute-start.16 = (bf16[768,512]{1,0:T(8,128)(2,1)S(1)}, bf16[768,512]{1,0:T(8,128)(2,1)S(1)}, u32[]{:S(2)}, u32[]{:S(2)}) collective-permute-start(bf16[768,512]{1,0:T(8,128)(2,1)S(1)} %shard_map.110.refs_7_), channel_id=1, source_target_pairs={{2,4},{3,5},{4,2},{5,3},{10,12},{11,13},{12,10},{13,11},{18,20},{1... | collective-permute-start | bytes 2359304 | tf_op jit(solution)/shard_map/ppermute | solution.py:168
  134.9 16.5 %collective-permute-start.24 = (bf16[2,384,512]{2,1,0:T(8,128)(2,1)}, bf16[2,384,512]{2,1,0:T(8,128)(2,1)S(1)}, u32[]{:S(2)}, u32[]{:S(2)}) collective-permute-start(bf16[2,384,512]{2,1,0:T(8,128)(2,1)} %get-tuple-element.56), channel_id=1, source_target_pairs={{0,16},{8,24},{16,0},{24,8},{1,17},{9,25},{17,1},{25,9},{2,18},{10... | collective-permute-start | bytes 2359304 | tf_op jit(solution)/shard_map/ppermute | solution.py:171
  135.0 16.4 %collective-permute-start.23 = (bf16[2,384,512]{2,1,0:T(8,128)(2,1)}, bf16[2,384,512]{2,1,0:T(8,128)(2,1)}, u32[]{:S(2)}, u32[]{:S(2)}) collective-permute-start(bf16[2,384,512]{2,1,0:T(8,128)(2,1)} %get-tuple-element.50.refs_4_), channel_id=1, source_target_pairs={{0,8},{8,0},{16,24},{24,16},{1,9},{9,1},{17,25},{25,17},{2,10},{10... | collective-permute-start | bytes 2359304 | tf_op jit(solution)/shard_map/ppermute | solution.py:171
  150.1 15.9 %collective-permute-start.21 = (bf16[2,384,512]{2,1,0:T(8,128)(2,1)S(1)}, bf16[2,384,512]{2,1,0:T(8,128)(2,1)S(1)}, u32[]{:S(2)}, u32[]{:S(2)}) collective-permute-start(bf16[2,384,512]{2,1,0:T(8,128)(2,1)S(1)} %get-tuple-element.52), channel_id=1, source_target_pairs={{0,8},{8,0},{16,24},{24,16},{1,9},{9,1},{17,25},{25,17},{2,10},{10... | collective-permute-start | bytes 2359304 | tf_op jit(solution)/shard_map/ppermute | solution.py:171
  150.9 15.2 %collective-permute-start.22 = (bf16[2,384,512]{2,1,0:T(8,128)(2,1)S(1)}, bf16[2,384,512]{2,1,0:T(8,128)(2,1)S(1)}, u32[]{:S(2)}, u32[]{:S(2)}) collective-permute-start(bf16[2,384,512]{2,1,0:T(8,128)(2,1)S(1)} %get-tuple-element.53), channel_id=1, source_target_pairs={{0,16},{8,24},{16,0},{24,8},{1,17},{9,25},{17,1},{25,9},{2,18},{10... | collective-permute-start | bytes 2359304 | tf_op jit(solution)/shard_map/ppermute | solution.py:171
  169.7 11.7 %collective-permute-start.30 = (bf16[768,512]{1,0:T(8,128)(2,1)S(1)}, bf16[768,512]{1,0:T(8,128)(2,1)S(1)}, u32[]{:S(2)}, u32[]{:S(2)}) collective-permute-start(bf16[768,512]{1,0:T(8,128)(2,1)S(1)} %shard_map.114.refs_4_.refs_0_), channel_id=1, source_target_pairs={{2,4},{3,5},{4,2},{5,3},{10,12},{11,13},{12,10},{13,11},{18,20},{1... | collective-permute-start | bytes 2359304 | tf_op jit(solution)/shard_map/ppermute | solution.py:168
  170.4 18.3 %collective-permute-start.29 = (bf16[768,512]{1,0:T(8,128)(2,1)S(1)}, bf16[768,512]{1,0:T(8,128)(2,1)S(1)}, u32[]{:S(2)}, u32[]{:S(2)}) collective-permute-start(bf16[768,512]{1,0:T(8,128)(2,1)S(1)} %shard_map.114.refs_4_.refs_0_), channel_id=1, source_target_pairs={{0,2},{1,3},{4,6},{5,7},{2,0},{3,1},{6,4},{7,5},{8,10},{9,11},{12,... | collective-permute-start | bytes 2359304 | tf_op jit(solution)/shard_map/ppermute | solution.py:168
  180.5 11.4 %collective-permute-start.27 = (bf16[384,512]{1,0:T(8,128)(2,1)S(1)}, bf16[384,512]{1,0:T(8,128)(2,1)S(1)}, u32[]{:S(2)}, u32[]{:S(2)}) collective-permute-start(bf16[384,512]{1,0:T(8,128)(2,1)S(1)} %get-tuple-element.63.refs_1_.refs_0_), channel_id=1, source_target_pairs={{0,16},{8,24},{16,0},{24,8},{1,17},{9,25},{17,1},{25,9},{2,18},{10... | collective-permute-start | bytes 1179656 | tf_op jit(solution)/shard_map/ppermute | solution.py:171
  181.9 20.1 %collective-permute-start.34 = (bf16[768,512]{1,0:T(8,128)(2,1)S(1)}, bf16[768,512]{1,0:T(8,128)(2,1)S(1)}, u32[]{:S(2)}, u32[]{:S(2)}) collective-permute-start(bf16[768,512]{1,0:T(8,128)(2,1)S(1)} %shard_map.117.refs_1_.refs_6_.refs_4_), channel_id=1, source_target_pairs={{4,6},{5,7},{2,0},{3,1},{12,14},{13,15},{10,8},{11,9},{20,22},{21,... | collective-permute-start | bytes 2359304 | tf_op jit(solution)/shard_map/ppermute | solution.py:168
  189.3 12.8 %collective-permute-start.33 = (bf16[768,512]{1,0:T(8,128)(2,1)S(1)}, bf16[768,512]{1,0:T(8,128)(2,1)S(1)}, u32[]{:S(2)}, u32[]{:S(2)}) collective-permute-start(bf16[768,512]{1,0:T(8,128)(2,1)S(1)} %shard_map.118.refs_4_.refs_3_.refs_2_), channel_id=1, source_target_pairs={{2,4},{3,5},{4,2},{5,3},{10,12},{11,13},{12,10},{13,11},{18,20},{1... | collective-permute-start | bytes 2359304 | tf_op jit(solution)/shard_map/ppermute | solution.py:168
  192.6 12.5 %collective-permute-start.32 = (bf16[2,384,512]{2,1,0:T(8,128)(2,1)S(1)}, bf16[2,384,512]{2,1,0:T(8,128)(2,1)S(1)}, u32[]{:S(2)}, u32[]{:S(2)}) collective-permute-start(bf16[2,384,512]{2,1,0:T(8,128)(2,1)S(1)} %get-tuple-element.66), channel_id=1, source_target_pairs={{0,16},{8,24},{16,0},{24,8},{1,17},{9,25},{17,1},{25,9},{2,18},{10... | collective-permute-start | bytes 2359304 | tf_op jit(solution)/shard_map/ppermute | solution.py:171
  192.9 12.6 %collective-permute-start.31 = (bf16[2,384,512]{2,1,0:T(8,128)(2,1)S(1)}, bf16[2,384,512]{2,1,0:T(8,128)(2,1)S(1)}, u32[]{:S(2)}, u32[]{:S(2)}) collective-permute-start(bf16[2,384,512]{2,1,0:T(8,128)(2,1)S(1)} %get-tuple-element.65.refs_2_), channel_id=1, source_target_pairs={{0,8},{8,0},{16,24},{24,16},{1,9},{9,1},{17,25},{25,17},{2,10},{10... | collective-permute-start | bytes 2359304 | tf_op jit(solution)/shard_map/ppermute | solution.py:171
  202.6 22.6 %collective-permute-start.37 = (bf16[768,512]{1,0:T(8,128)(2,1)S(1)}, bf16[768,512]{1,0:T(8,128)(2,1)S(1)}, u32[]{:S(2)}, u32[]{:S(2)}) collective-permute-start(bf16[768,512]{1,0:T(8,128)(2,1)S(1)} %shard_map.120.refs_10_.refs_7_), channel_id=1, source_target_pairs={{4,6},{5,7},{2,0},{3,1},{12,14},{13,15},{10,8},{11,9},{20,22},{21,... | collective-permute-start | bytes 2359304 | tf_op jit(solution)/shard_map/ppermute | solution.py:168
  209.4 21.5 %collective-permute-start.36 = (bf16[768,512]{1,0:T(8,128)(2,1)S(1)}, bf16[768,512]{1,0:T(8,128)(2,1)S(1)}, u32[]{:S(2)}, u32[]{:S(2)}) collective-permute-start(bf16[768,512]{1,0:T(8,128)(2,1)S(1)} %shard_map.121.refs_14_.refs_0_), channel_id=1, source_target_pairs={{2,4},{3,5},{4,2},{5,3},{10,12},{11,13},{12,10},{13,11},{18,20},{1... | collective-permute-start | bytes 2359304 | tf_op jit(solution)/shard_map/ppermute | solution.py:168
  210.1 32.0 %collective-permute-start.35 = (bf16[768,512]{1,0:T(8,128)(2,1)S(1)}, bf16[768,512]{1,0:T(8,128)(2,1)S(1)}, u32[]{:S(2)}, u32[]{:S(2)}) collective-permute-start(bf16[768,512]{1,0:T(8,128)(2,1)S(1)} %shard_map.121.refs_14_.refs_0_), channel_id=1, source_target_pairs={{0,2},{1,3},{4,6},{5,7},{2,0},{3,1},{6,4},{7,5},{8,10},{9,11},{12,... | collective-permute-start | bytes 2359304 | tf_op jit(solution)/shard_map/ppermute | solution.py:168
  231.5 20.7 %collective-permute-start.39 = (bf16[768,512]{1,0:T(8,128)(2,1)S(1)}, bf16[768,512]{1,0:T(8,128)(2,1)S(1)}, u32[]{:S(2)}, u32[]{:S(2)}) collective-permute-start(bf16[768,512]{1,0:T(8,128)(2,1)S(1)} %shard_map.123.refs_1_.refs_4_), channel_id=1, source_target_pairs={{4,6},{5,7},{2,0},{3,1},{12,14},{13,15},{10,8},{11,9},{20,22},{21,... | collective-permute-start | bytes 2359304 | tf_op jit(solution)/shard_map/ppermute | solution.py:168
  244.2 10.3 %collective-permute-start.42 = (bf16[768,512]{1,0:T(8,128)(2,1)S(1)}, bf16[768,512]{1,0:T(8,128)(2,1)S(1)}, u32[]{:S(2)}, u32[]{:S(2)}) collective-permute-start(bf16[768,512]{1,0:T(8,128)(2,1)S(1)} %shard_map.123.refs_1_.refs_4_), channel_id=1, source_target_pairs={{0,1},{1,0},{2,3},{3,2},{4,5},{5,4},{6,7},{7,6},{8,9},{9,8},{10,11... | collective-permute-start | bytes 2359304 | tf_op jit(solution)/shard_map/ppermute | solution.py:165
  252.1 26.1 %collective-permute-start.47 = (bf16[768,1024]{1,0:T(8,128)(2,1)}, bf16[768,1024]{1,0:T(8,128)(2,1)}, u32[]{:S(2)}, u32[]{:S(2)}) collective-permute-start(bf16[768,1024]{1,0:T(8,128)(2,1)} %shard_map.122.refs_1_), channel_id=1, source_target_pairs={{0,1},{1,0},{2,3},{3,2},{4,5},{5,4},{6,7},{7,6},{8,9},{9,8},{10,11... | collective-permute-start | bytes 4718600 | tf_op jit(solution)/shard_map/ppermute | solution.py:165
  253.2 23.4 %collective-permute-start.44 = (bf16[768,512]{1,0:T(8,128)(2,1)}, bf16[768,512]{1,0:T(8,128)(2,1)}, u32[]{:S(2)}, u32[]{:S(2)}) collective-permute-start(bf16[768,512]{1,0:T(8,128)(2,1)} %shard_map.125.refs_14_.refs_0_), channel_id=1, source_target_pairs={{4,6},{5,7},{2,0},{3,1},{12,14},{13,15},{10,8},{11,9},{20,22},{21,... | collective-permute-start | bytes 2359304 | tf_op jit(solution)/shard_map/ppermute | solution.py:168
  (59 other events, 372.6 us)

commit v3 on v2

--- a/solution.py
+++ b/solution.py
@@ -9,8 +9,8 @@
 from jax.sharding import PartitionSpec as P
 
 F32, BF16 = jnp.float32, jnp.bfloat16
-VMEM_BYTES = 40 * 2**20
-FLOPS_A_US = 10**10
+VMEM_BYTES = 38 * 2**20
+FLOPS_A_US = 6000000000
 ANY = pl.BlockSpec(memory_space=pl.ANY)
 
 

time: 289 us -> 283 us (0.979)
  local copies, waits for them, and re-layouts: 21.5 us -> 4.08 us
  waiting for transfers between devices: 88.8 us -> 105 us
  Pallas kernels: 100 us -> 96.5 us
    unnamed x86 -> x38, local copies, waits for them, and re-layouts: 20.8 us -> 3.38 us
    ppermute x20, waiting for transfers between devices: 48.5 us -> 62.9 us  [along(): lax.ppermute(x, 'col', [(2 * a + c, 2 * b + c) for a, b in pairs for c in...]
    pallas_call x37, Pallas kernels: 100 us -> 96.5 us  [call(): pl.pallas_call(wrapped, out_shape=outs, grid_spec=pltpu.PrefetchScalarGri...]
    ppermute x16, starting transfers between devices: 18.9 us -> 15.9 us  [to_partner(): return lax.ppermute(x, 'row', [(i, i ^ s) for i in range(row_size)])]
    ppermute x16, waiting for transfers between devices: 35.6 us -> 38.6 us  [to_partner(): return lax.ppermute(x, 'row', [(i, i ^ s) for i in range(row_size)])]
  transfers between devices with their start and end apart: 48 -> 48, of which waited for: 25 -> 26; matrix products, arithmetic and copies ran while one was open for 0% -> 0% of each run, Pallas kernels for 30% -> 30%
where the time goes in v3:
time: 283 us; the launch traced here: 282 us
  waiting for transfers between devices  105 us (37%)
  Pallas kernels  96.5 us (34%)
  starting transfers between devices  74.5 us (26%)
  local copies, waits for them, and re-layouts  4.08 us (1%)
    pallas_call x37, Pallas kernels, call(): pl.pallas_call(wrapped, out_shape=outs, grid_spec=pltpu.PrefetchScalarGri...  96.5 us
    ppermute x20, waiting for transfers between devices, along(): lax.ppermute(x, 'col', [(2 * a + c, 2 * b + c) for a, b in pairs for c in...  62.9 us
    ppermute x20, starting transfers between devices, along(): lax.ppermute(x, 'col', [(2 * a + c, 2 * b + c) for a, b in pairs for c in...  55.7 us
    ppermute x16, waiting for transfers between devices, to_partner(): return lax.ppermute(x, 'row', [(i, i ^ s) for i in range(row_size)])  38.6 us
    ppermute x16, starting transfers between devices, to_partner(): return lax.ppermute(x, 'row', [(i, i ^ s) for i in range(row_size)])  15.9 us
  transfers between devices with their start and end apart: 48, of which 26 were waited for; matrix products, arithmetic and copies ran while one was open for 0% of the time, Pallas kernels for 30%

profile of v3, /device:TPU:0, one launch (start us, length us, event | category | flops | bytes accessed | tf_op | source)
XLA Modules:
  0.0 281.7 jit_solution(11099507033705253546)
XLA Ops:
  8.6 3.6 %shard_map.96.refs_1_.refs_0_ = bf16[768,512]{1,0:T(8,128)(2,1)S(1)} custom-call(s32[17]{0:T(128)S(1)} %pad_add_fusion.place_ref, bf16[768,1024]{1,0:T(8,128)(2,1)S(1)} %copy-done.4, bf16[768,1024]{1,0:T(8,128)(2,1)S(1)} %collective-permute-done.refs_1_, bf16[1024,8192]{1,0:T(8,128)(2,1)} %refs_5_.5, ...), custom_call_target="tpu_custom_call" | custom-call | flops 15000000512 | bytes 1 | tf_op jit(solution)/shard_map/pallas_call | solution.py:32
  12.2 4.9 %collective-permute-start.2 = (bf16[768,512]{1,0:T(8,128)(2,1)S(1)}, bf16[768,512]{1,0:T(8,128)(2,1)S(1)}, u32[]{:S(2)}, u32[]{:S(2)}) collective-permute-start(bf16[768,512]{1,0:T(8,128)(2,1)S(1)} %shard_map.96.refs_1_.refs_0_), channel_id=1, source_target_pairs={{0,2},{1,3},{6,4},{7,5},{8,10},{9,11},{14,12},{15,13},{16,18},{17,... | collective-permute-start | bytes 2359304 | tf_op jit(solution)/shard_map/ppermute | solution.py:168
  19.5 8.3 %shard_map.98 = (bf16[768,512]{1,0:T(8,128)(2,1)S(1)}, bf16[768,512]{1,0:T(8,128)(2,1)S(1)}, bf16[768,512]{1,0:T(8,128)(2,1)S(1)}) custom-call(s32[17]{0:T(128)S(1)} %pad_add_fusion.place_ref, bf16[768,1024]{1,0:T(8,128)(2,1)S(1)} %copy-done.4, bf16[768,1024]{1,0:T(8,128)(2,1)S(1)} %collective-permute-done.refs_1_, bf16[1024,8192]{1,0:T(8,128)(2,1)} %refs_5_.5, ...), custom_call_target="tpu_custom_call" | custom-call | flops 44999999488 | bytes 1 | tf_op jit(solution)/shard_map/pallas_call | solution.py:32
  31.1 3.8 %collective-permute-done.2.refs_1_ = bf16[768,512]{1,0:T(8,128)(2,1)S(1)} collective-permute-done((bf16[768,512]{1,0:T(8,128)(2,1)S(1)}, bf16[768,512]{1,0:T(8,128)(2,1)S(1)}, u32[]{:S(2)}, u32[]{:S(2)}) %collective-permute-start.2) | collective-permute-done | bytes 786464 | tf_op jit(solution)/shard_map/ppermute | solution.py:168
  40.5 18.3 %collective-permute-start.9 = (bf16[768,512]{1,0:T(8,128)(2,1)S(1)}, bf16[768,512]{1,0:T(8,128)(2,1)S(1)}, u32[]{:S(2)}, u32[]{:S(2)}) collective-permute-start(bf16[768,512]{1,0:T(8,128)(2,1)S(1)} %shard_map.102.refs_2_), channel_id=1, source_target_pairs={{0,2},{1,3},{4,6},{5,7},{2,0},{3,1},{6,4},{7,5},{8,10},{9,11},{12,... | collective-permute-start | bytes 2359304 | tf_op jit(solution)/shard_map/ppermute | solution.py:168
  60.2 3.6 %shard_map.104.refs_4_.refs_0_ = bf16[768,512]{1,0:T(8,128)(2,1)S(1)} custom-call(s32[17]{0:T(128)S(1)} %pad_add_fusion.place_ref, bf16[768,1024]{1,0:T(8,128)(2,1)S(1)} %copy-done.4, bf16[768,1024]{1,0:T(8,128)(2,1)S(1)} %collective-permute-done.refs_1_, bf16[1024,8192]{1,0:T(8,128)(2,1)} %refs_5_.5, ...), custom_call_target="tpu_custom_call" | custom-call | flops 15000000512 | bytes 1 | tf_op jit(solution)/shard_map/pallas_call | solution.py:32
  63.8 4.9 %collective-permute-start.8 = (bf16[768,512]{1,0:T(8,128)(2,1)S(1)}, bf16[768,512]{1,0:T(8,128)(2,1)S(1)}, u32[]{:S(2)}, u32[]{:S(2)}) collective-permute-start(bf16[768,512]{1,0:T(8,128)(2,1)S(1)} %shard_map.104.refs_4_.refs_0_), channel_id=1, source_target_pairs={{0,2},{1,3},{6,4},{7,5},{8,10},{9,11},{14,12},{15,13},{16,18},{17,... | collective-permute-start | bytes 2359304 | tf_op jit(solution)/shard_map/ppermute | solution.py:168
  68.7 7.5 %shard_map.105 = (bf16[768,512]{1,0:T(8,128)(2,1)S(1)}, bf16[768,512]{1,0:T(8,128)(2,1)S(1)}, bf16[768,512]{1,0:T(8,128)(2,1)S(1)}) custom-call(s32[17]{0:T(128)S(1)} %pad_add_fusion.place_ref, bf16[768,1024]{1,0:T(8,128)(2,1)S(1)} %copy-done.4, bf16[768,1024]{1,0:T(8,128)(2,1)S(1)} %collective-permute-done.refs_1_, bf16[1024,8192]{1,0:T(8,128)(2,1)} %refs_5_.5, ...), custom_call_target="tpu_custom_call" | custom-call | flops 44999999488 | bytes 1 | tf_op jit(solution)/shard_map/pallas_call | solution.py:32
  79.4 4.4 %shard_map.106 = (bf16[768,512]{1,0:T(8,128)(2,1)S(1)}, bf16[2,384,512]{2,1,0:T(8,128)(2,1)S(1)}, bf16[2,384,512]{2,1,0:T(8,128)(2,1)S(1)}, bf16[384,512]{1,0:T(8,128)(2,1)S(1)}, bf16[384,512]{1,0:T(8,128)(2,1)S(1)}) custom-call(s32[17]{0:T(128)S(1)} %pad_add_fusion.place_ref, bf16[768,512]{1,0:T(8,128)(2,1)S(1)} %copy-done.14, ...), custom_call_target="tpu_custom_call" | custom-call | flops 30000001024 | bytes 1 | tf_op jit(solution)/shard_map/pallas_call | solution.py:32
  86.9 3.3 %collective-permute-done.8.refs_1_ = bf16[768,512]{1,0:T(8,128)(2,1)S(1)} collective-permute-done((bf16[768,512]{1,0:T(8,128)(2,1)S(1)}, bf16[768,512]{1,0:T(8,128)(2,1)S(1)}, u32[]{:S(2)}, u32[]{:S(2)}) %collective-permute-start.8) | collective-permute-done | bytes 786464 | tf_op jit(solution)/shard_map/ppermute | solution.py:168
  91.6 7.2 %collective-permute-start.15 = (bf16[768,512]{1,0:T(8,128)(2,1)S(1)}, bf16[768,512]{1,0:T(8,128)(2,1)S(1)}, u32[]{:S(2)}, u32[]{:S(2)}) collective-permute-start(bf16[768,512]{1,0:T(8,128)(2,1)S(1)} %get-tuple-element.40.refs_4_.refs_0_), channel_id=1, source_target_pairs={{0,2},{1,3},{6,4},{7,5},{8,10},{9,11},{14,12},{15,13},{16,18},{17,... | collective-permute-start | bytes 2359304 | tf_op jit(solution)/shard_map/ppermute | solution.py:168
  105.3 6.8 %collective-permute-done.15.refs_1_ = bf16[768,512]{1,0:T(8,128)(2,1)S(1)} collective-permute-done((bf16[768,512]{1,0:T(8,128)(2,1)S(1)}, bf16[768,512]{1,0:T(8,128)(2,1)S(1)}, u32[]{:S(2)}, u32[]{:S(2)}) %collective-permute-start.15) | collective-permute-done | bytes 786464 | tf_op jit(solution)/shard_map/ppermute | solution.py:168
  112.9 3.8 %shard_map.111 = (bf16[384,512]{1,0:T(8,128)(2,1)S(1)}, bf16[384,512]{1,0:T(8,128)(2,1)S(1)}, f32[768,1024]{1,0:T(8,128)}, f32[768,1024]{1,0:T(8,128)}) custom-call(s32[17]{0:T(128)S(1)} %pad_add_fusion.place_ref, bf16[768,512]{1,0:T(8,128)(2,1)S(1)} %get-tuple-element.41.refs_2_.refs_0_, bf16[2,384,512]{2,1,0:T(8,128)(2,1)S(1)} %collective-permute-done.12.refs_1_, ...), custom_call_target="tpu_custom_call" | custom-call | flops 30000001024 | bytes 1 | tf_op jit(solution)/shard_map/pallas_call | solution.py:32
  130.7 4.1 %collective-permute-done.14.refs_1_ = bf16[768,512]{1,0:T(8,128)(2,1)S(1)} collective-permute-done((bf16[768,512]{1,0:T(8,128)(2,1)S(1)}, bf16[768,512]{1,0:T(8,128)(2,1)S(1)}, u32[]{:S(2)}, u32[]{:S(2)}) %collective-permute-start.14) | collective-permute-done | bytes 786464 | tf_op jit(solution)/shard_map/ppermute | solution.py:168
  134.8 4.4 %shard_map.113 = (bf16[768,512]{1,0:T(8,128)(2,1)S(1)}, bf16[2,384,512]{2,1,0:T(8,128)(2,1)S(1)}, bf16[2,384,512]{2,1,0:T(8,128)(2,1)S(1)}, bf16[384,512]{1,0:T(8,128)(2,1)S(1)}, bf16[384,512]{1,0:T(8,128)(2,1)S(1)}) custom-call(s32[17]{0:T(128)S(1)} %pad_add_fusion.place_ref, bf16[768,512]{1,0:T(8,128)(2,1)S(1)} %copy-done.12, ...), custom_call_target="tpu_custom_call" | custom-call | flops 30000001024 | bytes 1 | tf_op jit(solution)/shard_map/pallas_call | solution.py:32
  140.3 5.9 %collective-permute-done.24.refs_5_ = bf16[2,384,512]{2,1,0:T(8,128)(2,1)S(1)} collective-permute-done((bf16[2,384,512]{2,1,0:T(8,128)(2,1)S(1)}, bf16[2,384,512]{2,1,0:T(8,128)(2,1)S(1)}, u32[]{:S(2)}, u32[]{:S(2)}) %collective-permute-start.24) | collective-permute-done | bytes 786464 | tf_op jit(solution)/shard_map/ppermute | solution.py:171
  149.4 3.9 %shard_map.114.refs_4_.refs_0_ = bf16[768,512]{1,0:T(8,128)(2,1)S(1)} custom-call(s32[17]{0:T(128)S(1)} %pad_add_fusion.place_ref, bf16[384,512]{1,0:T(8,128)(2,1)S(1)} %get-tuple-element.48.refs_0_.refs_4_, bf16[384,512]{1,0:T(8,128)(2,1)S(1)} %get-tuple-element.49.refs_2_.refs_1_, bf16[2,384,512]{2,1,0:T(8,128)(2,1)S(1)} %collective-permute-done.23.refs_2_, ...), custom_call_target="tpu_custom_call" | custom-call | flops 30000001024 | bytes 1 | tf_op jit(solution)/shard_map/pallas_call | solution.py:32
  153.4 9.1 %collective-permute-done.21.refs_1_ = bf16[2,384,512]{2,1,0:T(8,128)(2,1)S(1)} collective-permute-done((bf16[2,384,512]{2,1,0:T(8,128)(2,1)S(1)}, bf16[2,384,512]{2,1,0:T(8,128)(2,1)S(1)}, u32[]{:S(2)}, u32[]{:S(2)}) %collective-permute-start.21) | collective-permute-done | bytes 786464 | tf_op jit(solution)/shard_map/ppermute | solution.py:171
  166.0 3.4 %collective-permute-start.29 = (bf16[768,512]{1,0:T(8,128)(2,1)S(1)}, bf16[768,512]{1,0:T(8,128)(2,1)S(1)}, u32[]{:S(2)}, u32[]{:S(2)}) collective-permute-start(bf16[768,512]{1,0:T(8,128)(2,1)S(1)} %shard_map.114.refs_4_.refs_0_), channel_id=1, source_target_pairs={{0,2},{1,3},{4,6},{5,7},{2,0},{3,1},{6,4},{7,5},{8,10},{9,11},{12,... | collective-permute-start | bytes 2359304 | tf_op jit(solution)/shard_map/ppermute | solution.py:168
  173.8 3.8 %shard_map.116 = (bf16[384,512]{1,0:T(8,128)(2,1)S(1)}, bf16[384,512]{1,0:T(8,128)(2,1)S(1)}, f32[768,1024]{1,0:T(8,128)}, f32[768,1024]{1,0:T(8,128)}) custom-call(s32[17]{0:T(128)S(1)} %pad_add_fusion.place_ref, bf16[768,512]{1,0:T(8,128)(2,1)S(1)} %get-tuple-element.51.refs_10_.refs_0_, ...), custom_call_target="tpu_custom_call", output_to_operand_aliasing={{2}: (8, {}), {3}: (9, {})} | custom-call | flops 30000001024 | bytes 1 | tf_op jit(solution)/shard_map/pallas_call | solution.py:32
  180.5 5.1 %collective-permute-done.29.refs_0_ = bf16[768,512]{1,0:T(8,128)(2,1)S(1)} collective-permute-done((bf16[768,512]{1,0:T(8,128)(2,1)S(1)}, bf16[768,512]{1,0:T(8,128)(2,1)S(1)}, u32[]{:S(2)}, u32[]{:S(2)}) %collective-permute-start.29) | collective-permute-done | bytes 786464 | tf_op jit(solution)/shard_map/ppermute | solution.py:168
  192.9 4.2 %collective-permute-done.34.refs_1_.refs_7_.refs_5_ = bf16[768,512]{1,0:T(8,128)(2,1)S(1)} collective-permute-done((bf16[768,512]{1,0:T(8,128)(2,1)S(1)}, bf16[768,512]{1,0:T(8,128)(2,1)S(1)}, u32[]{:S(2)}, u32[]{:S(2)}) %collective-permute-start.34) | collective-permute-done | bytes 786464 | tf_op jit(solution)/shard_map/ppermute | solution.py:168
  199.2 3.7 %collective-permute-done.32.refs_5_ = bf16[2,384,512]{2,1,0:T(8,128)(2,1)S(1)} collective-permute-done((bf16[2,384,512]{2,1,0:T(8,128)(2,1)S(1)}, bf16[2,384,512]{2,1,0:T(8,128)(2,1)S(1)}, u32[]{:S(2)}, u32[]{:S(2)}) %collective-permute-start.32) | collective-permute-done | bytes 786464 | tf_op jit(solution)/shard_map/ppermute | solution.py:171
  203.4 3.9 %shard_map.121.refs_14_.refs_0_ = bf16[768,512]{1,0:T(8,128)(2,1)S(1)} custom-call(s32[17]{0:T(128)S(1)} %pad_add_fusion.place_ref, bf16[384,512]{1,0:T(8,128)(2,1)S(1)} %get-tuple-element.63.refs_1_.refs_0_, bf16[384,512]{1,0:T(8,128)(2,1)S(1)} %get-tuple-element.64.refs_2_.refs_1_, bf16[2,384,512]{2,1,0:T(8,128)(2,1)S(1)} %collective-permute-done.31.refs_2_, ...), custom_call_target="tpu_custom_call" | custom-call | flops 30000001024 | bytes 1 | tf_op jit(solution)/shard_map/pallas_call | solution.py:32
  209.9 10.5 %collective-permute-done.37.refs_11_.refs_8_ = bf16[768,512]{1,0:T(8,128)(2,1)S(1)} collective-permute-done((bf16[768,512]{1,0:T(8,128)(2,1)S(1)}, bf16[768,512]{1,0:T(8,128)(2,1)S(1)}, u32[]{:S(2)}, u32[]{:S(2)}) %collective-permute-start.37) | collective-permute-done | bytes 786464 | tf_op jit(solution)/shard_map/ppermute | solution.py:168
  220.4 4.9 %shard_map.122.refs_1_ = bf16[768,1024]{1,0:T(8,128)(2,1)S(1)} custom-call(s32[17]{0:T(128)S(1)} %pad_add_fusion.place_ref, bf16[768,512]{1,0:T(8,128)(2,1)S(1)} %shard_map.114.refs_4_.refs_0_, bf16[1,1024,512]{2,1,0:T(8,128)(2,1)S(1)} %copy-done.6, bf16[3,1024,512]{2,1,0:T(8,128)(2,1)S(1)} %copy-done.3, ...), custom_call_target="tpu_custom_call" | custom-call | flops 48000000000 | bytes 1 | tf_op jit(solution)/shard_map/pallas_call | solution.py:32
  227.2 10.0 %collective-permute-done.35.refs_0_ = bf16[768,512]{1,0:T(8,128)(2,1)S(1)} collective-permute-done((bf16[768,512]{1,0:T(8,128)(2,1)S(1)}, bf16[768,512]{1,0:T(8,128)(2,1)S(1)}, u32[]{:S(2)}, u32[]{:S(2)}) %collective-permute-start.35) | collective-permute-done | bytes 786464 | tf_op jit(solution)/shard_map/ppermute | solution.py:168
  239.2 8.5 %collective-permute-done.39.refs_1_.refs_5_ = bf16[768,512]{1,0:T(8,128)(2,1)S(1)} collective-permute-done((bf16[768,512]{1,0:T(8,128)(2,1)S(1)}, bf16[768,512]{1,0:T(8,128)(2,1)S(1)}, u32[]{:S(2)}, u32[]{:S(2)}) %collective-permute-start.39) | collective-permute-done | bytes 786464 | tf_op jit(solution)/shard_map/ppermute | solution.py:168
  250.1 8.1 %shard_map.126.refs_10_.refs_11_ = f32[768,1024]{1,0:T(8,128)S(1)} custom-call(s32[17]{0:T(128)S(1)} %pad_add_fusion.place_ref, bf16[768,512]{1,0:T(8,128)(2,1)S(1)} %shard_map.121.refs_14_.refs_0_, bf16[1024,8192]{1,0:T(8,128)(2,1)} %refs_5_.5, bf16[768,512]{1,0:T(8,128)(2,1)S(1)} %shard_map.124.refs_2_, bf16[1024,8192]{1,0:T(8,128)(2,1)} %refs_5_.5, ...), custom_call_target="tpu_custom_call" | custom-call | flops 48000000000 | bytes 1 | tf_op jit(solution)/shard_map/pallas_call | solution.py:32
  258.2 6.4 %shard_map.127.refs_1_.refs_7_ = f32[768,1024]{1,0:T(8,128)S(1)} custom-call(s32[17]{0:T(128)S(1)} %pad_add_fusion.place_ref, bf16[768,512]{1,0:T(8,128)(2,1)S(1)} %shard_map.114.refs_4_.refs_0_, bf16[1024,8192]{1,0:T(8,128)(2,1)} %refs_5_.5, bf16[768,512]{1,0:T(8,128)(2,1)S(1)} %shard_map.118.refs_4_.refs_3_.refs_2_, bf16[1024,8192]{1,0:T(8,128)(2,1)} %refs_5_.5, ...), custom_call_target="tpu_custom_call" | custom-call | flops 48000000000 | bytes 1 | tf_op jit(solution)/shard_map/pallas_call | solution.py:32
  264.7 6.6 %collective-permute-done.44.refs_0_ = bf16[768,512]{1,0:T(8,128)(2,1)S(1)} collective-permute-done((bf16[768,512]{1,0:T(8,128)(2,1)S(1)}, bf16[768,512]{1,0:T(8,128)(2,1)S(1)}, u32[]{:S(2)}, u32[]{:S(2)}) %collective-permute-start.44) | collective-permute-done | bytes 786464 | tf_op jit(solution)/shard_map/ppermute | solution.py:168
  275.8 5.8 %shard_map.130 = f32[768,1024]{1,0:T(8,128)} custom-call(s32[17]{0:T(128)S(1)} %pad_add_fusion.place_ref, bf16[768,512]{1,0:T(8,128)(2,1)S(1)} %shard_map.128.refs_1_.refs_0_, bf16[768,512]{1,0:T(8,128)(2,1)S(1)} %shard_map.129.refs_1_.refs_8_, bf16[1024,8192]{1,0:T(8,128)(2,1)} %refs_5_.5, bf16[768,512]{1,0:T(8,128)(2,1)S(1)} %collective-permute-done.45.refs_3_, ...), custom_call_target="tpu_custom_call" | custom-call | flops 48000000000 | bytes 1 | tf_op jit(solution)/shard_map/pallas_call | solution.py:32
  (144 shorter events, 87.6 us)
Async XLA Ops:
  7.4 12.1 %collective-permute-start.3 = (bf16[3,1024,512]{2,1,0:T(8,128)(2,1)S(1)}, bf16[3,1024,512]{2,1,0:T(8,128)(2,1)S(1)}, u32[]{:S(2)}, u32[]{:S(2)}) collective-permute-start(bf16[3,1024,512]{2,1,0:T(8,128)(2,1)S(1)} %shard_map.95.refs_4_), channel_id=1, source_target_pairs={{0,1},{1,0},{2,3},{3,2},{4,5},{5,4},{6,7},{7,6},{8,9},{9,8},{10,11... | collective-permute-start | bytes 9437192 | tf_op jit(solution)/shard_map/ppermute | solution.py:165
  12.2 22.7 %collective-permute-start.2 = (bf16[768,512]{1,0:T(8,128)(2,1)S(1)}, bf16[768,512]{1,0:T(8,128)(2,1)S(1)}, u32[]{:S(2)}, u32[]{:S(2)}) collective-permute-start(bf16[768,512]{1,0:T(8,128)(2,1)S(1)} %shard_map.96.refs_1_.refs_0_), channel_id=1, source_target_pairs={{0,2},{1,3},{6,4},{7,5},{8,10},{9,11},{14,12},{15,13},{16,18},{17,... | collective-permute-start | bytes 2359304 | tf_op jit(solution)/shard_map/ppermute | solution.py:168
  27.8 30.9 %collective-permute-start.6 = (bf16[768,512]{1,0:T(8,128)(2,1)S(1)}, bf16[768,512]{1,0:T(8,128)(2,1)S(1)}, u32[]{:S(2)}, u32[]{:S(2)}) collective-permute-start(bf16[768,512]{1,0:T(8,128)(2,1)S(1)} %get-tuple-element.35.refs_1_.refs_0_), channel_id=1, source_target_pairs={{0,2},{1,3},{6,4},{7,5},{8,10},{9,11},{14,12},{15,13},{16,18},{17,... | collective-permute-start | bytes 2359304 | tf_op jit(solution)/shard_map/ppermute | solution.py:168
  31.0 29.2 %collective-permute-start.5 = (bf16[1,1024,512]{2,1,0:T(8,128)(2,1)S(1)}, bf16[1,1024,512]{2,1,0:T(8,128)(2,1)S(1)}, u32[]{:S(2)}, u32[]{:S(2)}) collective-permute-start(bf16[1,1024,512]{2,1,0:T(8,128)(2,1)S(1)} %shard_map.99.refs_2_), channel_id=1, source_target_pairs={{0,1},{1,0},{2,3},{3,2},{4,5},{5,4},{6,7},{7,6},{8,9},{9,8},{10,11... | collective-permute-start | bytes 3145736 | tf_op jit(solution)/shard_map/ppermute | solution.py:165
  39.6 29.1 %collective-permute-start.4 = (bf16[3,1024,512]{2,1,0:T(8,128)(2,1)S(1)}, bf16[3,1024,512]{2,1,0:T(8,128)(2,1)S(1)}, u32[]{:S(2)}, u32[]{:S(2)}) collective-permute-start(bf16[3,1024,512]{2,1,0:T(8,128)(2,1)S(1)} %shard_map.101.refs_2_), channel_id=1, source_target_pairs={{0,1},{1,0},{2,3},{3,2},{4,5},{5,4},{6,7},{7,6},{8,9},{9,8},{10,11... | collective-permute-start | bytes 9437192 | tf_op jit(solution)/shard_map/ppermute | solution.py:165
  40.5 36.6 %collective-permute-start.9 = (bf16[768,512]{1,0:T(8,128)(2,1)S(1)}, bf16[768,512]{1,0:T(8,128)(2,1)S(1)}, u32[]{:S(2)}, u32[]{:S(2)}) collective-permute-start(bf16[768,512]{1,0:T(8,128)(2,1)S(1)} %shard_map.102.refs_2_), channel_id=1, source_target_pairs={{0,2},{1,3},{4,6},{5,7},{2,0},{3,1},{6,4},{7,5},{8,10},{9,11},{12,... | collective-permute-start | bytes 2359304 | tf_op jit(solution)/shard_map/ppermute | solution.py:168
  59.5 17.5 %collective-permute-start.10 = (bf16[768,512]{1,0:T(8,128)(2,1)S(1)}, bf16[768,512]{1,0:T(8,128)(2,1)S(1)}, u32[]{:S(2)}, u32[]{:S(2)}) collective-permute-start(bf16[768,512]{1,0:T(8,128)(2,1)S(1)} %shard_map.103.refs_4_), channel_id=1, source_target_pairs={{2,4},{3,5},{4,2},{5,3},{10,12},{11,13},{12,10},{13,11},{18,20},{1... | collective-permute-start | bytes 2359304 | tf_op jit(solution)/shard_map/ppermute | solution.py:168
  63.8 26.4 %collective-permute-start.8 = (bf16[768,512]{1,0:T(8,128)(2,1)S(1)}, bf16[768,512]{1,0:T(8,128)(2,1)S(1)}, u32[]{:S(2)}, u32[]{:S(2)}) collective-permute-start(bf16[768,512]{1,0:T(8,128)(2,1)S(1)} %shard_map.104.refs_4_.refs_0_), channel_id=1, source_target_pairs={{0,2},{1,3},{6,4},{7,5},{8,10},{9,11},{14,12},{15,13},{16,18},{17,... | collective-permute-start | bytes 2359304 | tf_op jit(solution)/shard_map/ppermute | solution.py:168
  83.8 16.5 %collective-permute-start.12 = (bf16[2,384,512]{2,1,0:T(8,128)(2,1)S(1)}, bf16[2,384,512]{2,1,0:T(8,128)(2,1)S(1)}, u32[]{:S(2)}, u32[]{:S(2)}) collective-permute-start(bf16[2,384,512]{2,1,0:T(8,128)(2,1)S(1)} %get-tuple-element.43), channel_id=1, source_target_pairs={{0,8},{8,0},{16,24},{24,16},{1,9},{9,1},{17,25},{25,17},{2,10},{10... | collective-permute-start | bytes 2359304 | tf_op jit(solution)/shard_map/ppermute | solution.py:171
  85.4 16.6 %collective-permute-start.13 = (bf16[2,384,512]{2,1,0:T(8,128)(2,1)S(1)}, bf16[2,384,512]{2,1,0:T(8,128)(2,1)S(1)}, u32[]{:S(2)}, u32[]{:S(2)}) collective-permute-start(bf16[2,384,512]{2,1,0:T(8,128)(2,1)S(1)} %get-tuple-element.45), channel_id=1, source_target_pairs={{0,16},{8,24},{16,0},{24,8},{1,17},{9,25},{17,1},{25,9},{2,18},{10... | collective-permute-start | bytes 2359304 | tf_op jit(solution)/shard_map/ppermute | solution.py:171
  90.9 13.7 %collective-permute-start.11 = (bf16[768,512]{1,0:T(8,128)(2,1)S(1)}, bf16[768,512]{1,0:T(8,128)(2,1)S(1)}, u32[]{:S(2)}, u32[]{:S(2)}) collective-permute-start(bf16[768,512]{1,0:T(8,128)(2,1)S(1)} %shard_map.107.refs_4_), channel_id=1, source_target_pairs={{2,4},{3,5},{4,2},{5,3},{10,12},{11,13},{12,10},{13,11},{18,20},{1... | collective-permute-start | bytes 2359304 | tf_op jit(solution)/shard_map/ppermute | solution.py:168
  91.6 20.5 %collective-permute-start.15 = (bf16[768,512]{1,0:T(8,128)(2,1)S(1)}, bf16[768,512]{1,0:T(8,128)(2,1)S(1)}, u32[]{:S(2)}, u32[]{:S(2)}) collective-permute-start(bf16[768,512]{1,0:T(8,128)(2,1)S(1)} %get-tuple-element.40.refs_4_.refs_0_), channel_id=1, source_target_pairs={{0,2},{1,3},{6,4},{7,5},{8,10},{9,11},{14,12},{15,13},{16,18},{17,... | collective-permute-start | bytes 2359304 | tf_op jit(solution)/shard_map/ppermute | solution.py:168
  119.7 15.1 %collective-permute-start.14 = (bf16[768,512]{1,0:T(8,128)(2,1)S(1)}, bf16[768,512]{1,0:T(8,128)(2,1)S(1)}, u32[]{:S(2)}, u32[]{:S(2)}) collective-permute-start(bf16[768,512]{1,0:T(8,128)(2,1)S(1)} %shard_map.109.refs_2_), channel_id=1, source_target_pairs={{0,2},{1,3},{4,6},{5,7},{2,0},{3,1},{6,4},{7,5},{8,10},{9,11},{12,... | collective-permute-start | bytes 2359304 | tf_op jit(solution)/shard_map/ppermute | solution.py:168
  122.2 12.6 %collective-permute-start.16 = (bf16[768,512]{1,0:T(8,128)(2,1)S(1)}, bf16[768,512]{1,0:T(8,128)(2,1)S(1)}, u32[]{:S(2)}, u32[]{:S(2)}) collective-permute-start(bf16[768,512]{1,0:T(8,128)(2,1)S(1)} %shard_map.110.refs_7_), channel_id=1, source_target_pairs={{2,4},{3,5},{4,2},{5,3},{10,12},{11,13},{12,10},{13,11},{18,20},{1... | collective-permute-start | bytes 2359304 | tf_op jit(solution)/shard_map/ppermute | solution.py:168
  129.1 17.2 %collective-permute-start.24 = (bf16[2,384,512]{2,1,0:T(8,128)(2,1)S(1)}, bf16[2,384,512]{2,1,0:T(8,128)(2,1)S(1)}, u32[]{:S(2)}, u32[]{:S(2)}) collective-permute-start(bf16[2,384,512]{2,1,0:T(8,128)(2,1)S(1)} %get-tuple-element.56), channel_id=1, source_target_pairs={{0,16},{8,24},{16,0},{24,8},{1,17},{9,25},{17,1},{25,9},{2,18},{10... | collective-permute-start | bytes 2359304 | tf_op jit(solution)/shard_map/ppermute | solution.py:171
  129.1 20.4 %collective-permute-start.23 = (bf16[2,384,512]{2,1,0:T(8,128)(2,1)S(1)}, bf16[2,384,512]{2,1,0:T(8,128)(2,1)S(1)}, u32[]{:S(2)}, u32[]{:S(2)}) collective-permute-start(bf16[2,384,512]{2,1,0:T(8,128)(2,1)S(1)} %get-tuple-element.50.refs_4_), channel_id=1, source_target_pairs={{0,8},{8,0},{16,24},{24,16},{1,9},{9,1},{17,25},{25,17},{2,10},{10... | collective-permute-start | bytes 2359304 | tf_op jit(solution)/shard_map/ppermute | solution.py:171
  139.2 23.3 %collective-permute-start.21 = (bf16[2,384,512]{2,1,0:T(8,128)(2,1)S(1)}, bf16[2,384,512]{2,1,0:T(8,128)(2,1)S(1)}, u32[]{:S(2)}, u32[]{:S(2)}) collective-permute-start(bf16[2,384,512]{2,1,0:T(8,128)(2,1)S(1)} %get-tuple-element.52), channel_id=1, source_target_pairs={{0,8},{8,0},{16,24},{24,16},{1,9},{9,1},{17,25},{25,17},{2,10},{10... | collective-permute-start | bytes 2359304 | tf_op jit(solution)/shard_map/ppermute | solution.py:171
  139.8 22.7 %collective-permute-start.22 = (bf16[2,384,512]{2,1,0:T(8,128)(2,1)S(1)}, bf16[2,384,512]{2,1,0:T(8,128)(2,1)S(1)}, u32[]{:S(2)}, u32[]{:S(2)}) collective-permute-start(bf16[2,384,512]{2,1,0:T(8,128)(2,1)S(1)} %get-tuple-element.53), channel_id=1, source_target_pairs={{0,16},{8,24},{16,0},{24,8},{1,17},{9,25},{17,1},{25,9},{2,18},{10... | collective-permute-start | bytes 2359304 | tf_op jit(solution)/shard_map/ppermute | solution.py:171
  165.3 13.3 %collective-permute-start.30 = (bf16[768,512]{1,0:T(8,128)(2,1)S(1)}, bf16[768,512]{1,0:T(8,128)(2,1)S(1)}, u32[]{:S(2)}, u32[]{:S(2)}) collective-permute-start(bf16[768,512]{1,0:T(8,128)(2,1)S(1)} %shard_map.114.refs_4_.refs_0_), channel_id=1, source_target_pairs={{2,4},{3,5},{4,2},{5,3},{10,12},{11,13},{12,10},{13,11},{18,20},{1... | collective-permute-start | bytes 2359304 | tf_op jit(solution)/shard_map/ppermute | solution.py:168
  166.0 19.5 %collective-permute-start.29 = (bf16[768,512]{1,0:T(8,128)(2,1)S(1)}, bf16[768,512]{1,0:T(8,128)(2,1)S(1)}, u32[]{:S(2)}, u32[]{:S(2)}) collective-permute-start(bf16[768,512]{1,0:T(8,128)(2,1)S(1)} %shard_map.114.refs_4_.refs_0_), channel_id=1, source_target_pairs={{0,2},{1,3},{4,6},{5,7},{2,0},{3,1},{6,4},{7,5},{8,10},{9,11},{12,... | collective-permute-start | bytes 2359304 | tf_op jit(solution)/shard_map/ppermute | solution.py:168
  177.6 11.9 %collective-permute-start.28 = (bf16[384,512]{1,0:T(8,128)(2,1)S(1)}, bf16[384,512]{1,0:T(8,128)(2,1)S(1)}, u32[]{:S(2)}, u32[]{:S(2)}) collective-permute-start(bf16[384,512]{1,0:T(8,128)(2,1)S(1)} %get-tuple-element.64.refs_2_.refs_1_), channel_id=1, source_target_pairs={{0,8},{8,0},{16,24},{24,16},{1,9},{9,1},{17,25},{25,17},{2,10},{10... | collective-permute-start | bytes 1179656 | tf_op jit(solution)/shard_map/ppermute | solution.py:171
  178.1 12.0 %collective-permute-start.27 = (bf16[384,512]{1,0:T(8,128)(2,1)S(1)}, bf16[384,512]{1,0:T(8,128)(2,1)S(1)}, u32[]{:S(2)}, u32[]{:S(2)}) collective-permute-start(bf16[384,512]{1,0:T(8,128)(2,1)S(1)} %get-tuple-element.63.refs_1_.refs_0_), channel_id=1, source_target_pairs={{0,16},{8,24},{16,0},{24,8},{1,17},{9,25},{17,1},{25,9},{2,18},{10... | collective-permute-start | bytes 1179656 | tf_op jit(solution)/shard_map/ppermute | solution.py:171
  179.2 17.9 %collective-permute-start.34 = (bf16[768,512]{1,0:T(8,128)(2,1)S(1)}, bf16[768,512]{1,0:T(8,128)(2,1)S(1)}, u32[]{:S(2)}, u32[]{:S(2)}) collective-permute-start(bf16[768,512]{1,0:T(8,128)(2,1)S(1)} %shard_map.117.refs_1_.refs_6_.refs_4_), channel_id=1, source_target_pairs={{4,6},{5,7},{2,0},{3,1},{12,14},{13,15},{10,8},{11,9},{20,22},{21,... | collective-permute-start | bytes 2359304 | tf_op jit(solution)/shard_map/ppermute | solution.py:168
  190.8 12.1 %collective-permute-start.32 = (bf16[2,384,512]{2,1,0:T(8,128)(2,1)S(1)}, bf16[2,384,512]{2,1,0:T(8,128)(2,1)S(1)}, u32[]{:S(2)}, u32[]{:S(2)}) collective-permute-start(bf16[2,384,512]{2,1,0:T(8,128)(2,1)S(1)} %get-tuple-element.66), channel_id=1, source_target_pairs={{0,16},{8,24},{16,0},{24,8},{1,17},{9,25},{17,1},{25,9},{2,18},{10... | collective-permute-start | bytes 2359304 | tf_op jit(solution)/shard_map/ppermute | solution.py:171
  191.4 12.0 %collective-permute-start.31 = (bf16[2,384,512]{2,1,0:T(8,128)(2,1)S(1)}, bf16[2,384,512]{2,1,0:T(8,128)(2,1)S(1)}, u32[]{:S(2)}, u32[]{:S(2)}) collective-permute-start(bf16[2,384,512]{2,1,0:T(8,128)(2,1)S(1)} %get-tuple-element.65.refs_2_), channel_id=1, source_target_pairs={{0,8},{8,0},{16,24},{24,16},{1,9},{9,1},{17,25},{25,17},{2,10},{10... | collective-permute-start | bytes 2359304 | tf_op jit(solution)/shard_map/ppermute | solution.py:171
  197.6 22.8 %collective-permute-start.37 = (bf16[768,512]{1,0:T(8,128)(2,1)S(1)}, bf16[768,512]{1,0:T(8,128)(2,1)S(1)}, u32[]{:S(2)}, u32[]{:S(2)}) collective-permute-start(bf16[768,512]{1,0:T(8,128)(2,1)S(1)} %shard_map.120.refs_10_.refs_7_), channel_id=1, source_target_pairs={{4,6},{5,7},{2,0},{3,1},{12,14},{13,15},{10,8},{11,9},{20,22},{21,... | collective-permute-start | bytes 2359304 | tf_op jit(solution)/shard_map/ppermute | solution.py:168
  207.3 18.0 %collective-permute-start.36 = (bf16[768,512]{1,0:T(8,128)(2,1)S(1)}, bf16[768,512]{1,0:T(8,128)(2,1)S(1)}, u32[]{:S(2)}, u32[]{:S(2)}) collective-permute-start(bf16[768,512]{1,0:T(8,128)(2,1)S(1)} %shard_map.121.refs_14_.refs_0_), channel_id=1, source_target_pairs={{2,4},{3,5},{4,2},{5,3},{10,12},{11,13},{12,10},{13,11},{18,20},{1... | collective-permute-start | bytes 2359304 | tf_op jit(solution)/shard_map/ppermute | solution.py:168
  208.0 29.2 %collective-permute-start.35 = (bf16[768,512]{1,0:T(8,128)(2,1)S(1)}, bf16[768,512]{1,0:T(8,128)(2,1)S(1)}, u32[]{:S(2)}, u32[]{:S(2)}) collective-permute-start(bf16[768,512]{1,0:T(8,128)(2,1)S(1)} %shard_map.121.refs_14_.refs_0_), channel_id=1, source_target_pairs={{0,2},{1,3},{4,6},{5,7},{2,0},{3,1},{6,4},{7,5},{8,10},{9,11},{12,... | collective-permute-start | bytes 2359304 | tf_op jit(solution)/shard_map/ppermute | solution.py:168
  225.9 21.8 %collective-permute-start.39 = (bf16[768,512]{1,0:T(8,128)(2,1)S(1)}, bf16[768,512]{1,0:T(8,128)(2,1)S(1)}, u32[]{:S(2)}, u32[]{:S(2)}) collective-permute-start(bf16[768,512]{1,0:T(8,128)(2,1)S(1)} %shard_map.123.refs_1_.refs_4_), channel_id=1, source_target_pairs={{4,6},{5,7},{2,0},{3,1},{12,14},{13,15},{10,8},{11,9},{20,22},{21,... | collective-permute-start | bytes 2359304 | tf_op jit(solution)/shard_map/ppermute | solution.py:168
  238.6 11.5 %collective-permute-start.42 = (bf16[768,512]{1,0:T(8,128)(2,1)S(1)}, bf16[768,512]{1,0:T(8,128)(2,1)S(1)}, u32[]{:S(2)}, u32[]{:S(2)}) collective-permute-start(bf16[768,512]{1,0:T(8,128)(2,1)S(1)} %shard_map.123.refs_1_.refs_4_), channel_id=1, source_target_pairs={{0,1},{1,0},{2,3},{3,2},{4,5},{5,4},{6,7},{7,6},{8,9},{9,8},{10,11... | collective-permute-start | bytes 2359304 | tf_op jit(solution)/shard_map/ppermute | solution.py:165
  247.7 25.2 %collective-permute-start.47 = (bf16[768,1024]{1,0:T(8,128)(2,1)S(1)}, bf16[768,1024]{1,0:T(8,128)(2,1)S(1)}, u32[]{:S(2)}, u32[]{:S(2)}) collective-permute-start(bf16[768,1024]{1,0:T(8,128)(2,1)S(1)} %shard_map.122.refs_1_), channel_id=1, source_target_pairs={{0,1},{1,0},{2,3},{3,2},{4,5},{5,4},{6,7},{7,6},{8,9},{9,8},{10,11... | collective-permute-start | bytes 4718600 | tf_op jit(solution)/shard_map/ppermute | solution.py:165
  248.8 22.5 %collective-permute-start.44 = (bf16[768,512]{1,0:T(8,128)(2,1)S(1)}, bf16[768,512]{1,0:T(8,128)(2,1)S(1)}, u32[]{:S(2)}, u32[]{:S(2)}) collective-permute-start(bf16[768,512]{1,0:T(8,128)(2,1)S(1)} %shard_map.125.refs_14_.refs_0_), channel_id=1, source_target_pairs={{4,6},{5,7},{2,0},{3,1},{12,14},{13,15},{10,8},{11,9},{20,22},{21,... | collective-permute-start | bytes 2359304 | tf_op jit(solution)/shard_map/ppermute | solution.py:168
  (35 other events, 318.0 us)

commit v4 on v3

--- a/solution.py
+++ b/solution.py
@@ -9,8 +9,8 @@
 from jax.sharding import PartitionSpec as P
 
 F32, BF16 = jnp.float32, jnp.bfloat16
-VMEM_BYTES = 38 * 2**20
-FLOPS_A_US = 6000000000
+VMEM_BYTES = 39 * 2**20
+FLOPS_A_US = 7 * 10**9
 ANY = pl.BlockSpec(memory_space=pl.ANY)
 
 
@@ -421,7 +421,7 @@
                     ns = 0.95 * ins[n + 1][...] + 0.05 * rotated * rotated
                     outs[2][...] = nf
                     outs[3][...] = ns
-                    outs[k][...] = (nf / first_fix / (jnp.sqrt(ns / second_fix) + 1e-08)).astype(BF16)
+                    outs[k][...] = (nf * (1.0 / first_fix) / (jnp.sqrt(ns * (1.0 / second_fix)) + 1e-08)).astype(BF16)
 
         spot = pl.BlockSpec((tile, width), lambda r, p: (r, first // width))
         half_specs = [

time: 283 us -> 283 us (level)
  waiting for transfers between devices: 105 us -> 91.7 us
  starting transfers between devices: 74.5 us -> 83.2 us
  local copies, waits for them, and re-layouts: 4.08 us -> 8.52 us
    ppermute x16, waiting for transfers between devices: 38.6 us -> 20.5 us  [to_partner(): return lax.ppermute(x, 'row', [(i, i ^ s) for i in range(row_size)])]
    ppermute x20, starting transfers between devices: 55.7 us -> 62.4 us  [along(): lax.ppermute(x, 'col', [(2 * a + c, 2 * b + c) for a, b in pairs for c in...]
    ppermute x20, waiting for transfers between devices: 62.9 us -> 67.6 us  [along(): lax.ppermute(x, 'col', [(2 * a + c, 2 * b + c) for a, b in pairs for c in...]
    unnamed x38 -> x56, local copies, waits for them, and re-layouts: 3.38 us -> 7.82 us
  transfers between devices with their start and end apart: 48 -> 48, of which waited for: 26 -> 21; matrix products, arithmetic and copies ran while one was open for 0% -> 0% of each run, Pallas kernels for 30% -> 30%
where the time goes in v4:
time: 283 us; the launch traced here: 282 us
  Pallas kernels  96.5 us (34%)
  waiting for transfers between devices  91.7 us (32%)
  starting transfers between devices  83.2 us (29%)
  local copies, waits for them, and re-layouts  8.52 us (3%)
    pallas_call x37, Pallas kernels, call(): pl.pallas_call(wrapped, out_shape=outs, grid_spec=pltpu.PrefetchScalarGri...  96.5 us
    ppermute x20, waiting for transfers between devices, along(): lax.ppermute(x, 'col', [(2 * a + c, 2 * b + c) for a, b in pairs for c in...  67.6 us
    ppermute x20, starting transfers between devices, along(): lax.ppermute(x, 'col', [(2 * a + c, 2 * b + c) for a, b in pairs for c in...  62.4 us
    ppermute x16, waiting for transfers between devices, to_partner(): return lax.ppermute(x, 'row', [(i, i ^ s) for i in range(row_size)])  20.5 us
    ppermute x16, starting transfers between devices, to_partner(): return lax.ppermute(x, 'row', [(i, i ^ s) for i in range(row_size)])  17.8 us
    unnamed x56, local copies, waits for them, and re-layouts  7.82 us
  transfers between devices with their start and end apart: 48, of which 21 were waited for; matrix products, arithmetic and copies ran while one was open for 0% of the time, Pallas kernels for 30%

profile of v4, /device:TPU:0, one launch (start us, length us, event | category | flops | bytes accessed | tf_op | source)
XLA Modules:
  0.0 281.5 jit_solution(11472545207069154674)
XLA Ops:
  8.6 3.6 %shard_map.96.refs_1_.refs_0_ = bf16[768,512]{1,0:T(8,128)(2,1)S(1)} custom-call(s32[17]{0:T(128)S(1)} %pad_add_fusion.place_ref, bf16[768,1024]{1,0:T(8,128)(2,1)S(1)} %copy-done.4, bf16[768,1024]{1,0:T(8,128)(2,1)S(1)} %collective-permute-done.refs_1_, bf16[1024,8192]{1,0:T(8,128)(2,1)} %refs_5_.5, ...), custom_call_target="tpu_custom_call" | custom-call | flops 17500000256 | bytes 1 | tf_op jit(solution)/shard_map/pallas_call | solution.py:32
  12.2 4.9 %collective-permute-start.2 = (bf16[768,512]{1,0:T(8,128)(2,1)S(1)}, bf16[768,512]{1,0:T(8,128)(2,1)S(1)}, u32[]{:S(2)}, u32[]{:S(2)}) collective-permute-start(bf16[768,512]{1,0:T(8,128)(2,1)S(1)} %shard_map.96.refs_1_.refs_0_), channel_id=1, source_target_pairs={{0,2},{1,3},{6,4},{7,5},{8,10},{9,11},{14,12},{15,13},{16,18},{17,... | collective-permute-start | bytes 2359304 | tf_op jit(solution)/shard_map/ppermute | solution.py:168
  19.5 8.3 %shard_map.98 = (bf16[768,512]{1,0:T(8,128)(2,1)S(1)}, bf16[768,512]{1,0:T(8,128)(2,1)S(1)}, bf16[768,512]{1,0:T(8,128)(2,1)S(1)}) custom-call(s32[17]{0:T(128)S(1)} %pad_add_fusion.place_ref, bf16[768,1024]{1,0:T(8,128)(2,1)S(1)} %copy-done.4, bf16[768,1024]{1,0:T(8,128)(2,1)S(1)} %collective-permute-done.refs_1_, bf16[1024,8192]{1,0:T(8,128)(2,1)} %refs_5_.5, ...), custom_call_target="tpu_custom_call" | custom-call | flops 52500000768 | bytes 1 | tf_op jit(solution)/shard_map/pallas_call | solution.py:32
  31.1 3.8 %collective-permute-done.2.refs_1_ = bf16[768,512]{1,0:T(8,128)(2,1)S(1)} collective-permute-done((bf16[768,512]{1,0:T(8,128)(2,1)S(1)}, bf16[768,512]{1,0:T(8,128)(2,1)S(1)}, u32[]{:S(2)}, u32[]{:S(2)}) %collective-permute-start.2) | collective-permute-done | bytes 786464 | tf_op jit(solution)/shard_map/ppermute | solution.py:168
  36.5 3.2 %shard_map.101.refs_2_ = bf16[3,1024,512]{2,1,0:T(8,128)(2,1)S(1)} custom-call(s32[17]{0:T(128)S(1)} %pad_add_fusion.place_ref, bf16[1024,8192]{1,0:T(8,128)(2,1)} %refs_5_.5, bf16[768,512]{1,0:T(8,128)(2,1)S(1)} %shard_map.100.refs_1_), custom_call_target="tpu_custom_call" | custom-call | flops 31499999232 | bytes 1 | tf_op jit(solution)/shard_map/pallas_call | solution.py:32
  40.6 18.3 %collective-permute-start.9 = (bf16[768,512]{1,0:T(8,128)(2,1)S(1)}, bf16[768,512]{1,0:T(8,128)(2,1)S(1)}, u32[]{:S(2)}, u32[]{:S(2)}) collective-permute-start(bf16[768,512]{1,0:T(8,128)(2,1)S(1)} %shard_map.102.refs_2_), channel_id=1, source_target_pairs={{0,2},{1,3},{4,6},{5,7},{2,0},{3,1},{6,4},{7,5},{8,10},{9,11},{12,... | collective-permute-start | bytes 2359304 | tf_op jit(solution)/shard_map/ppermute | solution.py:168
  60.4 3.6 %shard_map.104.refs_4_.refs_0_ = bf16[768,512]{1,0:T(8,128)(2,1)S(1)} custom-call(s32[17]{0:T(128)S(1)} %pad_add_fusion.place_ref, bf16[768,1024]{1,0:T(8,128)(2,1)S(1)} %copy-done.4, bf16[768,1024]{1,0:T(8,128)(2,1)S(1)} %collective-permute-done.refs_1_, bf16[1024,8192]{1,0:T(8,128)(2,1)} %refs_5_.5, ...), custom_call_target="tpu_custom_call" | custom-call | flops 17500000256 | bytes 1 | tf_op jit(solution)/shard_map/pallas_call | solution.py:32
  63.9 4.9 %collective-permute-start.8 = (bf16[768,512]{1,0:T(8,128)(2,1)S(1)}, bf16[768,512]{1,0:T(8,128)(2,1)S(1)}, u32[]{:S(2)}, u32[]{:S(2)}) collective-permute-start(bf16[768,512]{1,0:T(8,128)(2,1)S(1)} %shard_map.104.refs_4_.refs_0_), channel_id=1, source_target_pairs={{0,2},{1,3},{6,4},{7,5},{8,10},{9,11},{14,12},{15,13},{16,18},{17,... | collective-permute-start | bytes 2359304 | tf_op jit(solution)/shard_map/ppermute | solution.py:168
  68.8 7.5 %shard_map.105 = (bf16[768,512]{1,0:T(8,128)(2,1)S(1)}, bf16[768,512]{1,0:T(8,128)(2,1)S(1)}, bf16[768,512]{1,0:T(8,128)(2,1)S(1)}) custom-call(s32[17]{0:T(128)S(1)} %pad_add_fusion.place_ref, bf16[768,1024]{1,0:T(8,128)(2,1)S(1)} %copy-done.4, bf16[768,1024]{1,0:T(8,128)(2,1)S(1)} %collective-permute-done.refs_1_, bf16[1024,8192]{1,0:T(8,128)(2,1)} %refs_5_.5, ...), custom_call_target="tpu_custom_call" | custom-call | flops 52500000768 | bytes 1 | tf_op jit(solution)/shard_map/pallas_call | solution.py:32
  79.5 4.4 %shard_map.106 = (bf16[768,512]{1,0:T(8,128)(2,1)S(1)}, bf16[2,384,512]{2,1,0:T(8,128)(2,1)S(1)}, bf16[2,384,512]{2,1,0:T(8,128)(2,1)S(1)}, bf16[384,512]{1,0:T(8,128)(2,1)S(1)}, bf16[384,512]{1,0:T(8,128)(2,1)S(1)}) custom-call(s32[17]{0:T(128)S(1)} %pad_add_fusion.place_ref, bf16[768,512]{1,0:T(8,128)(2,1)S(1)} %copy-done.25, ...), custom_call_target="tpu_custom_call" | custom-call | flops 35000000512 | bytes 1 | tf_op jit(solution)/shard_map/pallas_call | solution.py:32
  87.0 3.3 %collective-permute-done.8.refs_1_ = bf16[768,512]{1,0:T(8,128)(2,1)S(1)} collective-permute-done((bf16[768,512]{1,0:T(8,128)(2,1)S(1)}, bf16[768,512]{1,0:T(8,128)(2,1)S(1)}, u32[]{:S(2)}, u32[]{:S(2)}) %collective-permute-start.8) | collective-permute-done | bytes 786464 | tf_op jit(solution)/shard_map/ppermute | solution.py:168
  91.8 7.2 %collective-permute-start.15 = (bf16[768,512]{1,0:T(8,128)(2,1)S(1)}, bf16[768,512]{1,0:T(8,128)(2,1)S(1)}, u32[]{:S(2)}, u32[]{:S(2)}) collective-permute-start(bf16[768,512]{1,0:T(8,128)(2,1)S(1)} %get-tuple-element.40.refs_4_.refs_0_), channel_id=1, source_target_pairs={{0,2},{1,3},{6,4},{7,5},{8,10},{9,11},{14,12},{15,13},{16,18},{17,... | collective-permute-start | bytes 2359304 | tf_op jit(solution)/shard_map/ppermute | solution.py:168
  105.5 6.8 %collective-permute-done.15.refs_1_ = bf16[768,512]{1,0:T(8,128)(2,1)S(1)} collective-permute-done((bf16[768,512]{1,0:T(8,128)(2,1)S(1)}, bf16[768,512]{1,0:T(8,128)(2,1)S(1)}, u32[]{:S(2)}, u32[]{:S(2)}) %collective-permute-start.15) | collective-permute-done | bytes 786464 | tf_op jit(solution)/shard_map/ppermute | solution.py:168
  113.0 3.8 %shard_map.111 = (bf16[384,512]{1,0:T(8,128)(2,1)S(1)}, bf16[384,512]{1,0:T(8,128)(2,1)S(1)}, f32[768,1024]{1,0:T(8,128)}, f32[768,1024]{1,0:T(8,128)}) custom-call(s32[17]{0:T(128)S(1)} %pad_add_fusion.place_ref, bf16[768,512]{1,0:T(8,128)(2,1)S(1)} %get-tuple-element.41.refs_2_.refs_0_, bf16[2,384,512]{2,1,0:T(8,128)(2,1)S(1)} %collective-permute-done.12.refs_1_, ...), custom_call_target="tpu_custom_call" | custom-call | flops 35000000512 | bytes 1 | tf_op jit(solution)/shard_map/pallas_call | solution.py:32
  130.8 4.1 %collective-permute-done.14.refs_1_ = bf16[768,512]{1,0:T(8,128)(2,1)S(1)} collective-permute-done((bf16[768,512]{1,0:T(8,128)(2,1)S(1)}, bf16[768,512]{1,0:T(8,128)(2,1)S(1)}, u32[]{:S(2)}, u32[]{:S(2)}) %collective-permute-start.14) | collective-permute-done | bytes 786464 | tf_op jit(solution)/shard_map/ppermute | solution.py:168
  139.4 4.4 %shard_map.113 = (bf16[768,512]{1,0:T(8,128)(2,1)S(1)}, bf16[2,384,512]{2,1,0:T(8,128)(2,1)S(1)}, bf16[2,384,512]{2,1,0:T(8,128)(2,1)S(1)}, bf16[384,512]{1,0:T(8,128)(2,1)S(1)}, bf16[384,512]{1,0:T(8,128)(2,1)S(1)}) custom-call(s32[17]{0:T(128)S(1)} %pad_add_fusion.place_ref, bf16[768,512]{1,0:T(8,128)(2,1)S(1)} %copy-done.23, ...), custom_call_target="tpu_custom_call" | custom-call | flops 35000000512 | bytes 1 | tf_op jit(solution)/shard_map/pallas_call | solution.py:32
  145.3 3.9 %shard_map.114.refs_4_.refs_0_ = bf16[768,512]{1,0:T(8,128)(2,1)S(1)} custom-call(s32[17]{0:T(128)S(1)} %pad_add_fusion.place_ref, bf16[384,512]{1,0:T(8,128)(2,1)S(1)} %copy-done.10, bf16[384,512]{1,0:T(8,128)(2,1)S(1)} %copy-done.12, bf16[2,384,512]{2,1,0:T(8,128)(2,1)S(1)} %collective-permute-done.23.refs_2_, bf16[384,512]{1,0:T(8,128)(2,1)S(1)} %copy-done.16, ...), custom_call_target="tpu_custom_call" | custom-call | flops 35000000512 | bytes 1 | tf_op jit(solution)/shard_map/pallas_call | solution.py:32
  149.2 10.7 %collective-permute-done.21.refs_1_ = bf16[2,384,512]{2,1,0:T(8,128)(2,1)S(1)} collective-permute-done((bf16[2,384,512]{2,1,0:T(8,128)(2,1)S(1)}, bf16[2,384,512]{2,1,0:T(8,128)(2,1)S(1)}, u32[]{:S(2)}, u32[]{:S(2)}) %collective-permute-start.21) | collective-permute-done | bytes 786464 | tf_op jit(solution)/shard_map/ppermute | solution.py:171
  163.3 6.4 %collective-permute-start.29 = (bf16[768,512]{1,0:T(8,128)(2,1)S(1)}, bf16[768,512]{1,0:T(8,128)(2,1)S(1)}, u32[]{:S(2)}, u32[]{:S(2)}) collective-permute-start(bf16[768,512]{1,0:T(8,128)(2,1)S(1)} %shard_map.114.refs_4_.refs_0_), channel_id=1, source_target_pairs={{0,2},{1,3},{4,6},{5,7},{2,0},{3,1},{6,4},{7,5},{8,10},{9,11},{12,... | collective-permute-start | bytes 2359304 | tf_op jit(solution)/shard_map/ppermute | solution.py:168
  169.9 3.8 %shard_map.116 = (bf16[384,512]{1,0:T(8,128)(2,1)S(1)}, bf16[384,512]{1,0:T(8,128)(2,1)S(1)}, f32[768,1024]{1,0:T(8,128)}, f32[768,1024]{1,0:T(8,128)}) custom-call(s32[17]{0:T(128)S(1)} %pad_add_fusion.place_ref, bf16[768,512]{1,0:T(8,128)(2,1)S(1)} %get-tuple-element.51.refs_10_.refs_0_, ...), custom_call_target="tpu_custom_call", output_to_operand_aliasing={{2}: (8, {}), {3}: (9, {})} | custom-call | flops 35000000512 | bytes 1 | tf_op jit(solution)/shard_map/pallas_call | solution.py:32
  177.6 6.1 %collective-permute-done.29.refs_0_ = bf16[768,512]{1,0:T(8,128)(2,1)S(1)} collective-permute-done((bf16[768,512]{1,0:T(8,128)(2,1)S(1)}, bf16[768,512]{1,0:T(8,128)(2,1)S(1)}, u32[]{:S(2)}, u32[]{:S(2)}) %collective-permute-start.29) | collective-permute-done | bytes 786464 | tf_op jit(solution)/shard_map/ppermute | solution.py:168
  188.8 8.2 %collective-permute-done.34.refs_1_.refs_7_.refs_5_ = bf16[768,512]{1,0:T(8,128)(2,1)S(1)} collective-permute-done((bf16[768,512]{1,0:T(8,128)(2,1)S(1)}, bf16[768,512]{1,0:T(8,128)(2,1)S(1)}, u32[]{:S(2)}, u32[]{:S(2)}) %collective-permute-start.34) | collective-permute-done | bytes 786464 | tf_op jit(solution)/shard_map/ppermute | solution.py:168
  200.0 3.9 %shard_map.121.refs_14_.refs_0_ = bf16[768,512]{1,0:T(8,128)(2,1)S(1)} custom-call(s32[17]{0:T(128)S(1)} %pad_add_fusion.place_ref, bf16[384,512]{1,0:T(8,128)(2,1)S(1)} %get-tuple-element.63.refs_1_.refs_0_, bf16[384,512]{1,0:T(8,128)(2,1)S(1)} %get-tuple-element.64.refs_2_.refs_1_, bf16[2,384,512]{2,1,0:T(8,128)(2,1)S(1)} %collective-permute-done.31.refs_2_, ...), custom_call_target="tpu_custom_call" | custom-call | flops 35000000512 | bytes 1 | tf_op jit(solution)/shard_map/pallas_call | solution.py:32
  204.6 5.5 %collective-permute-start.35 = (bf16[768,512]{1,0:T(8,128)(2,1)S(1)}, bf16[768,512]{1,0:T(8,128)(2,1)S(1)}, u32[]{:S(2)}, u32[]{:S(2)}) collective-permute-start(bf16[768,512]{1,0:T(8,128)(2,1)S(1)} %shard_map.121.refs_14_.refs_0_), channel_id=1, source_target_pairs={{0,2},{1,3},{4,6},{5,7},{2,0},{3,1},{6,4},{7,5},{8,10},{9,11},{12,... | collective-permute-start | bytes 2359304 | tf_op jit(solution)/shard_map/ppermute | solution.py:168
  210.1 10.1 %collective-permute-done.37.refs_11_.refs_8_ = bf16[768,512]{1,0:T(8,128)(2,1)S(1)} collective-permute-done((bf16[768,512]{1,0:T(8,128)(2,1)S(1)}, bf16[768,512]{1,0:T(8,128)(2,1)S(1)}, u32[]{:S(2)}, u32[]{:S(2)}) %collective-permute-start.37) | collective-permute-done | bytes 786464 | tf_op jit(solution)/shard_map/ppermute | solution.py:168
  220.2 4.9 %shard_map.122.refs_1_ = bf16[768,1024]{1,0:T(8,128)(2,1)S(1)} custom-call(s32[17]{0:T(128)S(1)} %pad_add_fusion.place_ref, bf16[768,512]{1,0:T(8,128)(2,1)S(1)} %shard_map.114.refs_4_.refs_0_, bf16[1,1024,512]{2,1,0:T(8,128)(2,1)S(1)} %copy-done.6, bf16[3,1024,512]{2,1,0:T(8,128)(2,1)S(1)} %copy-done.3, ...), custom_call_target="tpu_custom_call" | custom-call | flops 56000000000 | bytes 1 | tf_op jit(solution)/shard_map/pallas_call | solution.py:32
  227.0 10.0 %collective-permute-done.35.refs_0_ = bf16[768,512]{1,0:T(8,128)(2,1)S(1)} collective-permute-done((bf16[768,512]{1,0:T(8,128)(2,1)S(1)}, bf16[768,512]{1,0:T(8,128)(2,1)S(1)}, u32[]{:S(2)}, u32[]{:S(2)}) %collective-permute-start.35) | collective-permute-done | bytes 786464 | tf_op jit(solution)/shard_map/ppermute | solution.py:168
  239.0 9.2 %collective-permute-done.39.refs_1_.refs_5_ = bf16[768,512]{1,0:T(8,128)(2,1)S(1)} collective-permute-done((bf16[768,512]{1,0:T(8,128)(2,1)S(1)}, bf16[768,512]{1,0:T(8,128)(2,1)S(1)}, u32[]{:S(2)}, u32[]{:S(2)}) %collective-permute-start.39) | collective-permute-done | bytes 786464 | tf_op jit(solution)/shard_map/ppermute | solution.py:168
  250.6 8.1 %shard_map.126.refs_10_.refs_11_ = f32[768,1024]{1,0:T(8,128)S(1)} custom-call(s32[17]{0:T(128)S(1)} %pad_add_fusion.place_ref, bf16[768,512]{1,0:T(8,128)(2,1)S(1)} %shard_map.121.refs_14_.refs_0_, bf16[1024,8192]{1,0:T(8,128)(2,1)} %refs_5_.5, bf16[768,512]{1,0:T(8,128)(2,1)S(1)} %shard_map.124.refs_2_, bf16[1024,8192]{1,0:T(8,128)(2,1)} %refs_5_.5, ...), custom_call_target="tpu_custom_call" | custom-call | flops 56000000000 | bytes 1 | tf_op jit(solution)/shard_map/pallas_call | solution.py:32
  258.7 6.4 %shard_map.127.refs_1_.refs_7_ = f32[768,1024]{1,0:T(8,128)S(1)} custom-call(s32[17]{0:T(128)S(1)} %pad_add_fusion.place_ref, bf16[768,512]{1,0:T(8,128)(2,1)S(1)} %shard_map.114.refs_4_.refs_0_, bf16[1024,8192]{1,0:T(8,128)(2,1)} %refs_5_.5, bf16[768,512]{1,0:T(8,128)(2,1)S(1)} %shard_map.118.refs_4_.refs_3_.refs_2_, bf16[1024,8192]{1,0:T(8,128)(2,1)} %refs_5_.5, ...), custom_call_target="tpu_custom_call" | custom-call | flops 56000000000 | bytes 1 | tf_op jit(solution)/shard_map/pallas_call | solution.py:32
  265.2 5.9 %collective-permute-done.44.refs_0_ = bf16[768,512]{1,0:T(8,128)(2,1)S(1)} collective-permute-done((bf16[768,512]{1,0:T(8,128)(2,1)S(1)}, bf16[768,512]{1,0:T(8,128)(2,1)S(1)}, u32[]{:S(2)}, u32[]{:S(2)}) %collective-permute-start.44) | collective-permute-done | bytes 786464 | tf_op jit(solution)/shard_map/ppermute | solution.py:168
  275.7 5.8 %shard_map.130 = f32[768,1024]{1,0:T(8,128)} custom-call(s32[17]{0:T(128)S(1)} %pad_add_fusion.place_ref, bf16[768,512]{1,0:T(8,128)(2,1)S(1)} %shard_map.128.refs_1_.refs_0_, bf16[768,512]{1,0:T(8,128)(2,1)S(1)} %shard_map.129.refs_1_.refs_8_, bf16[1024,8192]{1,0:T(8,128)(2,1)} %refs_5_.5, bf16[768,512]{1,0:T(8,128)(2,1)S(1)} %collective-permute-done.45.refs_3_, ...), custom_call_target="tpu_custom_call" | custom-call | flops 56000000000 | bytes 1 | tf_op jit(solution)/shard_map/pallas_call | solution.py:32
  (161 shorter events, 78.9 us)
Async XLA Ops:
  7.4 12.1 %collective-permute-start.3 = (bf16[3,1024,512]{2,1,0:T(8,128)(2,1)S(1)}, bf16[3,1024,512]{2,1,0:T(8,128)(2,1)S(1)}, u32[]{:S(2)}, u32[]{:S(2)}) collective-permute-start(bf16[3,1024,512]{2,1,0:T(8,128)(2,1)S(1)} %shard_map.95.refs_4_), channel_id=1, source_target_pairs={{0,1},{1,0},{2,3},{3,2},{4,5},{5,4},{6,7},{7,6},{8,9},{9,8},{10,11... | collective-permute-start | bytes 9437192 | tf_op jit(solution)/shard_map/ppermute | solution.py:165
  12.2 22.7 %collective-permute-start.2 = (bf16[768,512]{1,0:T(8,128)(2,1)S(1)}, bf16[768,512]{1,0:T(8,128)(2,1)S(1)}, u32[]{:S(2)}, u32[]{:S(2)}) collective-permute-start(bf16[768,512]{1,0:T(8,128)(2,1)S(1)} %shard_map.96.refs_1_.refs_0_), channel_id=1, source_target_pairs={{0,2},{1,3},{6,4},{7,5},{8,10},{9,11},{14,12},{15,13},{16,18},{17,... | collective-permute-start | bytes 2359304 | tf_op jit(solution)/shard_map/ppermute | solution.py:168
  27.8 31.1 %collective-permute-start.6 = (bf16[768,512]{1,0:T(8,128)(2,1)S(1)}, bf16[768,512]{1,0:T(8,128)(2,1)S(1)}, u32[]{:S(2)}, u32[]{:S(2)}) collective-permute-start(bf16[768,512]{1,0:T(8,128)(2,1)S(1)} %get-tuple-element.35.refs_1_.refs_0_), channel_id=1, source_target_pairs={{0,2},{1,3},{6,4},{7,5},{8,10},{9,11},{14,12},{15,13},{16,18},{17,... | collective-permute-start | bytes 2359304 | tf_op jit(solution)/shard_map/ppermute | solution.py:168
  31.1 29.3 %collective-permute-start.5 = (bf16[1,1024,512]{2,1,0:T(8,128)(2,1)S(1)}, bf16[1,1024,512]{2,1,0:T(8,128)(2,1)S(1)}, u32[]{:S(2)}, u32[]{:S(2)}) collective-permute-start(bf16[1,1024,512]{2,1,0:T(8,128)(2,1)S(1)} %shard_map.99.refs_2_), channel_id=1, source_target_pairs={{0,1},{1,0},{2,3},{3,2},{4,5},{5,4},{6,7},{7,6},{8,9},{9,8},{10,11... | collective-permute-start | bytes 3145736 | tf_op jit(solution)/shard_map/ppermute | solution.py:165
  39.8 29.1 %collective-permute-start.4 = (bf16[3,1024,512]{2,1,0:T(8,128)(2,1)S(1)}, bf16[3,1024,512]{2,1,0:T(8,128)(2,1)S(1)}, u32[]{:S(2)}, u32[]{:S(2)}) collective-permute-start(bf16[3,1024,512]{2,1,0:T(8,128)(2,1)S(1)} %shard_map.101.refs_2_), channel_id=1, source_target_pairs={{0,1},{1,0},{2,3},{3,2},{4,5},{5,4},{6,7},{7,6},{8,9},{9,8},{10,11... | collective-permute-start | bytes 9437192 | tf_op jit(solution)/shard_map/ppermute | solution.py:165
  40.6 36.6 %collective-permute-start.9 = (bf16[768,512]{1,0:T(8,128)(2,1)S(1)}, bf16[768,512]{1,0:T(8,128)(2,1)S(1)}, u32[]{:S(2)}, u32[]{:S(2)}) collective-permute-start(bf16[768,512]{1,0:T(8,128)(2,1)S(1)} %shard_map.102.refs_2_), channel_id=1, source_target_pairs={{0,2},{1,3},{4,6},{5,7},{2,0},{3,1},{6,4},{7,5},{8,10},{9,11},{12,... | collective-permute-start | bytes 2359304 | tf_op jit(solution)/shard_map/ppermute | solution.py:168
  59.6 17.5 %collective-permute-start.10 = (bf16[768,512]{1,0:T(8,128)(2,1)S(1)}, bf16[768,512]{1,0:T(8,128)(2,1)S(1)}, u32[]{:S(2)}, u32[]{:S(2)}) collective-permute-start(bf16[768,512]{1,0:T(8,128)(2,1)S(1)} %shard_map.103.refs_4_), channel_id=1, source_target_pairs={{2,4},{3,5},{4,2},{5,3},{10,12},{11,13},{12,10},{13,11},{18,20},{1... | collective-permute-start | bytes 2359304 | tf_op jit(solution)/shard_map/ppermute | solution.py:168
  63.9 26.4 %collective-permute-start.8 = (bf16[768,512]{1,0:T(8,128)(2,1)S(1)}, bf16[768,512]{1,0:T(8,128)(2,1)S(1)}, u32[]{:S(2)}, u32[]{:S(2)}) collective-permute-start(bf16[768,512]{1,0:T(8,128)(2,1)S(1)} %shard_map.104.refs_4_.refs_0_), channel_id=1, source_target_pairs={{0,2},{1,3},{6,4},{7,5},{8,10},{9,11},{14,12},{15,13},{16,18},{17,... | collective-permute-start | bytes 2359304 | tf_op jit(solution)/shard_map/ppermute | solution.py:168
  83.9 16.5 %collective-permute-start.12 = (bf16[2,384,512]{2,1,0:T(8,128)(2,1)S(1)}, bf16[2,384,512]{2,1,0:T(8,128)(2,1)S(1)}, u32[]{:S(2)}, u32[]{:S(2)}) collective-permute-start(bf16[2,384,512]{2,1,0:T(8,128)(2,1)S(1)} %get-tuple-element.43), channel_id=1, source_target_pairs={{0,8},{8,0},{16,24},{24,16},{1,9},{9,1},{17,25},{25,17},{2,10},{10... | collective-permute-start | bytes 2359304 | tf_op jit(solution)/shard_map/ppermute | solution.py:171
  85.5 16.6 %collective-permute-start.13 = (bf16[2,384,512]{2,1,0:T(8,128)(2,1)S(1)}, bf16[2,384,512]{2,1,0:T(8,128)(2,1)S(1)}, u32[]{:S(2)}, u32[]{:S(2)}) collective-permute-start(bf16[2,384,512]{2,1,0:T(8,128)(2,1)S(1)} %get-tuple-element.45), channel_id=1, source_target_pairs={{0,16},{8,24},{16,0},{24,8},{1,17},{9,25},{17,1},{25,9},{2,18},{10... | collective-permute-start | bytes 2359304 | tf_op jit(solution)/shard_map/ppermute | solution.py:171
  91.0 13.7 %collective-permute-start.11 = (bf16[768,512]{1,0:T(8,128)(2,1)S(1)}, bf16[768,512]{1,0:T(8,128)(2,1)S(1)}, u32[]{:S(2)}, u32[]{:S(2)}) collective-permute-start(bf16[768,512]{1,0:T(8,128)(2,1)S(1)} %shard_map.107.refs_4_), channel_id=1, source_target_pairs={{2,4},{3,5},{4,2},{5,3},{10,12},{11,13},{12,10},{13,11},{18,20},{1... | collective-permute-start | bytes 2359304 | tf_op jit(solution)/shard_map/ppermute | solution.py:168
  91.8 20.5 %collective-permute-start.15 = (bf16[768,512]{1,0:T(8,128)(2,1)S(1)}, bf16[768,512]{1,0:T(8,128)(2,1)S(1)}, u32[]{:S(2)}, u32[]{:S(2)}) collective-permute-start(bf16[768,512]{1,0:T(8,128)(2,1)S(1)} %get-tuple-element.40.refs_4_.refs_0_), channel_id=1, source_target_pairs={{0,2},{1,3},{6,4},{7,5},{8,10},{9,11},{14,12},{15,13},{16,18},{17,... | collective-permute-start | bytes 2359304 | tf_op jit(solution)/shard_map/ppermute | solution.py:168
  119.9 15.1 %collective-permute-start.14 = (bf16[768,512]{1,0:T(8,128)(2,1)S(1)}, bf16[768,512]{1,0:T(8,128)(2,1)S(1)}, u32[]{:S(2)}, u32[]{:S(2)}) collective-permute-start(bf16[768,512]{1,0:T(8,128)(2,1)S(1)} %shard_map.109.refs_2_), channel_id=1, source_target_pairs={{0,2},{1,3},{4,6},{5,7},{2,0},{3,1},{6,4},{7,5},{8,10},{9,11},{12,... | collective-permute-start | bytes 2359304 | tf_op jit(solution)/shard_map/ppermute | solution.py:168
  122.3 12.6 %collective-permute-start.16 = (bf16[768,512]{1,0:T(8,128)(2,1)S(1)}, bf16[768,512]{1,0:T(8,128)(2,1)S(1)}, u32[]{:S(2)}, u32[]{:S(2)}) collective-permute-start(bf16[768,512]{1,0:T(8,128)(2,1)S(1)} %shard_map.110.refs_7_), channel_id=1, source_target_pairs={{2,4},{3,5},{4,2},{5,3},{10,12},{11,13},{12,10},{13,11},{18,20},{1... | collective-permute-start | bytes 2359304 | tf_op jit(solution)/shard_map/ppermute | solution.py:168
  129.2 15.6 %collective-permute-start.24 = (bf16[2,384,512]{2,1,0:T(8,128)(2,1)S(1)}, bf16[2,384,512]{2,1,0:T(8,128)(2,1)S(1)}, u32[]{:S(2)}, u32[]{:S(2)}) collective-permute-start(bf16[2,384,512]{2,1,0:T(8,128)(2,1)S(1)} %get-tuple-element.56), channel_id=1, source_target_pairs={{0,16},{8,24},{16,0},{24,8},{1,17},{9,25},{17,1},{25,9},{2,18},{10... | collective-permute-start | bytes 2359304 | tf_op jit(solution)/shard_map/ppermute | solution.py:171
  129.2 16.0 %collective-permute-start.23 = (bf16[2,384,512]{2,1,0:T(8,128)(2,1)S(1)}, bf16[2,384,512]{2,1,0:T(8,128)(2,1)S(1)}, u32[]{:S(2)}, u32[]{:S(2)}) collective-permute-start(bf16[2,384,512]{2,1,0:T(8,128)(2,1)S(1)} %get-tuple-element.50.refs_4_), channel_id=1, source_target_pairs={{0,8},{8,0},{16,24},{24,16},{1,9},{9,1},{17,25},{25,17},{2,10},{10... | collective-permute-start | bytes 2359304 | tf_op jit(solution)/shard_map/ppermute | solution.py:171
  143.8 16.2 %collective-permute-start.21 = (bf16[2,384,512]{2,1,0:T(8,128)(2,1)S(1)}, bf16[2,384,512]{2,1,0:T(8,128)(2,1)S(1)}, u32[]{:S(2)}, u32[]{:S(2)}) collective-permute-start(bf16[2,384,512]{2,1,0:T(8,128)(2,1)S(1)} %get-tuple-element.52), channel_id=1, source_target_pairs={{0,8},{8,0},{16,24},{24,16},{1,9},{9,1},{17,25},{25,17},{2,10},{10... | collective-permute-start | bytes 2359304 | tf_op jit(solution)/shard_map/ppermute | solution.py:171
  144.3 15.6 %collective-permute-start.22 = (bf16[2,384,512]{2,1,0:T(8,128)(2,1)S(1)}, bf16[2,384,512]{2,1,0:T(8,128)(2,1)S(1)}, u32[]{:S(2)}, u32[]{:S(2)}) collective-permute-start(bf16[2,384,512]{2,1,0:T(8,128)(2,1)S(1)} %get-tuple-element.53), channel_id=1, source_target_pairs={{0,16},{8,24},{16,0},{24,8},{1,17},{9,25},{17,1},{25,9},{2,18},{10... | collective-permute-start | bytes 2359304 | tf_op jit(solution)/shard_map/ppermute | solution.py:171
  162.6 13.2 %collective-permute-start.30 = (bf16[768,512]{1,0:T(8,128)(2,1)S(1)}, bf16[768,512]{1,0:T(8,128)(2,1)S(1)}, u32[]{:S(2)}, u32[]{:S(2)}) collective-permute-start(bf16[768,512]{1,0:T(8,128)(2,1)S(1)} %shard_map.114.refs_4_.refs_0_), channel_id=1, source_target_pairs={{2,4},{3,5},{4,2},{5,3},{10,12},{11,13},{12,10},{13,11},{18,20},{1... | collective-permute-start | bytes 2359304 | tf_op jit(solution)/shard_map/ppermute | solution.py:168
  163.3 20.4 %collective-permute-start.29 = (bf16[768,512]{1,0:T(8,128)(2,1)S(1)}, bf16[768,512]{1,0:T(8,128)(2,1)S(1)}, u32[]{:S(2)}, u32[]{:S(2)}) collective-permute-start(bf16[768,512]{1,0:T(8,128)(2,1)S(1)} %shard_map.114.refs_4_.refs_0_), channel_id=1, source_target_pairs={{0,2},{1,3},{4,6},{5,7},{2,0},{3,1},{6,4},{7,5},{8,10},{9,11},{12,... | collective-permute-start | bytes 2359304 | tf_op jit(solution)/shard_map/ppermute | solution.py:168
  176.3 20.7 %collective-permute-start.34 = (bf16[768,512]{1,0:T(8,128)(2,1)S(1)}, bf16[768,512]{1,0:T(8,128)(2,1)S(1)}, u32[]{:S(2)}, u32[]{:S(2)}) collective-permute-start(bf16[768,512]{1,0:T(8,128)(2,1)S(1)} %shard_map.117.refs_1_.refs_6_.refs_4_), channel_id=1, source_target_pairs={{4,6},{5,7},{2,0},{3,1},{12,14},{13,15},{10,8},{11,9},{20,22},{21,... | collective-permute-start | bytes 2359304 | tf_op jit(solution)/shard_map/ppermute | solution.py:168
  184.3 12.7 %collective-permute-start.33 = (bf16[768,512]{1,0:T(8,128)(2,1)S(1)}, bf16[768,512]{1,0:T(8,128)(2,1)S(1)}, u32[]{:S(2)}, u32[]{:S(2)}) collective-permute-start(bf16[768,512]{1,0:T(8,128)(2,1)S(1)} %shard_map.118.refs_4_.refs_3_.refs_2_), channel_id=1, source_target_pairs={{2,4},{3,5},{4,2},{5,3},{10,12},{11,13},{12,10},{13,11},{18,20},{1... | collective-permute-start | bytes 2359304 | tf_op jit(solution)/shard_map/ppermute | solution.py:168
  185.7 13.5 %collective-permute-start.32 = (bf16[2,384,512]{2,1,0:T(8,128)(2,1)S(1)}, bf16[2,384,512]{2,1,0:T(8,128)(2,1)S(1)}, u32[]{:S(2)}, u32[]{:S(2)}) collective-permute-start(bf16[2,384,512]{2,1,0:T(8,128)(2,1)S(1)} %get-tuple-element.66), channel_id=1, source_target_pairs={{0,16},{8,24},{16,0},{24,8},{1,17},{9,25},{17,1},{25,9},{2,18},{10... | collective-permute-start | bytes 2359304 | tf_op jit(solution)/shard_map/ppermute | solution.py:171
  188.0 12.0 %collective-permute-start.31 = (bf16[2,384,512]{2,1,0:T(8,128)(2,1)S(1)}, bf16[2,384,512]{2,1,0:T(8,128)(2,1)S(1)}, u32[]{:S(2)}, u32[]{:S(2)}) collective-permute-start(bf16[2,384,512]{2,1,0:T(8,128)(2,1)S(1)} %get-tuple-element.65.refs_2_), channel_id=1, source_target_pairs={{0,8},{8,0},{16,24},{24,16},{1,9},{9,1},{17,25},{25,17},{2,10},{10... | collective-permute-start | bytes 2359304 | tf_op jit(solution)/shard_map/ppermute | solution.py:171
  197.6 22.6 %collective-permute-start.37 = (bf16[768,512]{1,0:T(8,128)(2,1)S(1)}, bf16[768,512]{1,0:T(8,128)(2,1)S(1)}, u32[]{:S(2)}, u32[]{:S(2)}) collective-permute-start(bf16[768,512]{1,0:T(8,128)(2,1)S(1)} %shard_map.120.refs_10_.refs_7_), channel_id=1, source_target_pairs={{4,6},{5,7},{2,0},{3,1},{12,14},{13,15},{10,8},{11,9},{20,22},{21,... | collective-permute-start | bytes 2359304 | tf_op jit(solution)/shard_map/ppermute | solution.py:168
  203.9 21.3 %collective-permute-start.36 = (bf16[768,512]{1,0:T(8,128)(2,1)S(1)}, bf16[768,512]{1,0:T(8,128)(2,1)S(1)}, u32[]{:S(2)}, u32[]{:S(2)}) collective-permute-start(bf16[768,512]{1,0:T(8,128)(2,1)S(1)} %shard_map.121.refs_14_.refs_0_), channel_id=1, source_target_pairs={{2,4},{3,5},{4,2},{5,3},{10,12},{11,13},{12,10},{13,11},{18,20},{1... | collective-permute-start | bytes 2359304 | tf_op jit(solution)/shard_map/ppermute | solution.py:168
  204.6 32.4 %collective-permute-start.35 = (bf16[768,512]{1,0:T(8,128)(2,1)S(1)}, bf16[768,512]{1,0:T(8,128)(2,1)S(1)}, u32[]{:S(2)}, u32[]{:S(2)}) collective-permute-start(bf16[768,512]{1,0:T(8,128)(2,1)S(1)} %shard_map.121.refs_14_.refs_0_), channel_id=1, source_target_pairs={{0,2},{1,3},{4,6},{5,7},{2,0},{3,1},{6,4},{7,5},{8,10},{9,11},{12,... | collective-permute-start | bytes 2359304 | tf_op jit(solution)/shard_map/ppermute | solution.py:168
  225.7 22.5 %collective-permute-start.39 = (bf16[768,512]{1,0:T(8,128)(2,1)S(1)}, bf16[768,512]{1,0:T(8,128)(2,1)S(1)}, u32[]{:S(2)}, u32[]{:S(2)}) collective-permute-start(bf16[768,512]{1,0:T(8,128)(2,1)S(1)} %shard_map.123.refs_1_.refs_4_), channel_id=1, source_target_pairs={{4,6},{5,7},{2,0},{3,1},{12,14},{13,15},{10,8},{11,9},{20,22},{21,... | collective-permute-start | bytes 2359304 | tf_op jit(solution)/shard_map/ppermute | solution.py:168
  238.4 12.1 %collective-permute-start.42 = (bf16[768,512]{1,0:T(8,128)(2,1)S(1)}, bf16[768,512]{1,0:T(8,128)(2,1)S(1)}, u32[]{:S(2)}, u32[]{:S(2)}) collective-permute-start(bf16[768,512]{1,0:T(8,128)(2,1)S(1)} %shard_map.123.refs_1_.refs_4_), channel_id=1, source_target_pairs={{0,1},{1,0},{2,3},{3,2},{4,5},{5,4},{6,7},{7,6},{8,9},{9,8},{10,11... | collective-permute-start | bytes 2359304 | tf_op jit(solution)/shard_map/ppermute | solution.py:165
  238.9 11.7 %collective-permute-start.41 = (bf16[768,512]{1,0:T(8,128)(2,1)S(1)}, bf16[768,512]{1,0:T(8,128)(2,1)S(1)}, u32[]{:S(2)}, u32[]{:S(2)}) collective-permute-start(bf16[768,512]{1,0:T(8,128)(2,1)S(1)} %shard_map.124.refs_2_), channel_id=1, source_target_pairs={{0,1},{1,0},{2,3},{3,2},{4,5},{5,4},{6,7},{7,6},{8,9},{9,8},{10,11... | collective-permute-start | bytes 2359304 | tf_op jit(solution)/shard_map/ppermute | solution.py:165
  248.2 24.6 %collective-permute-start.47 = (bf16[768,1024]{1,0:T(8,128)(2,1)S(1)}, bf16[768,1024]{1,0:T(8,128)(2,1)S(1)}, u32[]{:S(2)}, u32[]{:S(2)}) collective-permute-start(bf16[768,1024]{1,0:T(8,128)(2,1)S(1)} %shard_map.122.refs_1_), channel_id=1, source_target_pairs={{0,1},{1,0},{2,3},{3,2},{4,5},{5,4},{6,7},{7,6},{8,9},{9,8},{10,11... | collective-permute-start | bytes 4718600 | tf_op jit(solution)/shard_map/ppermute | solution.py:165
  249.3 21.8 %collective-permute-start.44 = (bf16[768,512]{1,0:T(8,128)(2,1)S(1)}, bf16[768,512]{1,0:T(8,128)(2,1)S(1)}, u32[]{:S(2)}, u32[]{:S(2)}) collective-permute-start(bf16[768,512]{1,0:T(8,128)(2,1)S(1)} %shard_map.125.refs_14_.refs_0_), channel_id=1, source_target_pairs={{4,6},{5,7},{2,0},{3,1},{12,14},{13,15},{10,8},{11,9},{20,22},{21,... | collective-permute-start | bytes 2359304 | tf_op jit(solution)/shard_map/ppermute | solution.py:168
  (44 other events, 334.7 us)
